TPU v7x, 32 devices: a whole 2x2x4 slice. The times are simulated.
32 devices in a mesh: space: 8 (over z, core), mode: 4 (over y, x).
Axes of the slice: x: 2, y: 2, z: 4, core: 2. Of those that a mesh axis runs over, the one named last changes fastest.
Arguments:
- guess: float32 [4096, 2048], P('space', 'mode'), may hold values from -6 to 6
- forcing: float32 [4096, 2048], P('space', 'mode'), may hold values from -6 to 6
- spatial_diag: bfloat16 [4096, 512], P('space'), may hold values from -0.25 to 0.25
- spatial_ghost: bfloat16 [4096, 256], P('space'), may hold values from -0.375 to 0.375
- ghost_rows: int32 [16, 128], P('space'), may hold values from 0 to 511, as said below
- chaos_vals: bfloat16 [128, 128, 128], P('mode'), may hold values from -0.25 to 0.25
- chaos_targets: int32 [16, 8], replicated, may hold values from 0 to 15, as said below
- chaos_count: int32 [16], replicated, may hold values from 1 to 8, as said below
- mean_inverse: bfloat16 [2048, 2048], replicated, may hold values from -0.125 to 0.125
Outputs:
- field: float32 [4096, 2048], P('space', 'mode')
Inputs may be any that keep to these rules, and one draw needn't show every extreme that they name: `ghost_rows`: each row holds 128 distinct node numbers, 0 and 511 among them. `chaos_targets`: the targets in a row are distinct and the first is the row's own chaos block. Only the first chaos_count[j] slots of row j are used; some row uses all 8 slots and some row only one.
All inputs are finite; a program needn't handle non-finite values.
Results may differ from a plain program's by a relative error of at most 0.0021.
Values may be sent and summed in bfloat16 or wider, within the bound.
No kernel may reach another device: no remote copies, remote signals or barrier semaphores. Data moves between devices by JAX's collectives and lax.ppermute only.
A program may use at most 128 MiB of HBM per device.

v0:
```python
import jax
import jax.numpy as jnp
from jax import lax
from jax.sharding import PartitionSpec as P

ITERS = 3


step_gain = 0.5


def with_halo(cells, sides, width):
    for axis, dim in sides:
        count = lax.axis_size(axis)
        ends = count - 1
        head = lax.slice_in_dim(cells, 0, width, axis=dim)
        tail = lax.slice_in_dim(cells, cells.shape[dim] - width, cells.shape[dim], axis=dim)
        cells = jnp.concatenate(
            [
                lax.ppermute(tail, axis, [(i, (i + 1) % count) for i in range(ends)]),
                cells,
                lax.ppermute(head, axis, [((i + 1) % count, i) for i in range(ends)]),
            ],
            axis=dim,
        )
    return cells


def shards(
    guess,
    forcing,
    spatial_diag,
    spatial_ghost,
    ghost_rows,
    chaos_vals,
    chaos_targets,
    chaos_count,
    mean_inverse,
):
    node_rows, local_modes = guess.shape
    ghost_width = ghost_rows.shape[1]
    block_width = chaos_vals.shape[1]
    list_slots = chaos_targets.shape[1]
    all_blocks = chaos_targets.shape[0]
    total_cells = node_rows * lax.axis_size("space") * local_modes * lax.axis_size("mode")
    slab_tables = lax.all_gather(chaos_vals, "mode", axis=0, tiled=True)
    slab_tables = slab_tables.reshape(all_blocks, list_slots, block_width, block_width)
    slot_used = jnp.arange(list_slots, dtype=jnp.int32)[None, :] < chaos_count[:, None]
    every_block = jnp.arange(all_blocks, dtype=jnp.int32)
    target_hits = (chaos_targets[:, :, None] == every_block[None, None, :]) & slot_used[:, :, None]
    target_hits = target_hits.astype(jnp.bfloat16)
    full_table = jnp.einsum(
        "jsba,jst->jatb", slab_tables, target_hits, preferred_element_type=jnp.float32
    )
    full_table = full_table.astype(jnp.bfloat16).reshape(
        all_blocks * block_width, all_blocks * block_width
    )
    field = guess
    for iteration in range(ITERS):
        field_bf = field.astype(jnp.bfloat16)
        lower_sent = field_bf[ghost_rows[0]]
        upper_sent = field_bf[ghost_rows[1]]
        padded = with_halo(
            jnp.concatenate([lower_sent, upper_sent], axis=0), (("space", 0),), ghost_width
        )
        ghosts = jnp.concatenate([padded[:ghost_width], padded[3 * ghost_width :]], axis=0)
        spatial = jnp.dot(spatial_diag, field_bf, preferred_element_type=jnp.float32)
        spatial = spatial + jnp.dot(spatial_ghost, ghosts, preferred_element_type=jnp.float32)
        field_slab = lax.all_to_all(field_bf, "mode", split_axis=0, concat_axis=1, tiled=True)
        partial_slab = lax.all_to_all(
            forcing - spatial, "mode", split_axis=0, concat_axis=1, tiled=True
        )
        coupled_slab = jnp.dot(field_slab, full_table, preferred_element_type=jnp.float32)
        residual_slab = (partial_slab - coupled_slab).astype(jnp.bfloat16)
        update_slab = lax.dot_general(
            residual_slab,
            mean_inverse,
            (((1,), (1,)), ((), ())),
            preferred_element_type=jnp.float32,
        )
        update = lax.all_to_all(update_slab, "mode", split_axis=1, concat_axis=0, tiled=True)
        squares = lax.psum(jnp.sum(update * update), ("space", "mode"))
        damping = step_gain / jnp.sqrt(squares / total_cells + 1e-06)
        field = field + damping * update
    return field


def solution(mesh):
    placed = (
        P("space", "mode"),
        P("space", "mode"),
        P("space", None),
        P("space", None),
        P("space", None),
        P("mode", None, None),
        P(),
        P(),
        P(),
    )
    return jax.shard_map(
        shards, mesh=mesh, in_specs=placed, out_specs=P("space", "mode"), check_vma=False
    )
```

profile of v0, /device:TPU:0, one launch (start us, length us, event | category | flops | bytes accessed | tf_op | source)
XLA Modules:
  0.0 420.4 jit_solution(3426838757488246899)
XLA Ops:
  10.2 2.4 collective-permute-start
  15.7 4.5 %all-to-all-start.1 = ((bf16[4,128,512]{1,2,0:T(8,128)(2,1)}), bf16[4,128,512]{1,2,0:T(8,128)(2,1)S(1)}, u32[]{:S(2)}, u32[]{:S(2)}) async-start(bf16[4,128,512]{1,2,0:T(8,128)(2,1)} %copy.30), calls=%async_computation.1 | async-start | bytes 1048576 | tf_op jit(solution)/shard_map/all_to_all | solution.py:69
  22.0 2.5 copy.26
  24.6 10.1 %all-to-all-done.1 = bf16[4,128,512]{1,2,0:T(8,128)(2,1)S(1)} async-done(((bf16[4,128,512]{1,2,0:T(8,128)(2,1)}), bf16[4,128,512]{1,2,0:T(8,128)(2,1)S(1)}, u32[]{:S(2)}, u32[]{:S(2)}) %all-to-all-start.1) | async-done | bytes 524320 | tf_op jit(solution)/shard_map/all_to_all | solution.py:69
  34.7 3.5 all-to-all-start
  38.4 37.6 %all-gather.2.cloned.1.call-done = bf16[128,128,128]{2,1,0:T(8,128)(2,1)} async-done(((bf16[32,128,128]{2,1,0:T(8,128)(2,1)}), bf16[128,128,128]{2,1,0:T(8,128)(2,1)}) %all-gather.2.cloned.1.call-update) | async-done | bytes 4194320 | tf_op jit(solution)/shard_map/all_gather | solution.py:46
  76.0 7.5 %convert_bitcast_fusion = bf16[16,128,16,128]{1,2,3,0:T(8,128)(2,1)} fusion(bf16[16,8,128,128]{3,2,1,0:T(8,128)(2,1)} %bitcast.148, s32[16,8]{1,0:T(8,128)S(1)} %copy.27, pred[16,8]{1,0:T(8,128)(4,1)S(1)} %iota_compare_fusion.1), kind=kOutput, calls=%fused_computation.12 | convolution fusion | flops 71307264 | bytes 12583552 | tf_op jit(solution)/shard_map/jsba,jst->jatb/dot_general | solution.py:52
  83.5 13.3 %copy.29 = bf16[16,128,16,128]{3,2,1,0:T(8,128)(2,1)} copy(bf16[16,128,16,128]{1,2,3,0:T(8,128)(2,1)} %convert_bitcast_fusion) | data formatting | bytes 16777216 | tf_op jit(solution)/shard_map/convert_element_type | solution.py:55
  96.8 15.6 %fusion.38 = f32[128,2048]{1,0:T(8,128)} fusion(bf16[2048,2048]{1,0:T(8,128)(2,1)} %param.17, f32[128,2048]{0,1:T(8,128)S(1)} %bitcast.159, bf16[128,2048]{0,1:T(8,128)(2,1)S(1)} %bitcast.161, bf16[256,8,16,128]{3,2,1,0:T(8,128)(2,1)} %bitcast.142), kind=kOutput, calls=%fused_computation.33 | convolution fusion | flops 2148007936 | bytes 19398656 | tf_op jit(solution)/shard_map/dot_general | solution.py:75
  113.7 17.1 %all_to_all.153 = f32[128,4,512]{2,0,1:T(8,128)S(1)} all-to-all(f32[128,4,512]{2,0,1:T(8,128)S(1)} %bitcast.154), channel_id=1, replica_groups=mesh['space'=8,'mode'=4] {'mode'}, dimensions={1} | all-to-all | bytes 2097152 | tf_op jit(solution)/shard_map/all_to_all | solution.py:81
  131.6 40.3 %psum.21 = f32[]{:T(128)} all-reduce(f32[]{:T(128)} %multiply_reduce_fusion.2), channel_id=1, replica_groups=mesh['space'=8,'mode'=4] {'space','mode'}, use_global_device_ids=true, to_apply=%region_1.0 | all-reduce | flops 1 | bytes 8 | tf_op jit(solution)/shard_map/psum | solution.py:82
  181.2 2.5 fusion.36
  183.7 2.5 copy.32
  186.2 4.3 %all-to-all-start.3 = ((f32[4,128,512]{1,2,0:T(8,128)}), f32[4,128,512]{1,2,0:T(8,128)}, u32[]{:S(2)}, u32[]{:S(2)}) async-start(f32[4,128,512]{1,2,0:T(8,128)} %copy.32), calls=%async_computation.3 | async-start | bytes 2097152 | tf_op jit(solution)/shard_map/all_to_all | solution.py:70
  191.5 14.0 %all-to-all-done.3 = f32[4,128,512]{1,2,0:T(8,128)} async-done(((f32[4,128,512]{1,2,0:T(8,128)}), f32[4,128,512]{1,2,0:T(8,128)}, u32[]{:S(2)}, u32[]{:S(2)}) %all-to-all-start.3) | async-done | bytes 1048608 | tf_op jit(solution)/shard_map/all_to_all | solution.py:70
  205.5 3.5 all-to-all-start.4
  208.9 2.5 copy.34
  211.5 6.3 %all-to-all-done.4 = bf16[4,128,512]{1,2,0:T(8,128)(2,1)S(1)} async-done(((bf16[4,128,512]{1,2,0:T(8,128)(2,1)}), bf16[4,128,512]{1,2,0:T(8,128)(2,1)S(1)}, u32[]{:S(2)}, u32[]{:S(2)}) %all-to-all-start.4) | async-done | bytes 524320 | tf_op jit(solution)/shard_map/all_to_all | solution.py:69
  217.8 11.2 %fusion.41 = f32[128,2048]{1,0:T(8,128)} fusion(bf16[2048,2048]{1,0:T(8,128)(2,1)} %param.17, f32[128,2048]{1,0:T(8,128)} %copy.34, bf16[128,2048]{0,1:T(8,128)(2,1)S(1)} %bitcast.158, bf16[256,8,16,128]{3,2,1,0:T(8,128)(2,1)} %bitcast.143), kind=kOutput, calls=%fused_computation.34 | convolution fusion | flops 2148007936 | bytes 19398656 | tf_op jit(solution)/shard_map/dot_general | solution.py:75
  230.3 16.6 %all_to_all.154 = f32[128,4,512]{2,0,1:T(8,128)S(1)} all-to-all(f32[128,4,512]{2,0,1:T(8,128)S(1)} %bitcast.155), channel_id=1, replica_groups=mesh['space'=8,'mode'=4] {'mode'}, dimensions={1} | all-to-all | bytes 2097152 | tf_op jit(solution)/shard_map/all_to_all | solution.py:81
  248.8 41.1 %psum.22 = f32[]{:T(128)} all-reduce(f32[]{:T(128)} %multiply_reduce_fusion.1), channel_id=1, replica_groups=mesh['space'=8,'mode'=4] {'space','mode'}, use_global_device_ids=true, to_apply=%region_3.0 | all-reduce | flops 1 | bytes 8 | tf_op jit(solution)/shard_map/psum | solution.py:82
  300.4 2.5 fusion.34
  302.9 2.5 copy.36
  305.4 4.2 %all-to-all-start.6 = ((f32[4,128,512]{1,2,0:T(8,128)}), f32[4,128,512]{1,2,0:T(8,128)}, u32[]{:S(2)}, u32[]{:S(2)}) async-start(f32[4,128,512]{1,2,0:T(8,128)} %copy.36), calls=%async_computation.6 | async-start | bytes 2097152 | tf_op jit(solution)/shard_map/all_to_all | solution.py:70
  310.7 13.9 %all-to-all-done.6 = f32[4,128,512]{1,2,0:T(8,128)} async-done(((f32[4,128,512]{1,2,0:T(8,128)}), f32[4,128,512]{1,2,0:T(8,128)}, u32[]{:S(2)}, u32[]{:S(2)}) %all-to-all-start.6) | async-done | bytes 1048608 | tf_op jit(solution)/shard_map/all_to_all | solution.py:70
  324.6 3.7 all-to-all-start.7
  328.3 2.5 copy.38
  330.8 6.1 %all-to-all-done.7 = bf16[4,128,512]{1,2,0:T(8,128)(2,1)S(1)} async-done(((bf16[4,128,512]{1,2,0:T(8,128)(2,1)}), bf16[4,128,512]{1,2,0:T(8,128)(2,1)S(1)}, u32[]{:S(2)}, u32[]{:S(2)}) %all-to-all-start.7) | async-done | bytes 524320 | tf_op jit(solution)/shard_map/all_to_all | solution.py:69
  336.9 11.1 %fusion.44 = f32[128,2048]{1,0:T(8,128)} fusion(bf16[2048,2048]{1,0:T(8,128)(2,1)} %param.17, f32[128,2048]{1,0:T(8,128)} %copy.38, bf16[128,2048]{0,1:T(8,128)(2,1)S(1)} %bitcast.157, bf16[256,8,16,128]{3,2,1,0:T(8,128)(2,1)} %bitcast.144), kind=kOutput, calls=%fused_computation.35 | convolution fusion | flops 2148007936 | bytes 19398656 | tf_op jit(solution)/shard_map/dot_general | solution.py:75
  349.4 16.6 %all_to_all.155 = f32[128,4,512]{2,0,1:T(8,128)S(1)} all-to-all(f32[128,4,512]{2,0,1:T(8,128)S(1)} %bitcast.156), channel_id=1, replica_groups=mesh['space'=8,'mode'=4] {'mode'}, dimensions={1} | all-to-all | bytes 2097152 | tf_op jit(solution)/shard_map/all_to_all | solution.py:81
  367.9 41.2 %psum.23 = f32[]{:T(128)} all-reduce(f32[]{:T(128)} %multiply_reduce_fusion), channel_id=1, replica_groups=mesh['space'=8,'mode'=4] {'space','mode'}, use_global_device_ids=true, to_apply=%region_5.0 | all-reduce | flops 1 | bytes 8 | tf_op jit(solution)/shard_map/psum | solution.py:82
  411.1 2.5 bitcast_add_fusion
  (64 shorter events, 38.9 us)
Async XLA Ops:
  6.5 13.8 %copy-start = (bf16[512,512]{1,0:T(8,128)(2,1)S(1)}, bf16[512,512]{1,0:T(8,128)(2,1)}, u32[]{:S(2)}) copy-start(bf16[512,512]{1,0:T(8,128)(2,1)} %param.11) | copy-start | bytes 1572868
  6.5 14.2 %copy-start.7 = (bf16[512,256]{1,0:T(8,128)(2,1)S(1)}, bf16[512,256]{1,0:T(8,128)(2,1)}, u32[]{:S(2)}) copy-start(bf16[512,256]{1,0:T(8,128)(2,1)} %param.12) | copy-start | bytes 786436
  6.5 14.2 %copy-start.2 = (f32[512,512]{1,0:T(8,128)S(1)}, f32[512,512]{1,0:T(8,128)}, u32[]{:S(2)}) copy-start(f32[512,512]{1,0:T(8,128)} %param.10) | copy-start | bytes 3145732
  6.5 31.7 %copy-start.8 = (s32[16,8]{0,1:T(8,128)S(1)}, s32[16,8]{0,1:T(8,128)}, u32[]{:S(2)}) copy-start(s32[16,8]{0,1:T(8,128)} %param.15) | copy-start | bytes 1540
  6.5 31.8 %copy-start.9 = (s32[16]{0:T(128)S(1)}, s32[16]{0:T(128)}, u32[]{:S(2)}) copy-start(s32[16]{0:T(128)} %param.16) | copy-start | bytes 196
  6.5 69.5 %all-gather.2.cloned.1.call-start = ((), (), s32[]{:S(2)}) async-start(), calls=%async_computation.9 | async-start | bytes 5242880 | tf_op jit(solution)/shard_map/all_gather | solution.py:46
  10.2 10.5 %collective-permute-start = (bf16[128,512]{1,0:T(8,128)(2,1)S(1)}, bf16[128,512]{1,0:T(8,128)(2,1)S(1)}, u32[]{:S(2)}, u32[]{:S(2)}) collective-permute-start(bf16[128,512]{1,0:T(8,128)(2,1)S(1)} %gather_fusion), channel_id=1, source_target_pairs={{0,4},{4,8},{8,12},{12,16},{16,20},{20,24},{24,28},{1,5},{5,9},{9,... | collective-permute-start | bytes 393224 | tf_op jit(solution)/shard_map/ppermute | solution.py:20
  13.4 7.3 %collective-permute-start.1 = (bf16[128,512]{1,0:T(8,128)(2,1)S(1)}, bf16[128,512]{1,0:T(8,128)(2,1)S(1)}, u32[]{:S(2)}, u32[]{:S(2)}) collective-permute-start(bf16[128,512]{1,0:T(8,128)(2,1)S(1)} %gather_fusion.1), channel_id=1, source_target_pairs={{4,0},{8,4},{12,8},{16,12},{20,16},{24,20},{28,24},{5,1},{9,5},{13... | collective-permute-start | bytes 393224 | tf_op jit(solution)/shard_map/ppermute | solution.py:22
  15.7 18.9 %all-to-all-start.1 = ((bf16[4,128,512]{1,2,0:T(8,128)(2,1)}), bf16[4,128,512]{1,2,0:T(8,128)(2,1)S(1)}, u32[]{:S(2)}, u32[]{:S(2)}) async-start(bf16[4,128,512]{1,2,0:T(8,128)(2,1)} %copy.30), calls=%async_computation.1 | async-start | bytes 1048576 | tf_op jit(solution)/shard_map/all_to_all | solution.py:69
  34.7 62.1 %all-to-all-start = ((f32[4,128,512]{1,2,0:T(8,128)}), f32[4,128,512]{1,2,0:T(8,128)S(1)}, u32[]{:S(2)}, u32[]{:S(2)}) async-start(f32[4,128,512]{1,2,0:T(8,128)} %copy.26), calls=%async_computation | async-start | bytes 2097152 | tf_op jit(solution)/shard_map/all_to_all | solution.py:70
  96.8 77.1 %copy-start.1 = (f32[512,512]{1,0:T(8,128)S(1)}, f32[512,512]{1,0:T(8,128)}, u32[]{:S(2)}) copy-start(f32[512,512]{1,0:T(8,128)} %param.9) | copy-start | bytes 3145732
  130.8 41.8 %copy-start.5 = (f32[128,4,512]{2,0,1:T(8,128)}, f32[128,4,512]{2,0,1:T(8,128)S(1)}, u32[]{:S(2)}) copy-start(f32[128,4,512]{2,0,1:T(8,128)S(1)} %all_to_all.153) | copy-start | bytes 3145732
  176.5 3.0 collective-permute-start.2
  177.8 3.4 collective-permute-start.3
  186.2 19.2 %all-to-all-start.3 = ((f32[4,128,512]{1,2,0:T(8,128)}), f32[4,128,512]{1,2,0:T(8,128)}, u32[]{:S(2)}, u32[]{:S(2)}) async-start(f32[4,128,512]{1,2,0:T(8,128)} %copy.32), calls=%async_computation.3 | async-start | bytes 2097152 | tf_op jit(solution)/shard_map/all_to_all | solution.py:70
  205.5 12.3 %all-to-all-start.4 = ((bf16[4,128,512]{1,2,0:T(8,128)(2,1)}), bf16[4,128,512]{1,2,0:T(8,128)(2,1)S(1)}, u32[]{:S(2)}, u32[]{:S(2)}) async-start(bf16[4,128,512]{1,2,0:T(8,128)(2,1)} %copy.33), calls=%async_computation.4 | async-start | bytes 1048576 | tf_op jit(solution)/shard_map/all_to_all | solution.py:69
  247.0 1.0 copy-start.6
  291.9 1.1 copy-start.3
  295.7 3.0 collective-permute-start.4
  297.0 3.4 collective-permute-start.5
  305.4 19.2 %all-to-all-start.6 = ((f32[4,128,512]{1,2,0:T(8,128)}), f32[4,128,512]{1,2,0:T(8,128)}, u32[]{:S(2)}, u32[]{:S(2)}) async-start(f32[4,128,512]{1,2,0:T(8,128)} %copy.36), calls=%async_computation.6 | async-start | bytes 2097152 | tf_op jit(solution)/shard_map/all_to_all | solution.py:70
  324.6 12.3 %all-to-all-start.7 = ((bf16[4,128,512]{1,2,0:T(8,128)(2,1)}), bf16[4,128,512]{1,2,0:T(8,128)(2,1)S(1)}, u32[]{:S(2)}, u32[]{:S(2)}) async-start(bf16[4,128,512]{1,2,0:T(8,128)(2,1)} %copy.37), calls=%async_computation.7 | async-start | bytes 1048576 | tf_op jit(solution)/shard_map/all_to_all | solution.py:69
  366.0 1.0 copy-start.4
Sparse Core Ops, SparseCore 0:
  9.2 66.7 all-gather.1
where the time goes:
time: 422 us; the launch traced here: 420 us
  blocking collectives  173 us (41%)
  waiting for transfers between devices  92.1 us (22%)
  matrix products  53 us (13%)
  local copies, waits for them, and re-layouts  42.4 us (10%)
  starting transfers between devices  32.6 us (8%)
  between operations  15.6 us (4%)
  other arithmetic  11.9 us (3%)
    psum x3, blocking collectives, shards(): squares = lax.psum(jnp.sum(update * update), ('space', 'mode'))  123 us
    all_to_all x3, blocking collectives, shards(): lax.all_to_all(update_slab, 'mode', split_axis=1, concat_axis=0, tiled=True)  50.4 us
    dot_general x3, matrix products, shards(): lax.dot_general(residual_slab, mean_inverse, (((1,), (1,)), ((), ())), pr...  38 us
    all_gather x1, waiting for transfers between devices, shards(): slab_tables = lax.all_gather(chaos_vals, 'mode', axis=0, tiled=True)  37.6 us
    all_to_all x3, waiting for transfers between devices, shards(): lax.all_to_all(forcing - spatial, 'mode', split_axis=0, concat_axis=1, ti...  27.9 us
    all_to_all x3, waiting for transfers between devices, shards(): lax.all_to_all(field_bf, 'mode', split_axis=0, concat_axis=1, tiled=True)  22.5 us
    convert_element_type x1, local copies, waits for them, and re-layouts, shards(): full_table.astype(jnp.bfloat16)  13.3 us
    all_to_all x5, local copies, waits for them, and re-layouts, shards(): lax.all_to_all(forcing - spatial, 'mode', split_axis=0, concat_axis=1, ti...  12.7 us
  transfers between devices with their start and end apart: 13, of which 8 were waited for; matrix products, arithmetic and copies ran while one was open for 9% of the time, Pallas kernels for 0%

commit v1 on v0

v1 whole, which is shorter than its diff:
```python
import functools

import jax
import jax.numpy as jnp
from jax import lax
from jax.experimental import pallas as pl
from jax.experimental.pallas import tpu as pltpu
from jax.sharding import PartitionSpec as P


step_gain = 0.5
F32 = jnp.float32
BF16 = jnp.bfloat16
VMEM = pl.BlockSpec(memory_space=pltpu.VMEM)
SMEM = pl.BlockSpec(memory_space=pltpu.SMEM)


def call(body, outs, args, scalars=0, limit=40):
    return pl.pallas_call(
        body,
        out_shape=outs,
        in_specs=[SMEM] * scalars + [VMEM] * (len(args) - scalars),
        out_specs=[VMEM] * len(outs),
        compiler_params=pltpu.CompilerParams(vmem_limit_bytes=limit << 20),
    )(*args)


def shaped(shape, dtype=BF16):
    return jax.ShapeDtypeStruct(shape, dtype)


def rows_of(owner, rows):
    return pl.ds(pl.multiple_of(owner * rows, rows), rows)


def mm(a, b):
    return jnp.dot(a, b, preferred_element_type=F32)


def mmt(a, b):
    return lax.dot_general(a, b, (((1,), (1,)), ((), ())), preferred_element_type=F32)


def flip_permute(x, axis, bit):
    return lax.ppermute(x, axis, [(i, i ^ bit) for i in range(lax.axis_size(axis))])


def trade(pieces):
    return [pieces[0]] + [flip_permute(p, "mode", k) for k, p in enumerate(pieces) if k > 0]


def halo(lower, upper):
    count = lax.axis_size("space")
    below = lax.ppermute(upper, "space", [(i, i + 1) for i in range(count - 1)])
    above = lax.ppermute(lower, "space", [(i + 1, i) for i in range(count - 1)])
    return below, above


def start_body(n, where, u_ref, pick_ref, *outs):
    whole, lower, upper = outs[:3]
    rows = u_ref.shape[0] // n
    ghost = lower.shape[0]
    whole[...] = u_ref[...].astype(BF16)
    picked = mm(pick_ref[...], whole[...]).astype(BF16)
    lower[...] = picked[:ghost]
    upper[...] = picked[ghost:]
    for k in range(n):
        outs[3 + k][0] = whole[rows_of(where[0] ^ k, rows), :]


def spatial_of(diag, ghostly, x, below, above):
    ghost = below.shape[0]
    y = mm(diag[...], x[...])
    y = y + mm(ghostly[:, :ghost], below[...])
    return y + mm(ghostly[:, ghost:], above[...])


def first_body(n, where, diag, ghostly, x, below, above, f_ref, pick_ref, *outs):
    both, lower, upper = outs[:3]
    nodes, width = x.shape
    rows = nodes // n
    ghost = lower.shape[0]
    s = spatial_of(diag, ghostly, x, below, above)
    p = f_ref[...] - s
    high = p.astype(BF16)
    both[:, :width] = s.astype(BF16)
    both[:, width:] = high
    low = outs[-1]
    low[...] = (p - high.astype(F32)).astype(BF16)
    picked = mm(pick_ref[...], both[...]).astype(BF16)
    lower[...] = picked[:ghost]
    upper[...] = picked[ghost:]
    for k in range(n):
        at = rows_of(where[0] ^ k, rows)
        outs[3 + k][0] = both[at, width:]
        outs[3 + k][1] = low[at, :]
        outs[3 + k][2] = both[at, :width]


def second_body(n, where, diag, ghostly, x, below, above, pick_ref, *outs):
    p1, lower, upper = outs[:3]
    nodes, width = p1.shape
    rows = nodes // n
    ghost = lower.shape[0]
    y = spatial_of(diag, ghostly, x, below, above).astype(BF16)
    p1[...] = y[:, width:]
    picked = mm(pick_ref[...], p1[...]).astype(BF16)
    lower[...] = picked[:ghost]
    upper[...] = picked[ghost:]
    s2 = outs[-1]
    s2[...] = y[:, :width]
    for k in range(n):
        at = rows_of(where[0] ^ k, rows)
        outs[3 + k][0] = s2[at, :]
        outs[3 + k][1] = p1[at, :]


def third_body(n, where, diag, ghostly, x, below, above, *outs):
    rows = x.shape[0] // n
    whole = outs[-1]
    whole[...] = spatial_of(diag, ghostly, x, below, above).astype(BF16)
    for k in range(n):
        outs[k][0] = whole[rows_of(where[0] ^ k, rows), :]


def table_body(n, slots, per, where, targets, counts, *refs):
    out = refs[-1]
    step = 256
    width = refs[0].shape[-1]

    def clear(i, carry):
        out[pl.ds(pl.multiple_of(i * step, step), step), :] = jnp.zeros(
            (step, out.shape[1]), out.dtype
        )
        return carry

    lax.fori_loop(0, out.shape[0] // step, clear, 0)
    quarter = refs[0].shape[1]
    bits = n.bit_length() - 1
    for which in range(4):
        core = where[1] if which < 2 else 1 - where[1]
        base = core * (2 * quarter) + (which % 2) * quarter
        for k in range(n):
            at = k if which % 2 == 0 else int(format(k, "b").zfill(bits)[::-1], 2) if bits else 0
            owner = where[0] ^ k

            def place(i, carry, which=which, at=at, owner=owner, base=base):
                entry = base + i
                source = owner * per + entry // slots
                slot = entry % slots

                @pl.when(slot < counts[source])
                def _():
                    target = targets[source, slot]
                    out[
                        pl.ds(pl.multiple_of(target * width, width), width),
                        pl.ds(pl.multiple_of(source * width, width), width),
                    ] = refs[which][at, i]

                return carry

            lax.fori_loop(0, quarter, place, 0)


def apply(n, me, get, table, emit):
    width = table.shape[0] // n
    for g in range(n):
        out_rows = rows_of(me ^ g, width)
        total = None
        for k in range(n):
            part = mmt(get(k), table[out_rows, rows_of(me ^ k, width)])
            total = part if total is None else total + part
        emit(g, total)


def damping_of(squares, cells):
    total = jnp.sum(squares[...], axis=0, keepdims=True)[:, :1]
    return step_gain / jnp.sqrt(total / cells + 1e-06)


def stage_a(n, where, *refs):
    us, ps = refs[:n], refs[n : 2 * n]
    chaos, inverse, w0, c1, ca0, squares, pair, quick = refs[2 * n :]
    me = where[0]
    rows = us[0].shape[1]

    def residual(g, value):
        r = ps[g][0].astype(F32) + ps[g][1].astype(F32) - value[:rows]
        high = r.astype(BF16)
        pair[g, :rows] = high
        pair[g, rows:] = (r - high.astype(F32)).astype(BF16)
        c1[g] = value[rows:]

    apply(n, me, lambda k: jnp.concatenate([us[k][0], ps[k][2]], axis=0), chaos, residual)
    sums = []

    def updated(g, value):
        w = value[:rows] + value[rows:]
        w0[g] = w
        quick[g] = w.astype(BF16)
        sums.append(jnp.sum(w * w))

    apply(n, me, lambda k: pair[k], inverse, updated)
    squares[...] = jnp.full(squares.shape, sum(sums), F32)

    def coupled(g, value):
        ca0[g] = value

    apply(n, me, lambda k: quick[k], chaos, coupled)


def stage_b(n, cells, where, *refs):
    ps = refs[:n]
    chaos, inverse, w0, c1, ca0, sq0, v1, w1, c2, ca1, cv1, squares, one, three = refs[n:]
    me = where[0]
    rows = w0.shape[1]
    d0 = damping_of(sq0, cells)

    for g in range(n):
        one[g] = (ps[g][1].astype(F32) - c1[g]).astype(BF16)
        three[g, :rows] = ps[g][0]

    def moved(g, value):
        three[g, rows : 2 * rows] = value.astype(BF16)
        v1[g] = value + ca0[g]

    apply(n, me, lambda k: one[k], inverse, moved)
    for g in range(n):
        one[g] = v1[g].astype(BF16)
    sums = []

    def updated(g, value):
        v1[g] = value
        three[g, 2 * rows :] = value.astype(BF16)
        w = w0[g] - d0 * value
        w1[g] = w
        sums.append(jnp.sum(w * w))

    apply(n, me, lambda k: one[k], inverse, updated)
    squares[...] = jnp.full(squares.shape, sum(sums), F32)

    def coupled(g, value):
        c2[g] = value[:rows]
        ca1[g] = value[rows : 2 * rows]
        cv1[g] = value[2 * rows :]

    apply(n, me, lambda k: three[k], chaos, coupled)


def mix_body(n, cells, w0, w1, sq0, sq1, *outs):
    d0 = damping_of(sq0, cells)
    d1 = damping_of(sq1, cells)
    for g in range(n):
        e = d0 * w0[g] + d1 * w1[g]
        high = e.astype(BF16)
        outs[g][0] = high
        outs[g][1] = (e - high.astype(F32)).astype(BF16)


def stage_c(n, cells, where, *refs):
    ps = refs[:n]
    inverse, v1, w1, c2, ca1, cv1, sq0, sq1 = refs[n : n + 8]
    outs = refs[n + 8 : 2 * n + 8]
    squares, one, two = refs[2 * n + 8 :]
    me = where[0]
    d0 = damping_of(sq0, cells)
    d1 = damping_of(sq1, cells)
    for g in range(n):
        one[g] = (ps[g][0].astype(F32) - c2[g]).astype(BF16)

    def second(g, value):
        two[g] = (value + ca1[g]).astype(BF16)

    apply(n, me, lambda k: one[k], inverse, second)

    def third(g, value):
        one[g] = (value + cv1[g]).astype(BF16)

    apply(n, me, lambda k: two[k], inverse, third)
    sums = []

    def last(g, value):
        w = w1[g] - d1 * (v1[g] - d0 * value)
        outs[g][...] = w.astype(BF16)
        sums.append(jnp.sum(w * w))

    apply(n, me, lambda k: one[k], inverse, last)
    squares[...] = jnp.full(squares.shape, sum(sums), F32)


def end_body(n, cells, where, u_ref, sq2, *refs):
    es, ws, out = refs[:n], refs[n : 2 * n], refs[2 * n]
    rows = u_ref.shape[0] // n
    d2 = damping_of(sq2, cells)
    for k in range(n):
        at = rows_of(where[0] ^ k, rows)
        e = es[k][0].astype(F32) + es[k][1].astype(F32)
        out[at, :] = u_ref[at, :] + (e + d2 * ws[k][...].astype(F32))


def summed(squares):
    return lax.all_to_all(squares, ("space", "mode"), split_axis=0, concat_axis=0, tiled=True)


def gathered(vals, core, n):
    entries = vals.shape[0]
    half = lax.dynamic_slice_in_dim(vals, core * (entries // 2), entries // 2, 0)
    bits = [1 << b for b in range(n.bit_length() - 1)]
    found = []
    for part, order in ((half[: entries // 4], bits), (half[entries // 4 :], bits[::-1])):
        held = part[None]
        for bit in order:
            held = jnp.concatenate([held, flip_permute(held, "mode", bit)], axis=0)
        found.append(held)
    return found + [flip_permute(held, "space", 1) for held in found]


def shards(
    guess,
    forcing,
    spatial_diag,
    spatial_ghost,
    ghost_rows,
    chaos_vals,
    chaos_targets,
    chaos_count,
    mean_inverse,
):
    n = lax.axis_size("mode")
    devices = n * lax.axis_size("space")
    nodes, width = guess.shape
    rows = nodes // n
    ghost = ghost_rows.shape[1]
    modes = mean_inverse.shape[0]
    slots = chaos_targets.shape[1]
    per = chaos_targets.shape[0] // n
    cells = float(nodes * width * devices)
    me = lax.axis_index("mode").astype(jnp.int32)
    core = (lax.axis_index("space") % 2).astype(jnp.int32)
    where = jnp.stack([me, core])
    pick = (ghost_rows.reshape(-1)[:, None] == jnp.arange(nodes, dtype=jnp.int32)[None, :]).astype(
        BF16
    )

    def sent(count):
        return [shaped((count, rows, width))] * n

    def edges(times):
        return [shaped((ghost, times * width))] * 2

    tables = gathered(chaos_vals, core, n)
    whole, lower, upper, *us = call(
        functools.partial(start_body, n),
        [shaped((nodes, width))] + edges(1) + sent(1),
        [where, guess, pick],
        1,
    )
    below, above = halo(lower, upper)
    us = trade(us)
    both, lower, upper, *ps = call(
        functools.partial(first_body, n),
        [shaped((nodes, 2 * width))] + edges(2) + sent(3) + [shaped((nodes, width))],
        [where, spatial_diag, spatial_ghost, whole, below, above, forcing, pick],
        1,
    )[:-1]
    below, above = halo(lower, upper)
    ps = trade(ps)
    p1, lower, upper, *qs = call(
        functools.partial(second_body, n),
        [shaped((nodes, width))] + edges(1) + sent(2) + [shaped((nodes, width))],
        [where, spatial_diag, spatial_ghost, both, below, above, pick],
        1,
    )[:-1]
    below, above = halo(lower, upper)
    qs = trade(qs)
    last = call(
        functools.partial(third_body, n),
        sent(1) + [shaped((nodes, width))],
        [where, spatial_diag, spatial_ghost, p1, below, above],
        1,
    )[:-1]
    last = trade(last)

    (chaos,) = call(
        functools.partial(table_body, n, slots, per),
        [shaped((modes, modes))],
        [where, chaos_targets, chaos_count] + tables,
        3,
    )
    slab = shaped((n, rows, width), F32)
    tile = shaped((devices, 128), F32)
    low_slab = shaped((n, rows, width))
    w0, c1, ca0, sq0 = call(
        functools.partial(stage_a, n),
        [slab, slab, slab, tile, shaped((n, 2 * rows, width)), low_slab],
        [where] + us + ps + [chaos, mean_inverse],
        1,
    )[:4]
    sq0 = summed(sq0)
    v1, w1, c2, ca1, cv1, sq1 = call(
        functools.partial(stage_b, n, cells),
        [slab, slab, slab, slab, slab, tile, low_slab, shaped((n, 3 * rows, width))],
        [where] + qs + [chaos, mean_inverse, w0, c1, ca0, sq0],
        1,
    )[:6]
    sq1 = summed(sq1)
    es = trade(call(functools.partial(mix_body, n, cells), sent(2), [w0, w1, sq0, sq1]))
    *ws, sq2 = call(
        functools.partial(stage_c, n, cells),
        [shaped((rows, width))] * n + [tile, low_slab, low_slab],
        [where] + last + [mean_inverse, v1, w1, c2, ca1, cv1, sq0, sq1],
        1,
    )[: n + 1]
    ws = trade(ws)
    sq2 = summed(sq2)
    (field,) = call(
        functools.partial(end_body, n, cells),
        [shaped((nodes, width), F32)],
        [where, guess, sq2] + es + ws,
        1,
    )
    return field


def solution(mesh):
    placed = (
        P("space", "mode"),
        P("space", "mode"),
        P("space", None),
        P("space", None),
        P("space", None),
        P("mode", None, None),
        P(),
        P(),
        P(),
    )
    return jax.shard_map(
        shards, mesh=mesh, in_specs=placed, out_specs=P("space", "mode"), check_vma=False
    )
```

time: 422 us -> 185 us (0.44)
  blocking collectives: 173 us -> 22.9 us
  Pallas kernels: 0 us -> 56.8 us
  waiting for transfers between devices: 92.1 us -> 36.8 us
  matrix products: 53 us -> 0 us
  local copies, waits for them, and re-layouts: 42.4 us -> 19.3 us
  between operations: 15.6 us -> 0.38 us
  starting transfers between devices: 32.6 us -> 44.3 us
  other arithmetic: 11.9 us -> 3.32 us
    psum x3 -> x0, blocking collectives: 123 us -> none  [shards(): squares = lax.psum(jnp.sum(update * update), ('space', 'mode'))]
    pallas_call x0 -> x10, Pallas kernels: none -> 56.8 us  [call(): pl.pallas_call(body, out_shape=outs, in_specs=[SMEM] * scalars + [VMEM] *...]
    dot_general x10 -> x0, matrix products: 53 us -> none  [the longest x3 38 us: shards(): lax.dot_general(residual_slab, mean_inverse, (((1,), (1,)), ((), ())), pr...]
    all_to_all x6 -> x1, waiting for transfers between devices: 50.4 us -> 6.89 us  [summed(): lax.all_to_all(squares, ('space', 'mode'), split_axis=0, concat_axis=0, t...]
    all_gather x1 -> x0, waiting for transfers between devices: 37.6 us -> none  [shards(): slab_tables = lax.all_gather(chaos_vals, 'mode', axis=0, tiled=True)]
    ppermute x6 -> x30, starting transfers between devices: 8.81 us -> 37.7 us  [the longest x24 28.3 us: flip_permute(): lax.ppermute(x, axis, [(i, i ^ bit) for i in range(lax.axis_size(axis))])]
    all_to_all x3 -> x2, blocking collectives: 50.4 us -> 22.9 us  [summed(): lax.all_to_all(squares, ('space', 'mode'), split_axis=0, concat_axis=0, t...]
    ppermute x6 -> x30, waiting for transfers between devices: 3.36 us -> 29.9 us  [the longest x24 29.5 us: flip_permute(): lax.ppermute(x, axis, [(i, i ^ bit) for i in range(lax.axis_size(axis))])]
  transfers between devices with their start and end apart: 13 -> 31, of which waited for: 8 -> 10; matrix products, arithmetic and copies ran while one was open for 9% -> 2% of each run, Pallas kernels for 0% -> 23%
where the time goes in v1:
time: 185 us; the launch traced here: 184 us
  Pallas kernels  56.8 us (31%)
  starting transfers between devices  44.3 us (24%)
  waiting for transfers between devices  36.8 us (20%)
  blocking collectives  22.9 us (12%)
  local copies, waits for them, and re-layouts  19.3 us (10%)
  other arithmetic  3.32 us (2%)
    pallas_call x10, Pallas kernels, call(): pl.pallas_call(body, out_shape=outs, in_specs=[SMEM] * scalars + [VMEM] *...  56.8 us
    ppermute x24, waiting for transfers between devices, flip_permute(): lax.ppermute(x, axis, [(i, i ^ bit) for i in range(lax.axis_size(axis))])  29.5 us
    ppermute x24, starting transfers between devices, flip_permute(): lax.ppermute(x, axis, [(i, i ^ bit) for i in range(lax.axis_size(axis))])  28.3 us
    all_to_all x2, blocking collectives, summed(): lax.all_to_all(squares, ('space', 'mode'), split_axis=0, concat_axis=0, t...  22.9 us
    unnamed x69, local copies, waits for them, and re-layouts  18.2 us
    all_to_all x1, waiting for transfers between devices, summed(): lax.all_to_all(squares, ('space', 'mode'), split_axis=0, concat_axis=0, t...  6.89 us
    all_to_all x1, starting transfers between devices, summed(): lax.all_to_all(squares, ('space', 'mode'), split_axis=0, concat_axis=0, t...  6.54 us
    ppermute x3, starting transfers between devices, halo(): below = lax.ppermute(upper, 'space', [(i, i + 1) for i in range(count - 1)])  5.61 us
  transfers between devices with their start and end apart: 31, of which 10 were waited for; matrix products, arithmetic and copies ran while one was open for 2% of the time, Pallas kernels for 23%

profile of v1, /device:TPU:0, one launch (start us, length us, event | category | flops | bytes accessed | tf_op | source)
XLA Modules:
  0.0 183.8 jit_solution(11297452289426526385)
XLA Ops:
  1.2 3.0 %collective-permute-start.12 = (bf16[1,8,128,128]{3,2,1,0:T(8,128)(2,1)S(1)}, bf16[1,8,128,128]{3,2,1,0:T(8,128)(2,1)S(1)}, u32[]{:S(2)}, u32[]{:S(2)}) collective-permute-start(bf16[1,8,128,128]{3,2,1,0:T(8,128)(2,1)S(1)} %get-tuple-element.94), channel_id=1, source_target_pairs={{0,1},{1,0},{2,3},{3,2},{4,5},{5,4},{6,7},{7,6},{8,9},{9,8},{10,11... | collective-permute-start | bytes 786440 | tf_op jit(solution)/shard_map/ppermute | solution.py:45
  4.2 1.5 collective-permute-start.14
  5.7 4.8 %collective-permute-done.12 = bf16[1,8,128,128]{3,2,1,0:T(8,128)(2,1)S(1)} collective-permute-done((bf16[1,8,128,128]{3,2,1,0:T(8,128)(2,1)S(1)}, bf16[1,8,128,128]{3,2,1,0:T(8,128)(2,1)S(1)}, u32[]{:S(2)}, u32[]{:S(2)}) %collective-permute-start.12) | collective-permute-done | bytes 262176 | tf_op jit(solution)/shard_map/ppermute | solution.py:45
  10.5 1.8 collective-permute-start.13
  12.4 1.6 collective-permute-start.15
  20.2 3.7 %collective-permute-done.13 = bf16[2,8,128,128]{3,2,1,0:T(8,128)(2,1)} collective-permute-done((bf16[2,8,128,128]{3,2,1,0:T(8,128)(2,1)S(1)}, bf16[2,8,128,128]{3,2,1,0:T(8,128)(2,1)}, u32[]{:S(2)}, u32[]{:S(2)}) %collective-permute-start.13) | collective-permute-done | bytes 524320 | tf_op jit(solution)/shard_map/ppermute | solution.py:45
  29.5 2.3 %shard_map.92 = (bf16[512,1024]{1,0:T(8,128)(2,1)S(1)}, bf16[128,1024]{1,0:T(8,128)(2,1)S(1)}, bf16[128,1024]{1,0:T(8,128)(2,1)S(1)}, bf16[3,128,512]{2,1,0:T(8,...) custom-call(s32[2]{0:T(128)S(1)} %pad_add_fusion.where, ...), custom_call_target="tpu_custom_call" | custom-call | tf_op jit(solution)/shard_map/pallas_call | solution.py:19
  31.8 1.7 collective-permute-start.2
  36.2 2.3 %collective-permute-start.20 = (bf16[1,128,512]{2,1,0:T(8,128)(2,1)S(1)}, bf16[1,128,512]{2,1,0:T(8,128)(2,1)S(1)}, u32[]{:S(2)}, u32[]{:S(2)}) collective-permute-start(bf16[1,128,512]{2,1,0:T(8,128)(2,1)S(1)} %get-tuple-element.69), channel_id=1, source_target_pairs={{0,3},{1,2},{2,1},{3,0},{4,7},{5,6},{6,5},{7,4},{8,11},{9,10},{10,... | collective-permute-start | bytes 393224 | tf_op jit(solution)/shard_map/ppermute | solution.py:45
  38.4 3.6 %collective-permute-done.20.refs_3_ = bf16[1,128,512]{2,1,0:T(8,128)(2,1)S(1)} collective-permute-done((bf16[1,128,512]{2,1,0:T(8,128)(2,1)S(1)}, bf16[1,128,512]{2,1,0:T(8,128)(2,1)S(1)}, u32[]{:S(2)}, u32[]{:S(2)}) %collective-permute-start.20) | collective-permute-done | bytes 131104 | tf_op jit(solution)/shard_map/ppermute | solution.py:45
  42.0 1.5 collective-permute-start.21
  43.5 1.5 collective-permute-start.22
  45.5 2.8 %shard_map.93 = (bf16[512,512]{1,0:T(8,128)(2,1)S(1)}, bf16[128,512]{1,0:T(8,128)(2,1)S(1)}, bf16[128,512]{1,0:T(8,128)(2,1)S(1)}, bf16[2,128,512]{2,1,0:T(8,128...) custom-call(s32[2]{0:T(128)S(1)} %pad_add_fusion.where, ...), custom_call_target="tpu_custom_call" | custom-call | tf_op jit(solution)/shard_map/pallas_call | solution.py:19
  48.4 5.4 %collective-permute-done.21.refs_5_ = bf16[3,128,512]{2,1,0:T(8,128)(2,1)S(1)} collective-permute-done((bf16[3,128,512]{2,1,0:T(8,128)(2,1)S(1)}, bf16[3,128,512]{2,1,0:T(8,128)(2,1)S(1)}, u32[]{:S(2)}, u32[]{:S(2)}) %collective-permute-start.21) | collective-permute-done | bytes 393248 | tf_op jit(solution)/shard_map/ppermute | solution.py:45
  53.7 2.6 %collective-permute-start.4 = (bf16[128,512]{1,0:T(8,128)(2,1)S(1)}, bf16[128,512]{1,0:T(8,128)(2,1)S(1)}, u32[]{:S(2)}, u32[]{:S(2)}) collective-permute-start(bf16[128,512]{1,0:T(8,128)(2,1)S(1)} %get-tuple-element.56), channel_id=1, source_target_pairs={{0,4},{4,8},{8,12},{12,16},{16,20},{20,24},{24,28},{1,5},{5,9},{9,... | collective-permute-start | bytes 393224 | tf_op jit(solution)/shard_map/ppermute | solution.py:54
  56.3 7.5 %collective-permute-done.22.refs_6_ = bf16[3,128,512]{2,1,0:T(8,128)(2,1)S(1)} collective-permute-done((bf16[3,128,512]{2,1,0:T(8,128)(2,1)S(1)}, bf16[3,128,512]{2,1,0:T(8,128)(2,1)S(1)}, u32[]{:S(2)}, u32[]{:S(2)}) %collective-permute-start.22) | collective-permute-done | bytes 393248 | tf_op jit(solution)/shard_map/ppermute | solution.py:45
  67.1 1.6 collective-permute-start.11
  68.7 2.1 %shard_map.94 = (bf16[1,128,512]{2,1,0:T(8,128)(2,1)S(1)}, bf16[1,128,512]{2,1,0:T(8,128)(2,1)}, bf16[1,128,512]{2,1,0:T(8,128)(2,1)}, bf16[1,128,512]{2,1,0:T(8,128)(2,1)}, bf16[512,512]{1,0:T(8,128)(2,1)}) custom-call(s32[2]{0:T(128)S(1)} %pad_add_fusion.where, bf16[512,512]{1,0:T(8,128)(2,1)S(1)} %copy-done.1, bf16[512,256]{1,0:T(8,128)(2,1)S(1)} %copy-done.4, ...), custom_call_target="tpu_custom_call" | custom-call | tf_op jit(solution)/shard_map/pallas_call | solution.py:19
  71.5 2.7 %collective-permute-done.9.refs_1_ = bf16[2,128,512]{2,1,0:T(8,128)(2,1)S(1)} collective-permute-done((bf16[2,128,512]{2,1,0:T(8,128)(2,1)S(1)}, bf16[2,128,512]{2,1,0:T(8,128)(2,1)S(1)}, u32[]{:S(2)}, u32[]{:S(2)}) %collective-permute-start.9) | collective-permute-done | bytes 262176 | tf_op jit(solution)/shard_map/ppermute | solution.py:45
  78.4 2.1 %collective-permute-start.8 = (bf16[1,128,512]{2,1,0:T(8,128)(2,1)}, bf16[1,128,512]{2,1,0:T(8,128)(2,1)}, u32[]{:S(2)}, u32[]{:S(2)}) collective-permute-start(bf16[1,128,512]{2,1,0:T(8,128)(2,1)} %get-tuple-element.61), channel_id=1, source_target_pairs={{0,3},{1,2},{2,1},{3,0},{4,7},{5,6},{6,5},{7,4},{8,11},{9,10},{10,... | collective-permute-start | bytes 393224 | tf_op jit(solution)/shard_map/ppermute | solution.py:45
  83.0 4.5 %shard_map.95.refs_8_.refs_4_ = bf16[2048,2048]{1,0:T(8,128)(2,1)S(1)} custom-call(s32[2]{0:T(128)S(1)} %pad_add_fusion.where, s32[16,8]{1,0:T(8,128)S(1)} %copy.11.targets, s32[16]{0:T(128)S(1)} %copy-done.31, bf16[4,8,128,128]{3,2,1,0:T(8,128)(2,1)S(1)} %pad_maximum_fusion.refs_0_, bf16[4,8,128,128]{3,2,1,0:T(8,128)(2,1)S(1)} %pad_maximum_fusion.1.refs_1_, ...), custom_call_target="tpu_custom_call" | custom-call | tf_op jit(solution)/shard_map/pallas_call | solution.py:19
  87.5 3.3 %copy-done = bf16[2048,2048]{1,0:T(8,128)(2,1)} copy-done((bf16[2048,2048]{1,0:T(8,128)(2,1)}, bf16[2048,2048]{1,0:T(8,128)(2,1)S(1)}, u32[]{:S(2)}) %copy-start) | copy-done | bytes 8388632
  93.6 14.0 %shard_map.96 = (f32[4,128,512]{2,1,0:T(8,128)S(1)}, f32[4,128,512]{2,1,0:T(8,128)S(1)}, f32[4,128,512]{2,1,0:T(8,128)S(1)}, f32[32,128]{1,0:T(8,128)S(1)}, bf16...) custom-call(s32[2]{0:T(128)S(1)} %pad_add_fusion.where, bf16[1,128,512]{2,1,0:T(8,128)(2,1)S(1)} %copy-done.21, ...), custom_call_target="tpu_custom_call" | custom-call | tf_op jit(solution)/shard_map/pallas_call | solution.py:19
  108.2 6.5 %all-to-all-start = ((f32[32,1,128]{2,1,0:T(1,128)}), f32[32,1,128]{2,1,0:T(1,128)S(1)}, u32[]{:S(2)}, u32[]{:S(2)}) async-start(f32[32,1,128]{2,1,0:T(1,128)} %bitcast.26), calls=%async_computation | async-start | bytes 32768 | tf_op jit(solution)/shard_map/all_to_all | solution.py:302
  114.7 6.9 %all-to-all-done = f32[32,1,128]{2,1,0:T(1,128)S(1)} async-done(((f32[32,1,128]{2,1,0:T(1,128)}), f32[32,1,128]{2,1,0:T(1,128)S(1)}, u32[]{:S(2)}, u32[]{:S(2)}) %all-to-all-start) | async-done | bytes 16416 | tf_op jit(solution)/shard_map/all_to_all | solution.py:302
  123.5 15.1 %shard_map.97 = (f32[4,128,512]{2,1,0:T(8,128)S(1)}, f32[4,128,512]{2,1,0:T(8,128)S(1)}, f32[4,128,512]{2,1,0:T(8,128)S(1)}, f32[4,128,512]{2,1,0:T(8,128)S(1)},...) custom-call(s32[2]{0:T(128)S(1)} %pad_add_fusion.where, ...), custom_call_target="tpu_custom_call" | custom-call | tf_op jit(solution)/shard_map/pallas_call | solution.py:19
  138.6 9.0 %all_to_all.33 = f32[32,1,128]{2,1,0:T(1,128)S(1)} all-to-all(f32[32,1,128]{2,1,0:T(1,128)S(1)} %bitcast.27), channel_id=1, replica_groups=mesh['space'=8,'mode'=4] {'space','mode'}, dimensions={0} | all-to-all | bytes 32768 | tf_op jit(solution)/shard_map/all_to_all | solution.py:302
  148.1 12.8 %shard_map.98 = (bf16[128,512]{1,0:T(8,128)(2,1)S(1)}, bf16[128,512]{1,0:T(8,128)(2,1)S(1)}, bf16[128,512]{1,0:T(8,128)(2,1)S(1)}, bf16[128,512]{1,0:T(8,128)(2,...) custom-call(s32[2]{0:T(128)S(1)} %pad_add_fusion.where, ...), custom_call_target="tpu_custom_call" | custom-call | tf_op jit(solution)/shard_map/pallas_call | solution.py:19
  161.4 1.5 collective-permute-start.24
  165.5 1.8 collective-permute-done.27.refs_5_
  167.9 13.9 %all_to_all.34 = f32[32,1,128]{2,1,0:T(1,128)S(1)} all-to-all(f32[32,1,128]{2,1,0:T(1,128)S(1)} %bitcast.25), channel_id=1, replica_groups=mesh['space'=8,'mode'=4] {'space','mode'}, dimensions={0} | all-to-all | bytes 32768 | tf_op jit(solution)/shard_map/all_to_all | solution.py:302
  181.9 1.9 %shard_map.100 = f32[512,512]{1,0:T(8,128)} custom-call(s32[2]{0:T(128)S(1)} %pad_add_fusion.where, f32[512,512]{1,0:T(8,128)S(1)} %copy-done.3, f32[32,128]{1,0:T(8,128)S(1)} %bitcast.24, bf16[2,128,512]{2,1,0:T(8,128)(2,1)S(1)} %get-tuple-element.85.refs_0_, bf16[2,128,512]{2,1,0:T(8,128)(2,1)S(1)} %collective-permute-done.24.refs_1_, ...), custom_call_target="tpu_custom_call" | custom-call | tf_op jit(solution)/shard_map/pallas_call | solution.py:19
  (118 shorter events, 36.0 us)
Async XLA Ops:
  0.0 80.6 %copy-start.31 = (s32[16]{0:T(128)S(1)}, s32[16]{0:T(128)}, u32[]{:S(2)}) copy-start(s32[16]{0:T(128)} %counts.1) | copy-start | bytes 196
  1.2 9.3 %collective-permute-start.12 = (bf16[1,8,128,128]{3,2,1,0:T(8,128)(2,1)S(1)}, bf16[1,8,128,128]{3,2,1,0:T(8,128)(2,1)S(1)}, u32[]{:S(2)}, u32[]{:S(2)}) collective-permute-start(bf16[1,8,128,128]{3,2,1,0:T(8,128)(2,1)S(1)} %get-tuple-element.94), channel_id=1, source_target_pairs={{0,1},{1,0},{2,3},{3,2},{4,5},{5,4},{6,7},{7,6},{8,9},{9,8},{10,11... | collective-permute-start | bytes 786440 | tf_op jit(solution)/shard_map/ppermute | solution.py:45
  4.2 8.2 %collective-permute-start.14 = (bf16[1,8,128,128]{3,2,1,0:T(8,128)(2,1)S(1)}, bf16[1,8,128,128]{3,2,1,0:T(8,128)(2,1)S(1)}, u32[]{:S(2)}, u32[]{:S(2)}) collective-permute-start(bf16[1,8,128,128]{3,2,1,0:T(8,128)(2,1)S(1)} %get-tuple-element.93), channel_id=1, source_target_pairs={{0,2},{1,3},{2,0},{3,1},{4,6},{5,7},{6,4},{7,5},{8,10},{9,11},{10,... | collective-permute-start | bytes 786440 | tf_op jit(solution)/shard_map/ppermute | solution.py:45
  10.5 13.3 %collective-permute-start.13 = (bf16[2,8,128,128]{3,2,1,0:T(8,128)(2,1)S(1)}, bf16[2,8,128,128]{3,2,1,0:T(8,128)(2,1)}, u32[]{:S(2)}, u32[]{:S(2)}) collective-permute-start(bf16[2,8,128,128]{3,2,1,0:T(8,128)(2,1)S(1)} %pad_maximum_fusion.2), channel_id=1, source_target_pairs={{0,2},{1,3},{2,0},{3,1},{4,6},{5,7},{6,4},{7,5},{8,10},{9,11},{10,... | collective-permute-start | bytes 1572872 | tf_op jit(solution)/shard_map/ppermute | solution.py:45
  12.4 12.7 %collective-permute-start.15 = (bf16[2,8,128,128]{3,2,1,0:T(8,128)(2,1)S(1)}, bf16[2,8,128,128]{3,2,1,0:T(8,128)(2,1)}, u32[]{:S(2)}, u32[]{:S(2)}) collective-permute-start(bf16[2,8,128,128]{3,2,1,0:T(8,128)(2,1)S(1)} %pad_maximum_fusion.3), channel_id=1, source_target_pairs={{0,1},{1,0},{2,3},{3,2},{4,5},{5,4},{6,7},{7,6},{8,9},{9,8},{10,11... | collective-permute-start | bytes 1572872 | tf_op jit(solution)/shard_map/ppermute | solution.py:45
  16.9 9.9 %collective-permute-start = (bf16[128,512]{1,0:T(8,128)(2,1)S(1)}, bf16[128,512]{1,0:T(8,128)(2,1)S(1)}, u32[]{:S(2)}, u32[]{:S(2)}) collective-permute-start(bf16[128,512]{1,0:T(8,128)(2,1)S(1)} %get-tuple-element.50), channel_id=1, source_target_pairs={{0,4},{4,8},{8,12},{12,16},{16,20},{20,24},{24,28},{1,5},{5,9},{9,... | collective-permute-start | bytes 393224 | tf_op jit(solution)/shard_map/ppermute | solution.py:54
  18.3 10.0 %collective-permute-start.1 = (bf16[128,512]{1,0:T(8,128)(2,1)S(1)}, bf16[128,512]{1,0:T(8,128)(2,1)S(1)}, u32[]{:S(2)}, u32[]{:S(2)}) collective-permute-start(bf16[128,512]{1,0:T(8,128)(2,1)S(1)} %get-tuple-element.51), channel_id=1, source_target_pairs={{4,0},{8,4},{12,8},{16,12},{20,16},{24,20},{28,24},{5,1},{9,5},{13... | collective-permute-start | bytes 393224 | tf_op jit(solution)/shard_map/ppermute | solution.py:55
  19.6 14.0 %collective-permute-start.18 = (bf16[1,128,512]{2,1,0:T(8,128)(2,1)S(1)}, bf16[1,128,512]{2,1,0:T(8,128)(2,1)S(1)}, u32[]{:S(2)}, u32[]{:S(2)}) collective-permute-start(bf16[1,128,512]{2,1,0:T(8,128)(2,1)S(1)} %get-tuple-element.67), channel_id=1, source_target_pairs={{0,1},{1,0},{2,3},{3,2},{4,5},{5,4},{6,7},{7,6},{8,9},{9,8},{10,11... | collective-permute-start | bytes 393224 | tf_op jit(solution)/shard_map/ppermute | solution.py:45
  25.0 50.0 %collective-permute-start.16 = (bf16[4,8,128,128]{3,2,1,0:T(8,128)(2,1)S(1)}, bf16[4,8,128,128]{3,2,1,0:T(8,128)(2,1)S(1)}, u32[]{:S(2)}, u32[]{:S(2)}) collective-permute-start(bf16[4,8,128,128]{3,2,1,0:T(8,128)(2,1)S(1)} %pad_maximum_fusion.refs_0_), channel_id=1, source_target_pairs={{0,4},{4,0},{8,12},{12,8},{16,20},{20,16},{24,28},{28,24},{1,5},{5... | collective-permute-start | bytes 3145736 | tf_op jit(solution)/shard_map/ppermute | solution.py:45
  26.3 51.0 %collective-permute-start.17 = (bf16[4,8,128,128]{3,2,1,0:T(8,128)(2,1)S(1)}, bf16[4,8,128,128]{3,2,1,0:T(8,128)(2,1)S(1)}, u32[]{:S(2)}, u32[]{:S(2)}) collective-permute-start(bf16[4,8,128,128]{3,2,1,0:T(8,128)(2,1)S(1)} %pad_maximum_fusion.1.refs_1_), channel_id=1, source_target_pairs={{0,4},{4,0},{8,12},{12,8},{16,20},{20,16},{24,28},{28,24},{1,5},{5... | collective-permute-start | bytes 3145736 | tf_op jit(solution)/shard_map/ppermute | solution.py:45
  26.8 8.7 %collective-permute-start.19 = (bf16[1,128,512]{2,1,0:T(8,128)(2,1)S(1)}, bf16[1,128,512]{2,1,0:T(8,128)(2,1)S(1)}, u32[]{:S(2)}, u32[]{:S(2)}) collective-permute-start(bf16[1,128,512]{2,1,0:T(8,128)(2,1)S(1)} %get-tuple-element.68), channel_id=1, source_target_pairs={{0,2},{1,3},{2,0},{3,1},{4,6},{5,7},{6,4},{7,5},{8,10},{9,11},{10,... | collective-permute-start | bytes 393224 | tf_op jit(solution)/shard_map/ppermute | solution.py:45
  31.8 11.7 %collective-permute-start.2 = (bf16[128,1024]{1,0:T(8,128)(2,1)S(1)}, bf16[128,1024]{1,0:T(8,128)(2,1)S(1)}, u32[]{:S(2)}, u32[]{:S(2)}) collective-permute-start(bf16[128,1024]{1,0:T(8,128)(2,1)S(1)} %get-tuple-element.53), channel_id=1, source_target_pairs={{0,4},{4,8},{8,12},{12,16},{16,20},{20,24},{24,28},{1,5},{5,9},{9,... | collective-permute-start | bytes 786440 | tf_op jit(solution)/shard_map/ppermute | solution.py:54
  34.2 10.9 %collective-permute-start.3 = (bf16[128,1024]{1,0:T(8,128)(2,1)S(1)}, bf16[128,1024]{1,0:T(8,128)(2,1)S(1)}, u32[]{:S(2)}, u32[]{:S(2)}) collective-permute-start(bf16[128,1024]{1,0:T(8,128)(2,1)S(1)} %get-tuple-element.54), channel_id=1, source_target_pairs={{4,0},{8,4},{12,8},{16,12},{20,16},{24,20},{28,24},{5,1},{9,5},{13... | collective-permute-start | bytes 786440 | tf_op jit(solution)/shard_map/ppermute | solution.py:55
  36.2 5.9 %collective-permute-start.20 = (bf16[1,128,512]{2,1,0:T(8,128)(2,1)S(1)}, bf16[1,128,512]{2,1,0:T(8,128)(2,1)S(1)}, u32[]{:S(2)}, u32[]{:S(2)}) collective-permute-start(bf16[1,128,512]{2,1,0:T(8,128)(2,1)S(1)} %get-tuple-element.69), channel_id=1, source_target_pairs={{0,3},{1,2},{2,1},{3,0},{4,7},{5,6},{6,5},{7,4},{8,11},{9,10},{10,... | collective-permute-start | bytes 393224 | tf_op jit(solution)/shard_map/ppermute | solution.py:45
  42.0 11.7 %collective-permute-start.21 = (bf16[3,128,512]{2,1,0:T(8,128)(2,1)S(1)}, bf16[3,128,512]{2,1,0:T(8,128)(2,1)S(1)}, u32[]{:S(2)}, u32[]{:S(2)}) collective-permute-start(bf16[3,128,512]{2,1,0:T(8,128)(2,1)S(1)} %get-tuple-element.71), channel_id=1, source_target_pairs={{0,1},{1,0},{2,3},{3,2},{4,5},{5,4},{6,7},{7,6},{8,9},{9,8},{10,11... | collective-permute-start | bytes 1179656 | tf_op jit(solution)/shard_map/ppermute | solution.py:45
  43.5 20.3 %collective-permute-start.22 = (bf16[3,128,512]{2,1,0:T(8,128)(2,1)S(1)}, bf16[3,128,512]{2,1,0:T(8,128)(2,1)S(1)}, u32[]{:S(2)}, u32[]{:S(2)}) collective-permute-start(bf16[3,128,512]{2,1,0:T(8,128)(2,1)S(1)} %get-tuple-element.72), channel_id=1, source_target_pairs={{0,2},{1,3},{2,0},{3,1},{4,6},{5,7},{6,4},{7,5},{8,10},{9,11},{10,... | collective-permute-start | bytes 1179656 | tf_op jit(solution)/shard_map/ppermute | solution.py:45
  45.1 20.1 %collective-permute-start.23 = (bf16[3,128,512]{2,1,0:T(8,128)(2,1)S(1)}, bf16[3,128,512]{2,1,0:T(8,128)(2,1)S(1)}, u32[]{:S(2)}, u32[]{:S(2)}) collective-permute-start(bf16[3,128,512]{2,1,0:T(8,128)(2,1)S(1)} %get-tuple-element.73), channel_id=1, source_target_pairs={{0,3},{1,2},{2,1},{3,0},{4,7},{5,6},{6,5},{7,4},{8,11},{9,10},{10,... | collective-permute-start | bytes 1179656 | tf_op jit(solution)/shard_map/ppermute | solution.py:45
  53.7 11.5 %collective-permute-start.4 = (bf16[128,512]{1,0:T(8,128)(2,1)S(1)}, bf16[128,512]{1,0:T(8,128)(2,1)S(1)}, u32[]{:S(2)}, u32[]{:S(2)}) collective-permute-start(bf16[128,512]{1,0:T(8,128)(2,1)S(1)} %get-tuple-element.56), channel_id=1, source_target_pairs={{0,4},{4,8},{8,12},{12,16},{16,20},{20,24},{24,28},{1,5},{5,9},{9,... | collective-permute-start | bytes 393224 | tf_op jit(solution)/shard_map/ppermute | solution.py:54
  63.8 3.2 %collective-permute-start.5 = (bf16[128,512]{1,0:T(8,128)(2,1)S(1)}, bf16[128,512]{1,0:T(8,128)(2,1)S(1)}, u32[]{:S(2)}, u32[]{:S(2)}) collective-permute-start(bf16[128,512]{1,0:T(8,128)(2,1)S(1)} %get-tuple-element.57), channel_id=1, source_target_pairs={{4,0},{8,4},{12,8},{16,12},{20,16},{24,20},{28,24},{5,1},{9,5},{13... | collective-permute-start | bytes 393224 | tf_op jit(solution)/shard_map/ppermute | solution.py:55
  65.1 9.1 %collective-permute-start.9 = (bf16[2,128,512]{2,1,0:T(8,128)(2,1)S(1)}, bf16[2,128,512]{2,1,0:T(8,128)(2,1)S(1)}, u32[]{:S(2)}, u32[]{:S(2)}) collective-permute-start(bf16[2,128,512]{2,1,0:T(8,128)(2,1)S(1)} %get-tuple-element.63), channel_id=1, source_target_pairs={{0,1},{1,0},{2,3},{3,2},{4,5},{5,4},{6,7},{7,6},{8,9},{9,8},{10,11... | collective-permute-start | bytes 786440 | tf_op jit(solution)/shard_map/ppermute | solution.py:45
  65.2 49.5 %collective-permute-start.10 = (bf16[2,128,512]{2,1,0:T(8,128)(2,1)}, bf16[2,128,512]{2,1,0:T(8,128)(2,1)}, u32[]{:S(2)}, u32[]{:S(2)}) collective-permute-start(bf16[2,128,512]{2,1,0:T(8,128)(2,1)} %get-tuple-element.64), channel_id=1, source_target_pairs={{0,2},{1,3},{2,0},{3,1},{4,6},{5,7},{6,4},{7,5},{8,10},{9,11},{10,... | collective-permute-start | bytes 786440 | tf_op jit(solution)/shard_map/ppermute | solution.py:45
  67.1 47.7 %collective-permute-start.11 = (bf16[2,128,512]{2,1,0:T(8,128)(2,1)}, bf16[2,128,512]{2,1,0:T(8,128)(2,1)}, u32[]{:S(2)}, u32[]{:S(2)}) collective-permute-start(bf16[2,128,512]{2,1,0:T(8,128)(2,1)} %get-tuple-element.65), channel_id=1, source_target_pairs={{0,3},{1,2},{2,1},{3,0},{4,7},{5,6},{6,5},{7,4},{8,11},{9,10},{10,... | collective-permute-start | bytes 786440 | tf_op jit(solution)/shard_map/ppermute | solution.py:45
  74.9 73.1 %collective-permute-start.6 = (bf16[1,128,512]{2,1,0:T(8,128)(2,1)}, bf16[1,128,512]{2,1,0:T(8,128)(2,1)}, u32[]{:S(2)}, u32[]{:S(2)}) collective-permute-start(bf16[1,128,512]{2,1,0:T(8,128)(2,1)} %get-tuple-element.59), channel_id=1, source_target_pairs={{0,1},{1,0},{2,3},{3,2},{4,5},{5,4},{6,7},{7,6},{8,9},{9,8},{10,11... | collective-permute-start | bytes 393224 | tf_op jit(solution)/shard_map/ppermute | solution.py:45
  75.9 72.2 %collective-permute-start.7 = (bf16[1,128,512]{2,1,0:T(8,128)(2,1)}, bf16[1,128,512]{2,1,0:T(8,128)(2,1)}, u32[]{:S(2)}, u32[]{:S(2)}) collective-permute-start(bf16[1,128,512]{2,1,0:T(8,128)(2,1)} %get-tuple-element.60), channel_id=1, source_target_pairs={{0,2},{1,3},{2,0},{3,1},{4,6},{5,7},{6,4},{7,5},{8,10},{9,11},{10,... | collective-permute-start | bytes 393224 | tf_op jit(solution)/shard_map/ppermute | solution.py:45
  78.4 69.7 %collective-permute-start.8 = (bf16[1,128,512]{2,1,0:T(8,128)(2,1)}, bf16[1,128,512]{2,1,0:T(8,128)(2,1)}, u32[]{:S(2)}, u32[]{:S(2)}) collective-permute-start(bf16[1,128,512]{2,1,0:T(8,128)(2,1)} %get-tuple-element.61), channel_id=1, source_target_pairs={{0,3},{1,2},{2,1},{3,0},{4,7},{5,6},{6,5},{7,4},{8,11},{9,10},{10,... | collective-permute-start | bytes 393224 | tf_op jit(solution)/shard_map/ppermute | solution.py:45
  108.2 13.5 %all-to-all-start = ((f32[32,1,128]{2,1,0:T(1,128)}), f32[32,1,128]{2,1,0:T(1,128)S(1)}, u32[]{:S(2)}, u32[]{:S(2)}) async-start(f32[32,1,128]{2,1,0:T(1,128)} %bitcast.26), calls=%async_computation | async-start | bytes 32768 | tf_op jit(solution)/shard_map/all_to_all | solution.py:302
  160.9 6.4 %collective-permute-start.27 = (bf16[128,512]{1,0:T(8,128)(2,1)S(1)}, bf16[128,512]{1,0:T(8,128)(2,1)S(1)}, u32[]{:S(2)}, u32[]{:S(2)}) collective-permute-start(bf16[128,512]{1,0:T(8,128)(2,1)S(1)} %get-tuple-element.90), channel_id=1, source_target_pairs={{0,1},{1,0},{2,3},{3,2},{4,5},{5,4},{6,7},{7,6},{8,9},{9,8},{10,11... | collective-permute-start | bytes 393224 | tf_op jit(solution)/shard_map/ppermute | solution.py:45
  161.4 20.4 %collective-permute-start.24 = (bf16[2,128,512]{2,1,0:T(8,128)(2,1)S(1)}, bf16[2,128,512]{2,1,0:T(8,128)(2,1)S(1)}, u32[]{:S(2)}, u32[]{:S(2)}) collective-permute-start(bf16[2,128,512]{2,1,0:T(8,128)(2,1)S(1)} %get-tuple-element.86), channel_id=1, source_target_pairs={{0,1},{1,0},{2,3},{3,2},{4,5},{5,4},{6,7},{7,6},{8,9},{9,8},{10,11... | collective-permute-start | bytes 786440 | tf_op jit(solution)/shard_map/ppermute | solution.py:45
  163.0 18.9 %collective-permute-start.25 = (bf16[2,128,512]{2,1,0:T(8,128)(2,1)S(1)}, bf16[2,128,512]{2,1,0:T(8,128)(2,1)S(1)}, u32[]{:S(2)}, u32[]{:S(2)}) collective-permute-start(bf16[2,128,512]{2,1,0:T(8,128)(2,1)S(1)} %get-tuple-element.87), channel_id=1, source_target_pairs={{0,2},{1,3},{2,0},{3,1},{4,6},{5,7},{6,4},{7,5},{8,10},{9,11},{10,... | collective-permute-start | bytes 786440 | tf_op jit(solution)/shard_map/ppermute | solution.py:45
  163.5 18.4 %collective-permute-start.26 = (bf16[2,128,512]{2,1,0:T(8,128)(2,1)S(1)}, bf16[2,128,512]{2,1,0:T(8,128)(2,1)S(1)}, u32[]{:S(2)}, u32[]{:S(2)}) collective-permute-start(bf16[2,128,512]{2,1,0:T(8,128)(2,1)S(1)} %get-tuple-element.88), channel_id=1, source_target_pairs={{0,3},{1,2},{2,1},{3,0},{4,7},{5,6},{6,5},{7,4},{8,11},{9,10},{10,... | collective-permute-start | bytes 786440 | tf_op jit(solution)/shard_map/ppermute | solution.py:45
  164.9 16.9 %collective-permute-start.28 = (bf16[128,512]{1,0:T(8,128)(2,1)S(1)}, bf16[128,512]{1,0:T(8,128)(2,1)S(1)}, u32[]{:S(2)}, u32[]{:S(2)}) collective-permute-start(bf16[128,512]{1,0:T(8,128)(2,1)S(1)} %get-tuple-element.91), channel_id=1, source_target_pairs={{0,2},{1,3},{2,0},{3,1},{4,6},{5,7},{6,4},{7,5},{8,10},{9,11},{10,... | collective-permute-start | bytes 393224 | tf_op jit(solution)/shard_map/ppermute | solution.py:45
  167.3 14.5 %collective-permute-start.29 = (bf16[128,512]{1,0:T(8,128)(2,1)S(1)}, bf16[128,512]{1,0:T(8,128)(2,1)S(1)}, u32[]{:S(2)}, u32[]{:S(2)}) collective-permute-start(bf16[128,512]{1,0:T(8,128)(2,1)S(1)} %get-tuple-element.92), channel_id=1, source_target_pairs={{0,3},{1,2},{2,1},{3,0},{4,7},{5,6},{6,5},{7,4},{8,11},{9,10},{10,... | collective-permute-start | bytes 393224 | tf_op jit(solution)/shard_map/ppermute | solution.py:45
  (33 other events, 391.2 us)

commit v2 on v0

v2 whole, which is shorter than its diff:
```python
import functools

import jax
import jax.numpy as jnp
from jax import lax
from jax.experimental import pallas as pl
from jax.experimental.pallas import tpu as pltpu
from jax.sharding import PartitionSpec as P


step_gain = 0.5
F32 = jnp.float32
BF16 = jnp.bfloat16
VMEM = pl.BlockSpec(memory_space=pltpu.VMEM)
SMEM = pl.BlockSpec(memory_space=pltpu.SMEM)
HBM = pl.BlockSpec(memory_space=pltpu.HBM)


def call(body, outs, args, scalars=0, scratch=(), far=0, limit=16):
    far_at = slice(scalars, scalars + far)

    def whole(*refs):
        refs = list(refs)
        if far:
            sems = refs.pop()
            near = refs[len(refs) - far :]
            del refs[len(refs) - far :]
            copies = [
                pltpu.make_async_copy(a, b, sems.at[i])
                for i, (a, b) in enumerate(zip(refs[far_at], near))
            ]
            for copy in copies:
                copy.start()
            for copy in copies:
                copy.wait()
            refs[far_at] = near
        body(*refs)

    brought = [pltpu.VMEM(leaf.shape, leaf.dtype) for leaf in args[far_at]]
    return pl.pallas_call(
        whole,
        out_shape=outs,
        in_specs=[SMEM] * scalars
        + [HBM] * far
        + [VMEM] * (len(args) - scalars - far),
        out_specs=[VMEM] * len(outs),
        scratch_shapes=[pltpu.VMEM(leaf.shape, leaf.dtype) for leaf in scratch]
        + brought
        + ([pltpu.SemaphoreType.DMA((far,))] if far else []),
        compiler_params=pltpu.CompilerParams(vmem_limit_bytes=limit << 20),
        cost_estimate=pl.CostEstimate(flops=1, bytes_accessed=1, transcendentals=0),
    )(*args)


def shaped(shape, dtype=BF16):
    return jax.ShapeDtypeStruct(shape, dtype)


def rows_of(owner, rows):
    return pl.ds(pl.multiple_of(owner * rows, rows), rows)


def mm(a, b):
    return jnp.dot(a, b, preferred_element_type=F32)


def mmt(a, b):
    return lax.dot_general(a, b, (((1,), (1,)), ((), ())), preferred_element_type=F32)


def flip_permute(x, axis, bit):
    return lax.ppermute(x, axis, [(i, i ^ bit) for i in range(lax.axis_size(axis))])


def trade(pieces):
    return [pieces[0]] + [flip_permute(p, "mode", k) for k, p in enumerate(pieces) if k > 0]


def halo(lower, upper):
    count = lax.axis_size("space")
    below = lax.ppermute(upper, "space", [(i, i + 1) for i in range(count - 1)])
    above = lax.ppermute(lower, "space", [(i + 1, i) for i in range(count - 1)])
    return below, above


def picked_rows(pick, x, lower, upper):
    ghost = lower.shape[0]
    rows = mm(pick[...], x).astype(BF16)
    lower[...] = rows[:ghost]
    upper[...] = rows[ghost:]


def start_body(u_ref, pick, whole, lower, upper):
    whole[...] = u_ref[...].astype(BF16)
    picked_rows(pick, whole[...], lower, upper)


def spatial_of(diag, ghostly, x, below, above):
    ghost = below.shape[0]
    y = mm(diag[...], x[...])
    y = y + mm(ghostly[:, :ghost], below[...])
    return y + mm(ghostly[:, ghost:], above[...])


def first_body(n, where, diag, ghostly, f_ref, x, below, above, pick, *outs):
    both, lower, upper = outs[:3]
    low = outs[-1]
    nodes, width = x.shape
    s = spatial_of(diag, ghostly, x, below, above)
    p = f_ref[...] - s
    high = p.astype(BF16)
    both[:, :width] = s.astype(BF16)
    both[:, width:] = high
    low[...] = (p - high.astype(F32)).astype(BF16)
    picked_rows(pick, both[...], lower, upper)
    for k in range(n):
        at = rows_of(where[0] ^ k, nodes // n)
        outs[3 + k][0] = x[at, :]
        outs[3 + k][1] = both[at, width:]
        outs[3 + k][2] = low[at, :]
        outs[3 + k][3] = both[at, :width]


def second_body(diag, ghostly, x, below, above, pick, both, p1, lower, upper):
    both[...] = spatial_of(diag, ghostly, x, below, above).astype(BF16)
    p1[...] = both[:, both.shape[1] // 2 :]
    picked_rows(pick, p1[...], lower, upper)


def third_body(n, where, diag, ghostly, both, x, below, above, *outs):
    rows = x.shape[0] // n
    width = x.shape[1]
    whole = outs[-1]
    whole[...] = spatial_of(diag, ghostly, x, below, above).astype(BF16)
    for k in range(n):
        at = rows_of(where[0] ^ k, rows)
        outs[k][0] = both[at, :width]
        outs[k][1] = x[at, :]
        outs[k][2] = whole[at, :]


def table_body(n, slots, where, targets, counts, own, *refs):
    *refs, out = refs
    width = own.shape[-1]
    entries = own.shape[0]
    per = entries // slots
    quarter = entries // 4
    step = 256

    def clear(i, carry):
        out[rows_of(i, step), :] = jnp.zeros((step, out.shape[1]), out.dtype)
        return carry

    lax.fori_loop(0, out.shape[0] // step, clear, 0)

    def fill(owner, base, count, get):
        def place(i, carry):
            entry = base + i
            source = owner * per + entry // slots
            slot = entry % slots

            @pl.when(slot < counts[source])
            def _():
                out[rows_of(source, width), rows_of(targets[source, slot], width)] = get(i)

            return carry

        lax.fori_loop(0, count, place, 0)

    fill(where[0], 0, entries, lambda i: own[i])
    for which in range(4):
        for k in range(1, n):
            fill(
                where[0] ^ k,
                (where[1] ^ which) * quarter,
                quarter,
                lambda i, which=which, k=k: refs[which][k - 1, i],
            )


def by_table(n, me, get, table, emit):
    width = table.shape[0] // n
    for g in range(n):
        total = None
        for k in range(n):
            part = mm(get(k), table[rows_of(me ^ k, width), rows_of(me ^ g, width)])
            total = part if total is None else total + part
        emit(g, total)


def by_inverse(n, me, get, inverse, emit):
    width = inverse.shape[0] // n
    for g in range(n):
        total = None
        for k in range(n):
            part = mmt(get(k), inverse[rows_of(me ^ g, width), rows_of(me ^ k, width)])
            total = part if total is None else total + part
        emit(g, total)


def stage_a(n, where, *refs):
    ps = refs[:n]
    chaos, inverse, w0, c1, ca0 = refs[n : n + 5]
    outs = refs[n + 5 : 2 * n + 5]
    pair, quick = refs[2 * n + 5 :]
    me = where[0]
    rows = w0.shape[1]

    def residual(g, value):
        r = ps[g][1].astype(F32) + ps[g][2].astype(F32) - value[:rows]
        high = r.astype(BF16)
        pair[g, :rows] = high
        pair[g, rows:] = (r - high.astype(F32)).astype(BF16)
        c1[g] = value[rows:]

    by_table(n, me, lambda k: jnp.concatenate([ps[k][0], ps[k][3]], axis=0), chaos, residual)

    def updated(g, value):
        w = value[:rows] + value[rows:]
        w0[g] = w
        high = w.astype(BF16)
        quick[g] = high
        outs[g][0] = high
        outs[g][1] = (w - high.astype(F32)).astype(BF16)

    by_inverse(n, me, lambda k: pair[k], inverse, updated)

    def coupled(g, value):
        ca0[g] = value

    by_table(n, me, lambda k: quick[k], chaos, coupled)


def stage_b(n, where, *refs):
    qs = refs[:n]
    chaos, inverse, w0, c1, ca0 = refs[n : n + 5]
    outs = refs[n + 5 : 2 * n + 5]
    v1, held, sums_out, pair, more = refs[2 * n + 5 :]
    me = where[0]
    rows = w0.shape[1]
    for g in range(n):
        pair[g, :rows] = (qs[g][1].astype(F32) - c1[g]).astype(BF16)

    def residual(g, value):
        pair[g, rows:] = (qs[g][2].astype(F32) - value).astype(BF16)

    by_table(n, me, lambda k: qs[k][0], chaos, residual)

    def moved(g, value):
        more[g, :rows] = value[:rows].astype(BF16)
        held[g] = value[rows:]
        more[g, rows:] = (value[:rows] + ca0[g]).astype(BF16)

    by_inverse(n, me, lambda k: pair[k], inverse, moved)

    def coupled(g, value):
        pair[g, :rows] = more[g, rows:]
        pair[g, rows:] = (held[g] + value).astype(BF16)

    by_table(n, me, lambda k: more[k, :rows], chaos, coupled)
    sums = [0.0] * 3

    def first(g, value):
        v = value[:rows]
        v1[g] = v
        outs[g][0] = v.astype(BF16)
        held[g] = value[rows:]
        sums[0] += jnp.sum(w0[g] * w0[g])
        sums[1] += jnp.sum(w0[g] * v)
        sums[2] += jnp.sum(v * v)

    by_inverse(n, me, lambda k: pair[k], inverse, first)
    lanes_of(sums_out, sums, 0)


def lanes_of(out, sums, base):
    lane = lax.broadcasted_iota(jnp.int32, out.shape, 1)
    row = jnp.zeros(out.shape, F32)
    for at, value in enumerate(sums):
        row = jnp.where(lane == base + at, value, row)
    out[...] = row


def stage_c(n, where, chaos, inverse, w0, v1, held, sums_in, *refs):
    outs = refs[:n]
    dots, one, two = refs[n:]
    me = where[0]
    for g in range(n):
        one[g] = v1[g].astype(BF16)

    def last_in(g, value):
        two[g] = (held[g] + value).astype(BF16)

    by_table(n, me, lambda k: one[k], chaos, last_in)
    sums = [0.0] * 3

    def second(g, value):
        outs[g][0] = value.astype(BF16)
        sums[0] += jnp.sum(w0[g] * value)
        sums[1] += jnp.sum(v1[g] * value)
        sums[2] += jnp.sum(value * value)

    by_inverse(n, me, lambda k: two[k], inverse, second)
    lanes_of(dots, sums, 3)
    dots[...] = dots[...] + sums_in[...]


def end_body(n, cells, where, u_ref, dots, *refs):
    ws, vs, xs, out = refs[:n], refs[n : 2 * n], refs[2 * n : 3 * n], refs[3 * n]
    rows = u_ref.shape[0] // n
    means = jnp.sum(dots[...], axis=0, keepdims=True) / cells
    lane = lax.broadcasted_iota(jnp.int32, means.shape, 1)
    g00, g01, g11, g02, g12, g22 = [
        jnp.sum(jnp.where(lane == at, means, 0.0), axis=1, keepdims=True) for at in range(6)
    ]

    def damping(mean):
        return step_gain / jnp.sqrt(jnp.maximum(mean, 0.0) + 1e-06)

    d0 = damping(g00)
    d1 = damping(g00 - 2.0 * d0 * g01 + d0 * d0 * g11)
    a, b = d0 + d1, d0 * d1
    d2 = damping(
        g00 + a * a * g11 + b * b * g22 - 2.0 * a * g01 + 2.0 * b * g02 - 2.0 * a * b * g12
    )
    x0 = d0 + d1 + d2
    x1 = -(d1 * d0 + d2 * a)
    x2 = d2 * b
    for k in range(n):
        at = rows_of(where[0] ^ k, rows)
        w = ws[k][0].astype(F32) + ws[k][1].astype(F32)
        moved = x0 * w + x1 * vs[k][0].astype(F32) + x2 * xs[k][0].astype(F32)
        out[at, :] = u_ref[at, :] + moved


def gather_start(own, quarter, n):
    size = own.shape[0] // 4
    mine = lax.dynamic_slice_in_dim(own, quarter * size, size, 0)
    return [flip_permute(mine, "mode", k) for k in range(1, n)]


def gather_end(here, there):
    return [here, flip_permute(here, "space", 1), there, flip_permute(there, "space", 1)]


def shards(
    guess,
    forcing,
    spatial_diag,
    spatial_ghost,
    ghost_rows,
    chaos_vals,
    chaos_targets,
    chaos_count,
    mean_inverse,
):
    n = lax.axis_size("mode")
    devices = n * lax.axis_size("space")
    nodes, width = guess.shape
    rows = nodes // n
    ghost = ghost_rows.shape[1]
    modes = mean_inverse.shape[0]
    slots = chaos_targets.shape[1]
    cells = float(nodes * width * devices)
    me = lax.axis_index("mode").astype(jnp.int32)
    quarter = (lax.axis_index("space") % 4).astype(jnp.int32)
    where = jnp.stack([me, quarter])
    pick = (ghost_rows.reshape(-1)[:, None] == jnp.arange(nodes, dtype=jnp.int32)[None, :]).astype(
        BF16
    )

    def sent(count):
        return [shaped((count, rows, width))] * n

    def edges(times):
        return [shaped((ghost, times * width))] * 2

    one, two = shaped((nodes, width)), shaped((nodes, 2 * width))
    own = jnp.swapaxes(chaos_vals, 1, 2)
    pieces = gather_start(own, quarter, n)
    whole, lower, upper = call(start_body, [one] + edges(1), [guess, pick], far=1, limit=56)
    below, above = halo(lower, upper)
    both, lower, upper, *ps = call(
        functools.partial(first_body, n),
        [two] + edges(2) + sent(4),
        [where, spatial_diag, spatial_ghost, forcing, whole, below, above, pick],
        1,
        [one],
        3,
        56,
    )
    below, above = halo(lower, upper)
    ps = trade(ps)
    pieces, below, above = lax.optimization_barrier((pieces, below, above))
    here = jnp.stack(pieces)
    there = flip_permute(here, "space", 2)
    both, p1, lower, upper = call(
        second_body,
        [two, one] + edges(1),
        [spatial_diag, spatial_ghost, both, below, above, pick],
        far=2,
        limit=56,
    )
    below, above = halo(lower, upper)
    ps, below, above = lax.optimization_barrier((ps, below, above))
    qs = call(
        functools.partial(third_body, n),
        sent(3),
        [where, spatial_diag, spatial_ghost, both, p1, below, above],
        1,
        [one],
        2,
        56,
    )
    here, there, qs = lax.optimization_barrier((here, there, qs))
    qs = trade(qs)
    tables = gather_end(here, there)

    (chaos,) = call(
        functools.partial(table_body, n, slots),
        [shaped((modes, modes))],
        [where, chaos_targets, chaos_count, own] + tables,
        3,
    )
    slab = shaped((n, rows, width), F32)
    double = shaped((n, 2 * rows, width))
    w0, c1, ca0, *ws = call(
        functools.partial(stage_a, n),
        [slab, slab, slab] + sent(2),
        [where] + ps + [chaos, mean_inverse],
        1,
        [double, shaped((n, rows, width))],
    )
    ws = trade(ws)
    tile = shaped((devices, 128), F32)
    *vs, v1, held, sums = call(
        functools.partial(stage_b, n),
        sent(1) + [slab, slab, tile],
        [where] + qs + [chaos, mean_inverse, w0, c1, ca0],
        1,
        [double, double],
    )
    vs = trade(vs)
    *xs, dots = call(
        functools.partial(stage_c, n),
        sent(1) + [tile],
        [where, chaos, mean_inverse, w0, v1, held, sums],
        1,
        [shaped((n, rows, width))] * 2,
    )
    dots, xs, ws = lax.optimization_barrier((dots, xs, ws))
    xs = trade(xs)
    dots = lax.all_to_all(dots, ("space", "mode"), split_axis=0, concat_axis=0, tiled=True)
    (field,) = call(
        functools.partial(end_body, n, cells),
        [shaped((nodes, width), F32)],
        [where, guess, dots] + ws + vs + xs,
        1,
    )
    return field


def solution(mesh):
    placed = (
        P("space", "mode"),
        P("space", "mode"),
        P("space", None),
        P("space", None),
        P("space", None),
        P("mode", None, None),
        P(),
        P(),
        P(),
    )
    return jax.shard_map(
        shards, mesh=mesh, in_specs=placed, out_specs=P("space", "mode"), check_vma=False
    )
```

time: 422 us -> 125 us (0.30)
  blocking collectives: 173 us -> 0 us
  waiting for transfers between devices: 92.1 us -> 26.7 us
  matrix products: 53 us -> 0 us
  Pallas kernels: 0 us -> 46.3 us
  local copies, waits for them, and re-layouts: 42.4 us -> 5.84 us
  between operations: 15.6 us -> 0.37 us
  starting transfers between devices: 32.6 us -> 43.3 us
  other arithmetic: 11.9 us -> 2.24 us
    psum x3 -> x0, blocking collectives: 123 us -> none  [shards(): squares = lax.psum(jnp.sum(update * update), ('space', 'mode'))]
    dot_general x10 -> x0, matrix products: 53 us -> none  [the longest x3 38 us: shards(): lax.dot_general(residual_slab, mean_inverse, (((1,), (1,)), ((), ())), pr...]
    all_to_all x3 -> x0, blocking collectives: 50.4 us -> none  [shards(): lax.all_to_all(update_slab, 'mode', split_axis=1, concat_axis=0, tiled=True)]
    pallas_call x0 -> x9, Pallas kernels: none -> 46.3 us  [call(): pl.pallas_call(whole, out_shape=outs, in_specs=[SMEM] * scalars + [HBM] *...]
    all_to_all x6 -> x1, waiting for transfers between devices: 50.4 us -> 7.15 us  [shards(): lax.all_to_all(dots, ('space', 'mode'), split_axis=0, concat_axis=0, tile...]
    all_gather x1 -> x0, waiting for transfers between devices: 37.6 us -> none  [shards(): slab_tables = lax.all_gather(chaos_vals, 'mode', axis=0, tiled=True)]
    ppermute x6 -> x27, starting transfers between devices: 8.81 us -> 39.5 us  [the longest x21 26.8 us: flip_permute(): lax.ppermute(x, axis, [(i, i ^ bit) for i in range(lax.axis_size(axis))])]
    all_to_all x6 -> x1, starting transfers between devices: 23.7 us -> 3.79 us  [shards(): lax.all_to_all(dots, ('space', 'mode'), split_axis=0, concat_axis=0, tile...]
  transfers between devices with their start and end apart: 13 -> 28, of which waited for: 8 -> 5; matrix products, arithmetic and copies ran while one was open for 9% -> 2% of each run, Pallas kernels for 0% -> 33%
where the time goes in v2:
time: 125 us
  Pallas kernels  46.3 us (37%)
  starting transfers between devices  43.3 us (35%)
  waiting for transfers between devices  26.7 us (21%)
  local copies, waits for them, and re-layouts  5.84 us (5%)
  other arithmetic  2.24 us (2%)
    pallas_call x9, Pallas kernels, call(): pl.pallas_call(whole, out_shape=outs, in_specs=[SMEM] * scalars + [HBM] *...  46.3 us
    ppermute x21, starting transfers between devices, flip_permute(): lax.ppermute(x, axis, [(i, i ^ bit) for i in range(lax.axis_size(axis))])  26.8 us
    ppermute x3, waiting for transfers between devices, halo(): above = lax.ppermute(lower, 'space', [(i + 1, i) for i in range(count - 1)])  13.3 us
    ppermute x3, starting transfers between devices, halo(): below = lax.ppermute(upper, 'space', [(i, i + 1) for i in range(count - 1)])  8.86 us
    all_to_all x1, waiting for transfers between devices, shards(): lax.all_to_all(dots, ('space', 'mode'), split_axis=0, concat_axis=0, tile...  7.15 us
    unnamed x40, local copies, waits for them, and re-layouts  5.82 us
    ppermute x21, waiting for transfers between devices, flip_permute(): lax.ppermute(x, axis, [(i, i ^ bit) for i in range(lax.axis_size(axis))])  5.06 us
    ppermute x3, starting transfers between devices, halo(): above = lax.ppermute(lower, 'space', [(i + 1, i) for i in range(count - 1)])  3.86 us
  transfers between devices with their start and end apart: 28, of which 5 were waited for; matrix products, arithmetic and copies ran while one was open for 2% of the time, Pallas kernels for 33%

profile of v2, /device:TPU:0, one launch (start us, length us, event | category | flops | bytes accessed | tf_op | source)
XLA Modules:
  0.0 124.7 jit_solution(5334339957582694953)
XLA Ops:
  0.0 1.5 %fusion.refs_1_.refs_7_.refs_5_ = bf16[256,512]{1,0:T(8,128)(2,1)} fusion(s32[256]{0:T(256)} %bitcast.18), kind=kLoop, calls=%fused_computation.2 | loop fusion | flops 262144 | bytes 263168 | tf_op jit(solution)/shard_map/convert_element_type | solution.py:368
  1.5 3.2 %shard_map.91 = (bf16[512,512]{1,0:T(8,128)(2,1)}, bf16[128,512]{1,0:T(8,128)(2,1)}, bf16[128,512]{1,0:T(8,128)(2,1)}) custom-call(f32[512,512]{1,0:T(8,128)} %refs_1_.8, bf16[256,512]{1,0:T(8,128)(2,1)} %fusion.refs_1_.refs_7_.refs_5_), custom_call_target="tpu_custom_call" | custom-call | flops 1 | bytes 1 | tf_op jit(solution)/shard_map/pallas_call | solution.py:40
  4.7 2.4 %collective-permute-start.3 = (bf16[128,512]{1,0:T(8,128)(2,1)}, bf16[128,512]{1,0:T(8,128)(2,1)S(1)}, u32[]{:S(2)}, u32[]{:S(2)}) collective-permute-start(bf16[128,512]{1,0:T(8,128)(2,1)} %get-tuple-element.69), channel_id=1, source_target_pairs={{0,4},{4,8},{8,12},{12,16},{16,20},{20,24},{24,28},{1,5},{5,9},{9,... | collective-permute-start | bytes 393224 | tf_op jit(solution)/shard_map/ppermute | solution.py:81
  8.4 1.6 %copy.13 = bf16[32,128,128]{1,2,0:T(8,128)(2,1)S(1)} copy(bf16[32,128,128]{2,1,0:T(8,128)(2,1)} %param.14) | data formatting | bytes 2097152 | tf_op args[5]
  10.0 3.3 %collective-permute-start.2 = (bf16[8,128,128]{2,1,0:T(8,128)(2,1)S(1)}, bf16[8,128,128]{2,1,0:T(8,128)(2,1)S(1)}, u32[]{:S(2)}, u32[]{:S(2)}) collective-permute-start(bf16[8,128,128]{2,1,0:T(8,128)(2,1)S(1)} %dynamic-slice_bitcast_fusion), channel_id=1, source_target_pairs={{0,3},{1,2},{2,1},{3,0},{4,7},{5,6},{6,5},{7,4},{8,11},{9,10},{10,... | collective-permute-start | bytes 786440 | tf_op jit(solution)/shard_map/ppermute | solution.py:72
  15.4 5.5 %shard_map.92 = (bf16[512,1024]{1,0:T(8,128)(2,1)}, bf16[128,1024]{1,0:T(8,128)(2,1)}, bf16[128,1024]{1,0:T(8,128)(2,1)}, bf16[4,128,512]{2,1,0:T(8,128)(2,1)}, ...) custom-call(s32[2]{0:T(128)} %pad_add_fusion.refs_0_, ...), custom_call_target="tpu_custom_call" | custom-call | flops 1 | bytes 1 | tf_op jit(solution)/shard_map/pallas_call | solution.py:40
  20.9 4.0 %collective-permute-start.5 = (bf16[128,1024]{1,0:T(8,128)(2,1)}, bf16[128,1024]{1,0:T(8,128)(2,1)S(1)}, u32[]{:S(2)}, u32[]{:S(2)}) collective-permute-start(bf16[128,1024]{1,0:T(8,128)(2,1)} %get-tuple-element.71), channel_id=1, source_target_pairs={{0,4},{4,8},{8,12},{12,16},{16,20},{20,24},{24,28},{1,5},{5,9},{9,... | collective-permute-start | bytes 786440 | tf_op jit(solution)/shard_map/ppermute | solution.py:81
  26.2 4.4 %collective-permute-done.6.refs_4_ = bf16[128,1024]{1,0:T(8,128)(2,1)S(1)} collective-permute-done((bf16[128,1024]{1,0:T(8,128)(2,1)}, bf16[128,1024]{1,0:T(8,128)(2,1)S(1)}, u32[]{:S(2)}, u32[]{:S(2)}) %collective-permute-start.6) | collective-permute-done | bytes 262176 | tf_op jit(solution)/shard_map/ppermute | solution.py:82
  30.7 4.7 %collective-permute-start.7 = (bf16[3,8,128,128]{3,2,1,0:T(8,128)(2,1)S(1)}, bf16[3,8,128,128]{3,2,1,0:T(8,128)(2,1)S(1)}, u32[]{:S(2)}, u32[]{:S(2)}) collective-permute-start(bf16[3,8,128,128]{3,2,1,0:T(8,128)(2,1)S(1)} %pad_maximum_fusion.refs_4_), channel_id=1, source_target_pairs={{0,8},{4,12},{8,0},{12,4},{16,24},{20,28},{24,16},{28,20},{1,9},{5... | collective-permute-start | bytes 2359304 | tf_op jit(solution)/shard_map/ppermute | solution.py:72
  35.3 1.5 %collective-permute-start.8 = (bf16[4,128,512]{2,1,0:T(8,128)(2,1)}, bf16[4,128,512]{2,1,0:T(8,128)(2,1)S(1)}, u32[]{:S(2)}, u32[]{:S(2)}) collective-permute-start(bf16[4,128,512]{2,1,0:T(8,128)(2,1)} %get-tuple-element.82), channel_id=1, source_target_pairs={{0,1},{1,0},{2,3},{3,2},{4,5},{5,4},{6,7},{7,6},{8,9},{9,8},{10,11... | collective-permute-start | bytes 1572872 | tf_op jit(solution)/shard_map/ppermute | solution.py:72
  36.8 1.5 %collective-permute-start.9 = (bf16[4,128,512]{2,1,0:T(8,128)(2,1)}, bf16[4,128,512]{2,1,0:T(8,128)(2,1)S(1)}, u32[]{:S(2)}, u32[]{:S(2)}) collective-permute-start(bf16[4,128,512]{2,1,0:T(8,128)(2,1)} %get-tuple-element.83), channel_id=1, source_target_pairs={{0,2},{1,3},{2,0},{3,1},{4,6},{5,7},{6,4},{7,5},{8,10},{9,11},{10,... | collective-permute-start | bytes 1572872 | tf_op jit(solution)/shard_map/ppermute | solution.py:72
  38.8 5.1 %shard_map.93 = (bf16[512,1024]{1,0:T(8,128)(2,1)}, bf16[512,512]{1,0:T(8,128)(2,1)}, bf16[128,512]{1,0:T(8,128)(2,1)}, bf16[128,512]{1,0:T(8,128)(2,1)}) custom-call(bf16[512,512]{1,0:T(8,128)(2,1)} %refs_1_.7, bf16[512,256]{1,0:T(8,128)(2,1)} %refs_2_.5, bf16[512,1024]{1,0:T(8,128)(2,1)} %get-tuple-element.76.refs_2_, bf16[128,1024]{1,0:T(8,128)(2,1)} %copy-done.12, ...), custom_call_target="tpu_custom_call" | custom-call | flops 1 | bytes 1 | tf_op jit(solution)/shard_map/pallas_call | solution.py:40
  43.9 2.5 %collective-permute-start.11 = (bf16[128,512]{1,0:T(8,128)(2,1)}, bf16[128,512]{1,0:T(8,128)(2,1)S(1)}, u32[]{:S(2)}, u32[]{:S(2)}) collective-permute-start(bf16[128,512]{1,0:T(8,128)(2,1)} %get-tuple-element.85), channel_id=1, source_target_pairs={{0,4},{4,8},{8,12},{12,16},{16,20},{20,24},{24,28},{1,5},{5,9},{9,... | collective-permute-start | bytes 393224 | tf_op jit(solution)/shard_map/ppermute | solution.py:81
  48.9 8.9 %collective-permute-done.12.refs_6_ = bf16[128,512]{1,0:T(8,128)(2,1)S(1)} collective-permute-done((bf16[128,512]{1,0:T(8,128)(2,1)}, bf16[128,512]{1,0:T(8,128)(2,1)S(1)}, u32[]{:S(2)}, u32[]{:S(2)}) %collective-permute-start.12) | collective-permute-done | bytes 131104 | tf_op jit(solution)/shard_map/ppermute | solution.py:82
  57.8 5.0 %collective-permute-done.9.refs_3_ = bf16[4,128,512]{2,1,0:T(8,128)(2,1)S(1)} collective-permute-done((bf16[4,128,512]{2,1,0:T(8,128)(2,1)}, bf16[4,128,512]{2,1,0:T(8,128)(2,1)S(1)}, u32[]{:S(2)}, u32[]{:S(2)}) %collective-permute-start.9) | collective-permute-done | bytes 524320 | tf_op jit(solution)/shard_map/ppermute | solution.py:72
  62.9 4.8 %shard_map.94 = (bf16[3,128,512]{2,1,0:T(8,128)(2,1)}, bf16[3,128,512]{2,1,0:T(8,128)(2,1)}, bf16[3,128,512]{2,1,0:T(8,128)(2,1)}, bf16[3,128,512]{2,1,0:T(8,128)(2,1)}) custom-call(s32[2]{0:T(128)} %pad_add_fusion.refs_0_, bf16[512,512]{1,0:T(8,128)(2,1)} %refs_1_.7, bf16[512,256]{1,0:T(8,128)(2,1)} %refs_2_.5, ...), custom_call_target="tpu_custom_call" | custom-call | flops 1 | bytes 1 | tf_op jit(solution)/shard_map/pallas_call | solution.py:40
  69.0 1.4 %collective-permute-start.16 = (bf16[3,128,512]{2,1,0:T(8,128)(2,1)}, bf16[3,128,512]{2,1,0:T(8,128)(2,1)}, u32[]{:S(2)}, u32[]{:S(2)}) collective-permute-start(bf16[3,128,512]{2,1,0:T(8,128)(2,1)} %get-tuple-element.102), channel_id=1, source_target_pairs={{0,2},{1,3},{2,0},{3,1},{4,6},{5,7},{6,4},{7,5},{8,10},{9,11},{10,... | collective-permute-start | bytes 1179656 | tf_op jit(solution)/shard_map/ppermute | solution.py:72
  70.3 1.4 %collective-permute-start.17 = (bf16[3,128,512]{2,1,0:T(8,128)(2,1)}, bf16[3,128,512]{2,1,0:T(8,128)(2,1)}, u32[]{:S(2)}, u32[]{:S(2)}) collective-permute-start(bf16[3,128,512]{2,1,0:T(8,128)(2,1)} %get-tuple-element.103), channel_id=1, source_target_pairs={{0,3},{1,2},{2,1},{3,0},{4,7},{5,6},{6,5},{7,4},{8,11},{9,10},{10,... | collective-permute-start | bytes 1179656 | tf_op jit(solution)/shard_map/ppermute | solution.py:72
  71.9 5.2 %shard_map.95.refs_5_.refs_1_ = bf16[2048,2048]{1,0:T(8,128)(2,1)S(1)} custom-call(s32[2]{0:T(128)S(1)} %copy-done.10, s32[16,8]{1,0:T(8,128)S(1)} %copy.15.refs_1_, s32[16]{0:T(128)S(1)} %copy-done.11, bf16[32,128,128]{2,1,0:T(8,128)(2,1)S(1)} %bitcast.13, bf16[3,8,128,128]{3,2,1,0:T(8,128)(2,1)S(1)} %pad_maximum_fusion.refs_4_, ...), custom_call_target="tpu_custom_call" | custom-call | flops 1 | bytes 1 | tf_op jit(solution)/shard_map/pallas_call | solution.py:40
  77.1 3.4 %copy-done = bf16[2048,2048]{1,0:T(8,128)(2,1)S(1)} copy-done((bf16[2048,2048]{1,0:T(8,128)(2,1)S(1)}, bf16[2048,2048]{1,0:T(8,128)(2,1)}, u32[]{:S(2)}) %copy-start) | copy-done | bytes 8388632
  80.5 6.3 %shard_map.96 = (f32[4,128,512]{2,1,0:T(8,128)S(1)}, f32[4,128,512]{2,1,0:T(8,128)S(1)}, f32[4,128,512]{2,1,0:T(8,128)S(1)}, bf16[2,128,512]{2,1,0:T(8,128)(2,1)...) custom-call(s32[2]{0:T(128)S(1)} %copy-done.10, ...), custom_call_target="tpu_custom_call" | custom-call | flops 1 | bytes 1 | tf_op jit(solution)/shard_map/pallas_call | solution.py:40
  87.5 1.4 %collective-permute-start.19 = (bf16[2,128,512]{2,1,0:T(8,128)(2,1)S(1)}, bf16[2,128,512]{2,1,0:T(8,128)(2,1)S(1)}, u32[]{:S(2)}, u32[]{:S(2)}) collective-permute-start(bf16[2,128,512]{2,1,0:T(8,128)(2,1)S(1)} %get-tuple-element.116), channel_id=1, source_target_pairs={{0,2},{1,3},{2,0},{3,1},{4,6},{5,7},{6,4},{7,5},{8,10},{9,11},{10,... | collective-permute-start | bytes 786440 | tf_op jit(solution)/shard_map/ppermute | solution.py:72
  88.9 1.4 %collective-permute-start.20 = (bf16[2,128,512]{2,1,0:T(8,128)(2,1)S(1)}, bf16[2,128,512]{2,1,0:T(8,128)(2,1)S(1)}, u32[]{:S(2)}, u32[]{:S(2)}) collective-permute-start(bf16[2,128,512]{2,1,0:T(8,128)(2,1)S(1)} %get-tuple-element.117), channel_id=1, source_target_pairs={{0,3},{1,2},{2,1},{3,0},{4,7},{5,6},{6,5},{7,4},{8,11},{9,10},{10,... | collective-permute-start | bytes 786440 | tf_op jit(solution)/shard_map/ppermute | solution.py:72
  90.4 8.4 %shard_map.97 = (bf16[1,128,512]{2,1,0:T(8,128)(2,1)S(1)}, bf16[1,128,512]{2,1,0:T(8,128)(2,1)S(1)}, bf16[1,128,512]{2,1,0:T(8,128)(2,1)S(1)}, bf16[1,128,512]{2...) custom-call(s32[2]{0:T(128)S(1)} %copy-done.10, ...), custom_call_target="tpu_custom_call" | custom-call | flops 1 | bytes 1 | tf_op jit(solution)/shard_map/pallas_call | solution.py:40
  99.6 1.4 %collective-permute-start.22 = (bf16[1,128,512]{2,1,0:T(8,128)(2,1)S(1)}, bf16[1,128,512]{2,1,0:T(8,128)(2,1)S(1)}, u32[]{:S(2)}, u32[]{:S(2)}) collective-permute-start(bf16[1,128,512]{2,1,0:T(8,128)(2,1)S(1)} %get-tuple-element.125), channel_id=1, source_target_pairs={{0,2},{1,3},{2,0},{3,1},{4,6},{5,7},{6,4},{7,5},{8,10},{9,11},{10,... | collective-permute-start | bytes 393224 | tf_op jit(solution)/shard_map/ppermute | solution.py:72
  100.9 5.6 %shard_map.98 = (bf16[1,128,512]{2,1,0:T(8,128)(2,1)S(1)}, bf16[1,128,512]{2,1,0:T(8,128)(2,1)}, bf16[1,128,512]{2,1,0:T(8,128)(2,1)}, bf16[1,128,512]{2,1,0:T(8,128)(2,1)}, f32[32,128]{1,0:T(8,128)}) custom-call(s32[2]{0:T(128)S(1)} %copy-done.10, bf16[2048,2048]{1,0:T(8,128)(2,1)S(1)} %shard_map.95.refs_5_.refs_1_, bf16[2048,2048]{1,0:T(8,128)(2,1)S(1)} %copy-done, ...), custom_call_target="tpu_custom_call" | custom-call | flops 1 | bytes 1 | tf_op jit(solution)/shard_map/pallas_call | solution.py:40
  106.6 1.4 %collective-permute-start.23 = (bf16[1,128,512]{2,1,0:T(8,128)(2,1)S(1)}, bf16[1,128,512]{2,1,0:T(8,128)(2,1)S(1)}, u32[]{:S(2)}, u32[]{:S(2)}) collective-permute-start(bf16[1,128,512]{2,1,0:T(8,128)(2,1)S(1)} %get-tuple-element.126), channel_id=1, source_target_pairs={{0,3},{1,2},{2,1},{3,0},{4,7},{5,6},{6,5},{7,4},{8,11},{9,10},{10,... | collective-permute-start | bytes 393224 | tf_op jit(solution)/shard_map/ppermute | solution.py:72
  108.7 1.4 %collective-permute-start.25 = (bf16[1,128,512]{2,1,0:T(8,128)(2,1)}, bf16[1,128,512]{2,1,0:T(8,128)(2,1)S(1)}, u32[]{:S(2)}, u32[]{:S(2)}) collective-permute-start(bf16[1,128,512]{2,1,0:T(8,128)(2,1)} %get-tuple-element.129), channel_id=1, source_target_pairs={{0,2},{1,3},{2,0},{3,1},{4,6},{5,7},{6,4},{7,5},{8,10},{9,11},{10,... | collective-permute-start | bytes 393224 | tf_op jit(solution)/shard_map/ppermute | solution.py:72
  110.1 1.4 %collective-permute-start.26 = (bf16[1,128,512]{2,1,0:T(8,128)(2,1)}, bf16[1,128,512]{2,1,0:T(8,128)(2,1)S(1)}, u32[]{:S(2)}, u32[]{:S(2)}) collective-permute-start(bf16[1,128,512]{2,1,0:T(8,128)(2,1)} %get-tuple-element.130), channel_id=1, source_target_pairs={{0,3},{1,2},{2,1},{3,0},{4,7},{5,6},{6,5},{7,4},{8,11},{9,10},{10,... | collective-permute-start | bytes 393224 | tf_op jit(solution)/shard_map/ppermute | solution.py:72
  111.5 3.8 %all-to-all-start = ((f32[32,1,128]{2,1,0:T(1,128)}), f32[32,1,128]{2,1,0:T(1,128)S(1)}, u32[]{:S(2)}, u32[]{:S(2)}) async-start(f32[32,1,128]{2,1,0:T(1,128)} %bitcast.9), calls=%async_computation | async-start | bytes 32768 | tf_op jit(solution)/shard_map/all_to_all | solution.py:453
  115.3 7.2 %all-to-all-done = f32[32,1,128]{2,1,0:T(1,128)S(1)} async-done(((f32[32,1,128]{2,1,0:T(1,128)}), f32[32,1,128]{2,1,0:T(1,128)S(1)}, u32[]{:S(2)}, u32[]{:S(2)}) %all-to-all-start) | async-done | bytes 16416 | tf_op jit(solution)/shard_map/all_to_all | solution.py:453
  122.5 2.2 %shard_map.99 = f32[512,512]{1,0:T(8,128)} custom-call(s32[2]{0:T(128)S(1)} %copy-done.10, f32[512,512]{1,0:T(8,128)S(1)} %copy-done.1, f32[32,128]{1,0:T(8,128)S(1)} %bitcast.14, bf16[2,128,512]{2,1,0:T(8,128)(2,1)S(1)} %get-tuple-element.119.refs_3_, bf16[2,128,512]{2,1,0:T(8,128)(2,1)S(1)} %collective-permute-done.18.refs_4_, ...), custom_call_target="tpu_custom_call" | custom-call | flops 1 | bytes 1 | tf_op jit(solution)/shard_map/pallas_call | solution.py:40
  (77 shorter events, 11.3 us)
Async XLA Ops:
  0.0 71.8 %copy-start.18 = (s32[16,8]{0,1:T(8,128)S(1)}, s32[16,8]{0,1:T(8,128)}, u32[]{:S(2)}) copy-start(s32[16,8]{0,1:T(8,128)} %param.15) | copy-start | bytes 1540
  0.0 71.9 %copy-start.11 = (s32[16]{0:T(128)S(1)}, s32[16]{0:T(128)}, u32[]{:S(2)}) copy-start(s32[16]{0:T(128)} %refs_2_.6) | copy-start | bytes 196
  4.7 10.0 %collective-permute-start.3 = (bf16[128,512]{1,0:T(8,128)(2,1)}, bf16[128,512]{1,0:T(8,128)(2,1)S(1)}, u32[]{:S(2)}, u32[]{:S(2)}) collective-permute-start(bf16[128,512]{1,0:T(8,128)(2,1)} %get-tuple-element.69), channel_id=1, source_target_pairs={{0,4},{4,8},{8,12},{12,16},{16,20},{20,24},{24,28},{1,5},{5,9},{9,... | collective-permute-start | bytes 393224 | tf_op jit(solution)/shard_map/ppermute | solution.py:81
  7.1 7.6 %collective-permute-start.4 = (bf16[128,512]{1,0:T(8,128)(2,1)}, bf16[128,512]{1,0:T(8,128)(2,1)S(1)}, u32[]{:S(2)}, u32[]{:S(2)}) collective-permute-start(bf16[128,512]{1,0:T(8,128)(2,1)} %get-tuple-element.70), channel_id=1, source_target_pairs={{4,0},{8,4},{12,8},{16,12},{20,16},{24,20},{28,24},{5,1},{9,5},{13... | collective-permute-start | bytes 393224 | tf_op jit(solution)/shard_map/ppermute | solution.py:82
  10.0 16.1 %collective-permute-start.2 = (bf16[8,128,128]{2,1,0:T(8,128)(2,1)S(1)}, bf16[8,128,128]{2,1,0:T(8,128)(2,1)S(1)}, u32[]{:S(2)}, u32[]{:S(2)}) collective-permute-start(bf16[8,128,128]{2,1,0:T(8,128)(2,1)S(1)} %dynamic-slice_bitcast_fusion), channel_id=1, source_target_pairs={{0,3},{1,2},{2,1},{3,0},{4,7},{5,6},{6,5},{7,4},{8,11},{9,10},{10,... | collective-permute-start | bytes 786440 | tf_op jit(solution)/shard_map/ppermute | solution.py:72
  13.4 12.8 %collective-permute-start.1 = (bf16[8,128,128]{2,1,0:T(8,128)(2,1)S(1)}, bf16[8,128,128]{2,1,0:T(8,128)(2,1)S(1)}, u32[]{:S(2)}, u32[]{:S(2)}) collective-permute-start(bf16[8,128,128]{2,1,0:T(8,128)(2,1)S(1)} %dynamic-slice_bitcast_fusion), channel_id=1, source_target_pairs={{0,2},{1,3},{2,0},{3,1},{4,6},{5,7},{6,4},{7,5},{8,10},{9,11},{10,... | collective-permute-start | bytes 786440 | tf_op jit(solution)/shard_map/ppermute | solution.py:72
  13.9 12.3 %collective-permute-start = (bf16[8,128,128]{2,1,0:T(8,128)(2,1)S(1)}, bf16[8,128,128]{2,1,0:T(8,128)(2,1)S(1)}, u32[]{:S(2)}, u32[]{:S(2)}) collective-permute-start(bf16[8,128,128]{2,1,0:T(8,128)(2,1)S(1)} %dynamic-slice_bitcast_fusion), channel_id=1, source_target_pairs={{0,1},{1,0},{2,3},{3,2},{4,5},{5,4},{6,7},{7,6},{8,9},{9,8},{10,11... | collective-permute-start | bytes 786440 | tf_op jit(solution)/shard_map/ppermute | solution.py:72
  14.7 57.2 %copy-start.10 = (s32[2]{0:T(128)S(1)}, s32[2]{0:T(128)}, u32[]{:S(2)}) copy-start(s32[2]{0:T(128)} %pad_add_fusion.refs_0_) | copy-start | bytes 28
  20.9 5.3 %collective-permute-start.5 = (bf16[128,1024]{1,0:T(8,128)(2,1)}, bf16[128,1024]{1,0:T(8,128)(2,1)S(1)}, u32[]{:S(2)}, u32[]{:S(2)}) collective-permute-start(bf16[128,1024]{1,0:T(8,128)(2,1)} %get-tuple-element.71), channel_id=1, source_target_pairs={{0,4},{4,8},{8,12},{12,16},{16,20},{20,24},{24,28},{1,5},{5,9},{9,... | collective-permute-start | bytes 786440 | tf_op jit(solution)/shard_map/ppermute | solution.py:81
  24.9 5.7 %collective-permute-start.6 = (bf16[128,1024]{1,0:T(8,128)(2,1)}, bf16[128,1024]{1,0:T(8,128)(2,1)S(1)}, u32[]{:S(2)}, u32[]{:S(2)}) collective-permute-start(bf16[128,1024]{1,0:T(8,128)(2,1)} %get-tuple-element.72), channel_id=1, source_target_pairs={{4,0},{8,4},{12,8},{16,12},{20,16},{24,20},{28,24},{5,1},{9,5},{13... | collective-permute-start | bytes 786440 | tf_op jit(solution)/shard_map/ppermute | solution.py:82
  30.7 37.0 %collective-permute-start.7 = (bf16[3,8,128,128]{3,2,1,0:T(8,128)(2,1)S(1)}, bf16[3,8,128,128]{3,2,1,0:T(8,128)(2,1)S(1)}, u32[]{:S(2)}, u32[]{:S(2)}) collective-permute-start(bf16[3,8,128,128]{3,2,1,0:T(8,128)(2,1)S(1)} %pad_maximum_fusion.refs_4_), channel_id=1, source_target_pairs={{0,8},{4,12},{8,0},{12,4},{16,24},{20,28},{24,16},{28,20},{1,9},{5... | collective-permute-start | bytes 2359304 | tf_op jit(solution)/shard_map/ppermute | solution.py:72
  35.3 22.5 %collective-permute-start.8 = (bf16[4,128,512]{2,1,0:T(8,128)(2,1)}, bf16[4,128,512]{2,1,0:T(8,128)(2,1)S(1)}, u32[]{:S(2)}, u32[]{:S(2)}) collective-permute-start(bf16[4,128,512]{2,1,0:T(8,128)(2,1)} %get-tuple-element.82), channel_id=1, source_target_pairs={{0,1},{1,0},{2,3},{3,2},{4,5},{5,4},{6,7},{7,6},{8,9},{9,8},{10,11... | collective-permute-start | bytes 1572872 | tf_op jit(solution)/shard_map/ppermute | solution.py:72
  36.8 26.0 %collective-permute-start.9 = (bf16[4,128,512]{2,1,0:T(8,128)(2,1)}, bf16[4,128,512]{2,1,0:T(8,128)(2,1)S(1)}, u32[]{:S(2)}, u32[]{:S(2)}) collective-permute-start(bf16[4,128,512]{2,1,0:T(8,128)(2,1)} %get-tuple-element.83), channel_id=1, source_target_pairs={{0,2},{1,3},{2,0},{3,1},{4,6},{5,7},{6,4},{7,5},{8,10},{9,11},{10,... | collective-permute-start | bytes 1572872 | tf_op jit(solution)/shard_map/ppermute | solution.py:72
  38.3 24.5 %collective-permute-start.10 = (bf16[4,128,512]{2,1,0:T(8,128)(2,1)}, bf16[4,128,512]{2,1,0:T(8,128)(2,1)S(1)}, u32[]{:S(2)}, u32[]{:S(2)}) collective-permute-start(bf16[4,128,512]{2,1,0:T(8,128)(2,1)} %get-tuple-element.84), channel_id=1, source_target_pairs={{0,3},{1,2},{2,1},{3,0},{4,7},{5,6},{6,5},{7,4},{8,11},{9,10},{10,... | collective-permute-start | bytes 1572872 | tf_op jit(solution)/shard_map/ppermute | solution.py:72
  43.9 3.7 %collective-permute-start.11 = (bf16[128,512]{1,0:T(8,128)(2,1)}, bf16[128,512]{1,0:T(8,128)(2,1)S(1)}, u32[]{:S(2)}, u32[]{:S(2)}) collective-permute-start(bf16[128,512]{1,0:T(8,128)(2,1)} %get-tuple-element.85), channel_id=1, source_target_pairs={{0,4},{4,8},{8,12},{12,16},{16,20},{20,24},{24,28},{1,5},{5,9},{9,... | collective-permute-start | bytes 393224 | tf_op jit(solution)/shard_map/ppermute | solution.py:81
  47.6 10.2 %collective-permute-start.12 = (bf16[128,512]{1,0:T(8,128)(2,1)}, bf16[128,512]{1,0:T(8,128)(2,1)S(1)}, u32[]{:S(2)}, u32[]{:S(2)}) collective-permute-start(bf16[128,512]{1,0:T(8,128)(2,1)} %get-tuple-element.86), channel_id=1, source_target_pairs={{4,0},{8,4},{12,8},{16,12},{20,16},{24,20},{28,24},{5,1},{9,5},{13... | collective-permute-start | bytes 393224 | tf_op jit(solution)/shard_map/ppermute | solution.py:82
  67.7 4.2 %collective-permute-start.13 = (bf16[3,8,128,128]{3,2,1,0:T(8,128)(2,1)S(1)}, bf16[3,8,128,128]{3,2,1,0:T(8,128)(2,1)S(1)}, u32[]{:S(2)}, u32[]{:S(2)}) collective-permute-start(bf16[3,8,128,128]{3,2,1,0:T(8,128)(2,1)S(1)} %pad_maximum_fusion.refs_4_), channel_id=1, source_target_pairs={{0,4},{4,0},{8,12},{12,8},{16,20},{20,16},{24,28},{28,24},{1,5},{5... | collective-permute-start | bytes 2359304 | tf_op jit(solution)/shard_map/ppermute | solution.py:72
  67.9 4.0 %collective-permute-start.14 = (bf16[3,8,128,128]{3,2,1,0:T(8,128)(2,1)S(1)}, bf16[3,8,128,128]{3,2,1,0:T(8,128)(2,1)}, u32[]{:S(2)}, u32[]{:S(2)}) collective-permute-start(bf16[3,8,128,128]{3,2,1,0:T(8,128)(2,1)S(1)} %collective-permute-done.7.refs_6_), channel_id=1, source_target_pairs={{0,4},{4,0},{8,12},{12,8},{16,20},{20,16},{24,28},{28,24},{1,5},{5... | collective-permute-start | bytes 2359304 | tf_op jit(solution)/shard_map/ppermute | solution.py:72
  68.3 20.7 %collective-permute-start.15 = (bf16[3,128,512]{2,1,0:T(8,128)(2,1)}, bf16[3,128,512]{2,1,0:T(8,128)(2,1)}, u32[]{:S(2)}, u32[]{:S(2)}) collective-permute-start(bf16[3,128,512]{2,1,0:T(8,128)(2,1)} %get-tuple-element.101), channel_id=1, source_target_pairs={{0,1},{1,0},{2,3},{3,2},{4,5},{5,4},{6,7},{7,6},{8,9},{9,8},{10,11... | collective-permute-start | bytes 1179656 | tf_op jit(solution)/shard_map/ppermute | solution.py:72
  69.0 21.4 %collective-permute-start.16 = (bf16[3,128,512]{2,1,0:T(8,128)(2,1)}, bf16[3,128,512]{2,1,0:T(8,128)(2,1)}, u32[]{:S(2)}, u32[]{:S(2)}) collective-permute-start(bf16[3,128,512]{2,1,0:T(8,128)(2,1)} %get-tuple-element.102), channel_id=1, source_target_pairs={{0,2},{1,3},{2,0},{3,1},{4,6},{5,7},{6,4},{7,5},{8,10},{9,11},{10,... | collective-permute-start | bytes 1179656 | tf_op jit(solution)/shard_map/ppermute | solution.py:72
  70.3 20.0 %collective-permute-start.17 = (bf16[3,128,512]{2,1,0:T(8,128)(2,1)}, bf16[3,128,512]{2,1,0:T(8,128)(2,1)}, u32[]{:S(2)}, u32[]{:S(2)}) collective-permute-start(bf16[3,128,512]{2,1,0:T(8,128)(2,1)} %get-tuple-element.103), channel_id=1, source_target_pairs={{0,3},{1,2},{2,1},{3,0},{4,7},{5,6},{6,5},{7,4},{8,11},{9,10},{10,... | collective-permute-start | bytes 1179656 | tf_op jit(solution)/shard_map/ppermute | solution.py:72
  86.8 19.8 %collective-permute-start.18 = (bf16[2,128,512]{2,1,0:T(8,128)(2,1)S(1)}, bf16[2,128,512]{2,1,0:T(8,128)(2,1)S(1)}, u32[]{:S(2)}, u32[]{:S(2)}) collective-permute-start(bf16[2,128,512]{2,1,0:T(8,128)(2,1)S(1)} %get-tuple-element.115), channel_id=1, source_target_pairs={{0,1},{1,0},{2,3},{3,2},{4,5},{5,4},{6,7},{7,6},{8,9},{9,8},{10,11... | collective-permute-start | bytes 786440 | tf_op jit(solution)/shard_map/ppermute | solution.py:72
  87.5 20.5 %collective-permute-start.19 = (bf16[2,128,512]{2,1,0:T(8,128)(2,1)S(1)}, bf16[2,128,512]{2,1,0:T(8,128)(2,1)S(1)}, u32[]{:S(2)}, u32[]{:S(2)}) collective-permute-start(bf16[2,128,512]{2,1,0:T(8,128)(2,1)S(1)} %get-tuple-element.116), channel_id=1, source_target_pairs={{0,2},{1,3},{2,0},{3,1},{4,6},{5,7},{6,4},{7,5},{8,10},{9,11},{10,... | collective-permute-start | bytes 786440 | tf_op jit(solution)/shard_map/ppermute | solution.py:72
  88.9 19.1 %collective-permute-start.20 = (bf16[2,128,512]{2,1,0:T(8,128)(2,1)S(1)}, bf16[2,128,512]{2,1,0:T(8,128)(2,1)S(1)}, u32[]{:S(2)}, u32[]{:S(2)}) collective-permute-start(bf16[2,128,512]{2,1,0:T(8,128)(2,1)S(1)} %get-tuple-element.117), channel_id=1, source_target_pairs={{0,3},{1,2},{2,1},{3,0},{4,7},{5,6},{6,5},{7,4},{8,11},{9,10},{10,... | collective-permute-start | bytes 786440 | tf_op jit(solution)/shard_map/ppermute | solution.py:72
  98.8 11.3 %collective-permute-start.21 = (bf16[1,128,512]{2,1,0:T(8,128)(2,1)S(1)}, bf16[1,128,512]{2,1,0:T(8,128)(2,1)S(1)}, u32[]{:S(2)}, u32[]{:S(2)}) collective-permute-start(bf16[1,128,512]{2,1,0:T(8,128)(2,1)S(1)} %get-tuple-element.124), channel_id=1, source_target_pairs={{0,1},{1,0},{2,3},{3,2},{4,5},{5,4},{6,7},{7,6},{8,9},{9,8},{10,11... | collective-permute-start | bytes 393224 | tf_op jit(solution)/shard_map/ppermute | solution.py:72
  99.6 15.8 %collective-permute-start.22 = (bf16[1,128,512]{2,1,0:T(8,128)(2,1)S(1)}, bf16[1,128,512]{2,1,0:T(8,128)(2,1)S(1)}, u32[]{:S(2)}, u32[]{:S(2)}) collective-permute-start(bf16[1,128,512]{2,1,0:T(8,128)(2,1)S(1)} %get-tuple-element.125), channel_id=1, source_target_pairs={{0,2},{1,3},{2,0},{3,1},{4,6},{5,7},{6,4},{7,5},{8,10},{9,11},{10,... | collective-permute-start | bytes 393224 | tf_op jit(solution)/shard_map/ppermute | solution.py:72
  100.9 21.6 %copy-start.1 = (f32[512,512]{1,0:T(8,128)S(1)}, f32[512,512]{1,0:T(8,128)}, u32[]{:S(2)}) copy-start(f32[512,512]{1,0:T(8,128)} %refs_1_.8) | copy-start | bytes 3145732
  106.6 8.7 %collective-permute-start.23 = (bf16[1,128,512]{2,1,0:T(8,128)(2,1)S(1)}, bf16[1,128,512]{2,1,0:T(8,128)(2,1)S(1)}, u32[]{:S(2)}, u32[]{:S(2)}) collective-permute-start(bf16[1,128,512]{2,1,0:T(8,128)(2,1)S(1)} %get-tuple-element.126), channel_id=1, source_target_pairs={{0,3},{1,2},{2,1},{3,0},{4,7},{5,6},{6,5},{7,4},{8,11},{9,10},{10,... | collective-permute-start | bytes 393224 | tf_op jit(solution)/shard_map/ppermute | solution.py:72
  108.0 14.5 %collective-permute-start.24 = (bf16[1,128,512]{2,1,0:T(8,128)(2,1)}, bf16[1,128,512]{2,1,0:T(8,128)(2,1)S(1)}, u32[]{:S(2)}, u32[]{:S(2)}) collective-permute-start(bf16[1,128,512]{2,1,0:T(8,128)(2,1)} %get-tuple-element.128), channel_id=1, source_target_pairs={{0,1},{1,0},{2,3},{3,2},{4,5},{5,4},{6,7},{7,6},{8,9},{9,8},{10,11... | collective-permute-start | bytes 393224 | tf_op jit(solution)/shard_map/ppermute | solution.py:72
  108.7 13.8 %collective-permute-start.25 = (bf16[1,128,512]{2,1,0:T(8,128)(2,1)}, bf16[1,128,512]{2,1,0:T(8,128)(2,1)S(1)}, u32[]{:S(2)}, u32[]{:S(2)}) collective-permute-start(bf16[1,128,512]{2,1,0:T(8,128)(2,1)} %get-tuple-element.129), channel_id=1, source_target_pairs={{0,2},{1,3},{2,0},{3,1},{4,6},{5,7},{6,4},{7,5},{8,10},{9,11},{10,... | collective-permute-start | bytes 393224 | tf_op jit(solution)/shard_map/ppermute | solution.py:72
  110.1 12.4 %collective-permute-start.26 = (bf16[1,128,512]{2,1,0:T(8,128)(2,1)}, bf16[1,128,512]{2,1,0:T(8,128)(2,1)S(1)}, u32[]{:S(2)}, u32[]{:S(2)}) collective-permute-start(bf16[1,128,512]{2,1,0:T(8,128)(2,1)} %get-tuple-element.130), channel_id=1, source_target_pairs={{0,3},{1,2},{2,1},{3,0},{4,7},{5,6},{6,5},{7,4},{8,11},{9,10},{10,... | collective-permute-start | bytes 393224 | tf_op jit(solution)/shard_map/ppermute | solution.py:72
  111.5 11.0 %all-to-all-start = ((f32[32,1,128]{2,1,0:T(1,128)}), f32[32,1,128]{2,1,0:T(1,128)S(1)}, u32[]{:S(2)}, u32[]{:S(2)}) async-start(f32[32,1,128]{2,1,0:T(1,128)} %bitcast.9), calls=%async_computation | async-start | bytes 32768 | tf_op jit(solution)/shard_map/all_to_all | solution.py:453
  (15 other events, 97.0 us)

commit v3 on v2

--- a/solution.py
+++ b/solution.py
@@ -13,40 +13,15 @@
 BF16 = jnp.bfloat16
 VMEM = pl.BlockSpec(memory_space=pltpu.VMEM)
 SMEM = pl.BlockSpec(memory_space=pltpu.SMEM)
-HBM = pl.BlockSpec(memory_space=pltpu.HBM)
-
-
-def call(body, outs, args, scalars=0, scratch=(), far=0, limit=16):
-    far_at = slice(scalars, scalars + far)
-
-    def whole(*refs):
-        refs = list(refs)
-        if far:
-            sems = refs.pop()
-            near = refs[len(refs) - far :]
-            del refs[len(refs) - far :]
-            copies = [
-                pltpu.make_async_copy(a, b, sems.at[i])
-                for i, (a, b) in enumerate(zip(refs[far_at], near))
-            ]
-            for copy in copies:
-                copy.start()
-            for copy in copies:
-                copy.wait()
-            refs[far_at] = near
-        body(*refs)
-
-    brought = [pltpu.VMEM(leaf.shape, leaf.dtype) for leaf in args[far_at]]
+
+
+def call(body, outs, args, scalars=0, scratch=(), limit=16):
     return pl.pallas_call(
-        whole,
+        body,
         out_shape=outs,
-        in_specs=[SMEM] * scalars
-        + [HBM] * far
-        + [VMEM] * (len(args) - scalars - far),
+        in_specs=[SMEM] * scalars + [VMEM] * (len(args) - scalars),
         out_specs=[VMEM] * len(outs),
-        scratch_shapes=[pltpu.VMEM(leaf.shape, leaf.dtype) for leaf in scratch]
-        + brought
-        + ([pltpu.SemaphoreType.DMA((far,))] if far else []),
+        scratch_shapes=[pltpu.VMEM(leaf.shape, leaf.dtype) for leaf in scratch],
         compiler_params=pltpu.CompilerParams(vmem_limit_bytes=limit << 20),
         cost_estimate=pl.CostEstimate(flops=1, bytes_accessed=1, transcendentals=0),
     )(*args)
@@ -74,6 +49,10 @@
 
 def trade(pieces):
     return [pieces[0]] + [flip_permute(p, "mode", k) for k, p in enumerate(pieces) if k > 0]
+
+
+def swap(x):
+    return lax.all_to_all(x, "mode", split_axis=0, concat_axis=0, tiled=True)
 
 
 def halo(lower, upper):
@@ -102,23 +81,22 @@
     return y + mm(ghostly[:, ghost:], above[...])
 
 
-def first_body(n, where, diag, ghostly, f_ref, x, below, above, pick, *outs):
-    both, lower, upper = outs[:3]
-    low = outs[-1]
+def first_body(n, diag, ghostly, f_ref, x, below, above, pick, both, lower, upper, sent):
     nodes, width = x.shape
+    rows = nodes // n
     s = spatial_of(diag, ghostly, x, below, above)
     p = f_ref[...] - s
     high = p.astype(BF16)
+    low = (p - high.astype(F32)).astype(BF16)
     both[:, :width] = s.astype(BF16)
     both[:, width:] = high
-    low[...] = (p - high.astype(F32)).astype(BF16)
     picked_rows(pick, both[...], lower, upper)
     for k in range(n):
-        at = rows_of(where[0] ^ k, nodes // n)
-        outs[3 + k][0] = x[at, :]
-        outs[3 + k][1] = both[at, width:]
-        outs[3 + k][2] = low[at, :]
-        outs[3 + k][3] = both[at, :width]
+        at = slice(k * rows, (k + 1) * rows)
+        sent[k, 0] = x[at, :]
+        sent[k, 1] = high[at]
+        sent[k, 2] = low[at]
+        sent[k, 3] = both[at, :width]
 
 
 def second_body(diag, ghostly, x, below, above, pick, both, p1, lower, upper):
@@ -139,10 +117,8 @@
         outs[k][2] = whole[at, :]
 
 
-def table_body(n, slots, where, targets, counts, own, *refs):
-    *refs, out = refs
-    width = own.shape[-1]
-    entries = own.shape[0]
+def table_body(n, slots, where, targets, counts, own, here, beside, there, across, out):
+    entries, width = own.shape[:2]
     per = entries // slots
     quarter = entries // 4
     step = 256
@@ -165,16 +141,17 @@
 
             return carry
 
-        lax.fori_loop(0, count, place, 0)
+        lax.fori_loop(0, count, place, 0, unroll=True)
 
     fill(where[0], 0, entries, lambda i: own[i])
-    for which in range(4):
-        for k in range(1, n):
+    for at in range(n - 1):
+        owner = lax.rem(where[0] + 1 + at, n)
+        for which, ref in enumerate((here, beside, there, across)):
             fill(
-                where[0] ^ k,
+                owner,
                 (where[1] ^ which) * quarter,
                 quarter,
-                lambda i, which=which, k=k: refs[which][k - 1, i],
+                lambda i, ref=ref, at=at: ref[at, i],
             )
 
 
@@ -198,22 +175,20 @@
         emit(g, total)
 
 
-def stage_a(n, where, *refs):
-    ps = refs[:n]
-    chaos, inverse, w0, c1, ca0 = refs[n : n + 5]
-    outs = refs[n + 5 : 2 * n + 5]
-    pair, quick = refs[2 * n + 5 :]
+def stage_a(n, where, ps, chaos, inverse, w0, c1, ca0, *refs):
+    outs = refs[:n]
+    pair, quick = refs[n:]
     me = where[0]
     rows = w0.shape[1]
 
     def residual(g, value):
-        r = ps[g][1].astype(F32) + ps[g][2].astype(F32) - value[:rows]
+        r = ps[me ^ g, 1].astype(F32) + ps[me ^ g, 2].astype(F32) - value[:rows]
         high = r.astype(BF16)
         pair[g, :rows] = high
         pair[g, rows:] = (r - high.astype(F32)).astype(BF16)
         c1[g] = value[rows:]
 
-    by_table(n, me, lambda k: jnp.concatenate([ps[k][0], ps[k][3]], axis=0), chaos, residual)
+    by_table(n, me, lambda k: jnp.concatenate([ps[me ^ k, 0], ps[me ^ k, 3]], axis=0), chaos, residual)
 
     def updated(g, value):
         w = value[:rows] + value[rows:]
@@ -274,7 +249,7 @@
 
 
 def lanes_of(out, sums, base):
-    lane = lax.broadcasted_iota(jnp.int32, out.shape, 1)
+    lane = lax.broadcasted_iota(jnp.int32, out.shape, 2)
     row = jnp.zeros(out.shape, F32)
     for at, value in enumerate(sums):
         row = jnp.where(lane == base + at, value, row)
@@ -308,7 +283,7 @@
 def end_body(n, cells, where, u_ref, dots, *refs):
     ws, vs, xs, out = refs[:n], refs[n : 2 * n], refs[2 * n : 3 * n], refs[3 * n]
     rows = u_ref.shape[0] // n
-    means = jnp.sum(dots[...], axis=0, keepdims=True) / cells
+    means = jnp.sum(dots[...], axis=0)[:1] / cells
     lane = lax.broadcasted_iota(jnp.int32, means.shape, 1)
     g00, g01, g11, g02, g12, g22 = [
         jnp.sum(jnp.where(lane == at, means, 0.0), axis=1, keepdims=True) for at in range(6)
@@ -331,16 +306,6 @@
         w = ws[k][0].astype(F32) + ws[k][1].astype(F32)
         moved = x0 * w + x1 * vs[k][0].astype(F32) + x2 * xs[k][0].astype(F32)
         out[at, :] = u_ref[at, :] + moved
-
-
-def gather_start(own, quarter, n):
-    size = own.shape[0] // 4
-    mine = lax.dynamic_slice_in_dim(own, quarter * size, size, 0)
-    return [flip_permute(mine, "mode", k) for k in range(1, n)]
-
-
-def gather_end(here, there):
-    return [here, flip_permute(here, "space", 1), there, flip_permute(there, "space", 1)]
 
 
 def shards(
@@ -376,50 +341,45 @@
         return [shaped((ghost, times * width))] * 2
 
     one, two = shaped((nodes, width)), shaped((nodes, 2 * width))
+    square = shaped((modes, modes))
     own = jnp.swapaxes(chaos_vals, 1, 2)
-    pieces = gather_start(own, quarter, n)
-    whole, lower, upper = call(start_body, [one] + edges(1), [guess, pick], far=1, limit=56)
+    share = own.shape[0] // 4
+    mine = lax.dynamic_slice_in_dim(own, quarter * share, share, 0)
+    here = swap(jnp.broadcast_to(mine[None], (n,) + mine.shape))
+    here = lax.dynamic_slice_in_dim(jnp.concatenate([here, here], axis=0), me + 1, n - 1, 0)
+    whole, lower, upper = call(start_body, [one] + edges(1), [guess, pick])
     below, above = halo(lower, upper)
-    both, lower, upper, *ps = call(
+    own, below, above = lax.optimization_barrier((own, below, above))
+    both, lower, upper, ps = call(
         functools.partial(first_body, n),
-        [two] + edges(2) + sent(4),
-        [where, spatial_diag, spatial_ghost, forcing, whole, below, above, pick],
-        1,
-        [one],
-        3,
-        56,
+        [two] + edges(2) + [shaped((n, 4, rows, width))],
+        [spatial_diag, spatial_ghost, forcing, whole, below, above, pick],
     )
     below, above = halo(lower, upper)
-    ps = trade(ps)
-    pieces, below, above = lax.optimization_barrier((pieces, below, above))
-    here = jnp.stack(pieces)
+    ps = swap(ps)
+    here, below, above = lax.optimization_barrier((here, below, above))
     there = flip_permute(here, "space", 2)
     both, p1, lower, upper = call(
         second_body,
         [two, one] + edges(1),
         [spatial_diag, spatial_ghost, both, below, above, pick],
-        far=2,
-        limit=56,
     )
     below, above = halo(lower, upper)
-    ps, below, above = lax.optimization_barrier((ps, below, above))
     qs = call(
         functools.partial(third_body, n),
         sent(3),
         [where, spatial_diag, spatial_ghost, both, p1, below, above],
         1,
         [one],
-        2,
-        56,
-    )
-    here, there, qs = lax.optimization_barrier((here, there, qs))
+    )
+    there, qs = lax.optimization_barrier((there, qs))
     qs = trade(qs)
-    tables = gather_end(here, there)
-
+    beside, across = flip_permute(here, "space", 1), flip_permute(there, "space", 1)
+    across, ps = lax.optimization_barrier((across, ps))
     (chaos,) = call(
         functools.partial(table_body, n, slots),
-        [shaped((modes, modes))],
-        [where, chaos_targets, chaos_count, own] + tables,
+        [square],
+        [where, chaos_targets, chaos_count, own, here, beside, there, across],
         3,
     )
     slab = shaped((n, rows, width), F32)
@@ -427,12 +387,12 @@
     w0, c1, ca0, *ws = call(
         functools.partial(stage_a, n),
         [slab, slab, slab] + sent(2),
-        [where] + ps + [chaos, mean_inverse],
+        [where, ps, chaos, mean_inverse],
         1,
         [double, shaped((n, rows, width))],
     )
     ws = trade(ws)
-    tile = shaped((devices, 128), F32)
+    tile = shaped((devices, 8, 128), F32)
     *vs, v1, held, sums = call(
         functools.partial(stage_b, n),
         sent(1) + [slab, slab, tile],

time: 125 us -> 122 us (0.976)
  Pallas kernels: 46.3 us -> 33.6 us
  local copies, waits for them, and re-layouts: 5.84 us -> 15.4 us
  waiting for transfers between devices: 26.7 us -> 17.6 us
  starting transfers between devices: 43.3 us -> 52.2 us
    pallas_call x9, Pallas kernels: 46.3 us -> 33.6 us  [call(): pl.pallas_call(body, out_shape=outs, in_specs=[SMEM] * scalars + [VMEM] *...]
    ppermute x3, waiting for transfers between devices: 13.3 us -> 3.72 us  [halo(): above = lax.ppermute(lower, 'space', [(i + 1, i) for i in range(count - 1)])]
    all_to_all x0 -> x2, starting transfers between devices: none -> 9.28 us  [swap(): return lax.all_to_all(x, 'mode', split_axis=0, concat_axis=0, tiled=True)]
    unnamed x40, local copies, waits for them, and re-layouts: 5.82 us -> 13 us
    all_to_all x1, waiting for transfers between devices: 7.15 us -> 0.01 us  [shards(): lax.all_to_all(dots, ('space', 'mode'), split_axis=0, concat_axis=0, tile...]
    ppermute x21 -> x15, waiting for transfers between devices: 5.06 us -> 9.8 us  [flip_permute(): lax.ppermute(x, axis, [(i, i ^ bit) for i in range(lax.axis_size(axis))])]
    all_to_all x0 -> x2, waiting for transfers between devices: none -> 4.06 us  [swap(): return lax.all_to_all(x, 'mode', split_axis=0, concat_axis=0, tiled=True)]
    ppermute x21 -> x15, starting transfers between devices: 26.8 us -> 24.2 us  [flip_permute(): lax.ppermute(x, axis, [(i, i ^ bit) for i in range(lax.axis_size(axis))])]
  transfers between devices with their start and end apart: 28 -> 24, of which waited for: 5 -> 7; matrix products, arithmetic and copies ran while one was open for 2% -> 4% of each run, Pallas kernels for 33% -> 26%
where the time goes in v3:
time: 122 us
  starting transfers between devices  52.2 us (43%)
  Pallas kernels  33.6 us (28%)
  waiting for transfers between devices  17.6 us (14%)
  local copies, waits for them, and re-layouts  15.4 us (13%)
  other arithmetic  2.49 us (2%)
    pallas_call x9, Pallas kernels, call(): pl.pallas_call(body, out_shape=outs, in_specs=[SMEM] * scalars + [VMEM] *...  33.6 us
    ppermute x15, starting transfers between devices, flip_permute(): lax.ppermute(x, axis, [(i, i ^ bit) for i in range(lax.axis_size(axis))])  24.2 us
    unnamed x40, local copies, waits for them, and re-layouts  13 us
    ppermute x3, starting transfers between devices, halo(): below = lax.ppermute(upper, 'space', [(i, i + 1) for i in range(count - 1)])  10.7 us
    ppermute x15, waiting for transfers between devices, flip_permute(): lax.ppermute(x, axis, [(i, i ^ bit) for i in range(lax.axis_size(axis))])  9.8 us
    all_to_all x2, starting transfers between devices, swap(): return lax.all_to_all(x, 'mode', split_axis=0, concat_axis=0, tiled=True)  9.28 us
    all_to_all x1, starting transfers between devices, shards(): lax.all_to_all(dots, ('space', 'mode'), split_axis=0, concat_axis=0, tile...  4.08 us
    all_to_all x2, waiting for transfers between devices, swap(): return lax.all_to_all(x, 'mode', split_axis=0, concat_axis=0, tiled=True)  4.06 us
  transfers between devices with their start and end apart: 24, of which 7 were waited for; matrix products, arithmetic and copies ran while one was open for 4% of the time, Pallas kernels for 26%

profile of v3, /device:TPU:0, one launch (start us, length us, event | category | flops | bytes accessed | tf_op | source)
XLA Modules:
  0.0 121.5 jit_solution(2425026522217376662)
XLA Ops:
  2.4 5.2 %all-to-all-start = ((bf16[4,8,128,128]{3,2,1,0:T(8,128)(2,1)}), bf16[4,8,128,128]{3,2,1,0:T(8,128)(2,1)}, u32[]{:S(2)}, u32[]{:S(2)}) async-start(bf16[4,8,128,128]{3,2,1,0:T(8,128)(2,1)} %broadcast_in_dim.2), calls=%async_computation | async-start | bytes 2097152 | tf_op jit(solution)/shard_map/all_to_all | solution.py:55
  8.8 1.6 %collective-permute-start = (bf16[128,512]{1,0:T(8,128)(2,1)S(1)}, bf16[128,512]{1,0:T(8,128)(2,1)S(1)}, u32[]{:S(2)}, u32[]{:S(2)}) collective-permute-start(bf16[128,512]{1,0:T(8,128)(2,1)S(1)} %get-tuple-element.61), channel_id=1, source_target_pairs={{0,4},{4,8},{8,12},{12,16},{16,20},{20,24},{24,28},{1,5},{5,9},{9,... | collective-permute-start | bytes 393224 | tf_op jit(solution)/shard_map/ppermute | solution.py:60
  11.8 2.3 %copy.10 = bf16[32,128,128]{1,2,0:T(8,128)(2,1)} copy(bf16[32,128,128]{2,1,0:T(8,128)(2,1)} %param.14) | data formatting | bytes 2097152 | tf_op args[5]
  14.0 1.9 %collective-permute-done.1.above = bf16[128,512]{1,0:T(8,128)(2,1)S(1)} collective-permute-done((bf16[128,512]{1,0:T(8,128)(2,1)S(1)}, bf16[128,512]{1,0:T(8,128)(2,1)S(1)}, u32[]{:S(2)}, u32[]{:S(2)}) %collective-permute-start.1) | collective-permute-done | bytes 131104 | tf_op jit(solution)/shard_map/ppermute | solution.py:61
  15.9 1.8 %shard_map.92 = (bf16[512,1024]{1,0:T(8,128)(2,1)S(1)}, bf16[128,1024]{1,0:T(8,128)(2,1)S(1)}, bf16[128,1024]{1,0:T(8,128)(2,1)}, bf16[4,4,128,512]{3,2,1,0:T(8,128)(2,1)S(1)}) custom-call(bf16[512,512]{1,0:T(8,128)(2,1)S(1)} %copy-done.1, bf16[512,256]{1,0:T(8,128)(2,1)S(1)} %copy-done.5, f32[512,512]{1,0:T(8,128)S(1)} %copy-done.9, ...), custom_call_target="tpu_custom_call" | custom-call | flops 1 | bytes 1 | tf_op jit(solution)/shard_map/pallas_call | solution.py:19
  20.1 5.9 %collective-permute-start.2 = (bf16[128,1024]{1,0:T(8,128)(2,1)}, bf16[128,1024]{1,0:T(8,128)(2,1)S(1)}, u32[]{:S(2)}, u32[]{:S(2)}) collective-permute-start(bf16[128,1024]{1,0:T(8,128)(2,1)} %get-tuple-element.67), channel_id=1, source_target_pairs={{0,4},{4,8},{8,12},{12,16},{16,20},{20,24},{24,28},{1,5},{5,9},{9,... | collective-permute-start | bytes 786440 | tf_op jit(solution)/shard_map/ppermute | solution.py:60
  27.2 2.3 %fusion.here = bf16[3,8,128,128]{3,2,1,0:T(8,128)(2,1)} fusion(s32[]{:T(128)S(6)} %select_n.15, bf16[4,8,128,128]{3,2,1,0:T(8,128)(2,1)} %all-to-all-done), kind=kLoop, calls=%fused_computation.2 | loop fusion | flops 393216 | bytes 1835012 | tf_op jit(solution)/shard_map/concatenate | solution.py:349
  30.3 3.8 %collective-permute-start.5 = (bf16[3,8,128,128]{3,2,1,0:T(8,128)(2,1)}, bf16[3,8,128,128]{3,2,1,0:T(8,128)(2,1)}, u32[]{:S(2)}, u32[]{:S(2)}) collective-permute-start(bf16[3,8,128,128]{3,2,1,0:T(8,128)(2,1)} %fusion.here), channel_id=1, source_target_pairs={{0,8},{4,12},{8,0},{12,4},{16,24},{20,28},{24,16},{28,20},{1,9},{5... | collective-permute-start | bytes 2359304 | tf_op jit(solution)/shard_map/ppermute | solution.py:47
  34.1 4.1 %all-to-all-start.1 = ((bf16[4,4,128,512]{3,2,1,0:T(8,128)(2,1)}), bf16[4,4,128,512]{3,2,1,0:T(8,128)(2,1)S(1)}, u32[]{:S(2)}, u32[]{:S(2)}) async-start(bf16[4,4,128,512]{3,2,1,0:T(8,128)(2,1)} %copy-done.6), calls=%async_computation.1 | async-start | bytes 4194304 | tf_op jit(solution)/shard_map/all_to_all | solution.py:55
  41.8 3.2 %collective-permute-start.6 = (bf16[128,512]{1,0:T(8,128)(2,1)S(1)}, bf16[128,512]{1,0:T(8,128)(2,1)S(1)}, u32[]{:S(2)}, u32[]{:S(2)}) collective-permute-start(bf16[128,512]{1,0:T(8,128)(2,1)S(1)} %get-tuple-element.75), channel_id=1, source_target_pairs={{0,4},{4,8},{8,12},{12,16},{16,20},{20,24},{24,28},{1,5},{5,9},{9,... | collective-permute-start | bytes 393224 | tf_op jit(solution)/shard_map/ppermute | solution.py:60
  46.4 1.9 %collective-permute-done.7.above = bf16[128,512]{1,0:T(8,128)(2,1)S(1)} collective-permute-done((bf16[128,512]{1,0:T(8,128)(2,1)S(1)}, bf16[128,512]{1,0:T(8,128)(2,1)S(1)}, u32[]{:S(2)}, u32[]{:S(2)}) %collective-permute-start.7) | collective-permute-done | bytes 131104 | tf_op jit(solution)/shard_map/ppermute | solution.py:61
  48.2 2.3 %shard_map.94 = (bf16[3,128,512]{2,1,0:T(8,128)(2,1)S(1)}, bf16[3,128,512]{2,1,0:T(8,128)(2,1)}, bf16[3,128,512]{2,1,0:T(8,128)(2,1)}, bf16[3,128,512]{2,1,0:T(8,128)(2,1)}) custom-call(s32[2]{0:T(128)S(1)} %pad_add_fusion.where, bf16[512,512]{1,0:T(8,128)(2,1)S(1)} %copy-done.1, bf16[512,256]{1,0:T(8,128)(2,1)S(1)} %copy-done.5, ...), custom_call_target="tpu_custom_call" | custom-call | flops 1 | bytes 1 | tf_op jit(solution)/shard_map/pallas_call | solution.py:19
  51.4 5.0 %collective-permute-start.8 = (bf16[3,8,128,128]{3,2,1,0:T(8,128)(2,1)}, bf16[3,8,128,128]{3,2,1,0:T(8,128)(2,1)S(1)}, u32[]{:S(2)}, u32[]{:S(2)}) collective-permute-start(bf16[3,8,128,128]{3,2,1,0:T(8,128)(2,1)} %collective-permute-done.5.there), channel_id=1, source_target_pairs={{0,4},{4,0},{8,12},{12,8},{16,20},{20,16},{24,28},{28,24},{1,5},{5... | collective-permute-start | bytes 2359304 | tf_op jit(solution)/shard_map/ppermute | solution.py:47
  56.5 1.9 %collective-permute-start.9 = (bf16[3,128,512]{2,1,0:T(8,128)(2,1)}, bf16[3,128,512]{2,1,0:T(8,128)(2,1)}, u32[]{:S(2)}, u32[]{:S(2)}) collective-permute-start(bf16[3,128,512]{2,1,0:T(8,128)(2,1)} %get-tuple-element.87), channel_id=1, source_target_pairs={{0,1},{1,0},{2,3},{3,2},{4,5},{5,4},{6,7},{7,6},{8,9},{9,8},{10,11... | collective-permute-start | bytes 1179656 | tf_op jit(solution)/shard_map/ppermute | solution.py:47
  58.4 1.5 %collective-permute-start.10 = (bf16[3,128,512]{2,1,0:T(8,128)(2,1)}, bf16[3,128,512]{2,1,0:T(8,128)(2,1)}, u32[]{:S(2)}, u32[]{:S(2)}) collective-permute-start(bf16[3,128,512]{2,1,0:T(8,128)(2,1)} %get-tuple-element.88), channel_id=1, source_target_pairs={{0,2},{1,3},{2,0},{3,1},{4,6},{5,7},{6,4},{7,5},{8,10},{9,11},{10,... | collective-permute-start | bytes 1179656 | tf_op jit(solution)/shard_map/ppermute | solution.py:47
  60.1 4.1 %all-to-all-done.1.ps = bf16[4,4,128,512]{3,2,1,0:T(8,128)(2,1)S(1)} async-done(((bf16[4,4,128,512]{3,2,1,0:T(8,128)(2,1)}), bf16[4,4,128,512]{3,2,1,0:T(8,128)(2,1)S(1)}, u32[]{:S(2)}, u32[]{:S(2)}) %all-to-all-start.1) | async-done | bytes 2097184 | tf_op jit(solution)/shard_map/all_to_all | solution.py:55
  65.4 4.6 %shard_map.95.chaos.refs_4_ = bf16[2048,2048]{1,0:T(8,128)(2,1)S(1)} custom-call(s32[2]{0:T(128)S(1)} %pad_add_fusion.where, s32[16,8]{1,0:T(8,128)S(1)} %copy.12.targets, s32[16]{0:T(128)S(1)} %copy-done.16, bf16[32,128,128]{2,1,0:T(8,128)(2,1)S(1)} %bitcast.6, bf16[3,8,128,128]{3,2,1,0:T(8,128)(2,1)} %fusion.here, ...), custom_call_target="tpu_custom_call" | custom-call | flops 1 | bytes 1 | tf_op jit(solution)/shard_map/pallas_call | solution.py:19
  70.0 3.4 %copy-done = bf16[2048,2048]{1,0:T(8,128)(2,1)S(1)} copy-done((bf16[2048,2048]{1,0:T(8,128)(2,1)S(1)}, bf16[2048,2048]{1,0:T(8,128)(2,1)}, u32[]{:S(2)}) %copy-start) | copy-done | bytes 8388632
  73.4 6.4 %shard_map.96 = (f32[4,128,512]{2,1,0:T(8,128)S(1)}, f32[4,128,512]{2,1,0:T(8,128)S(1)}, f32[4,128,512]{2,1,0:T(8,128)S(1)}, bf16[2,128,512]{2,1,0:T(8,128)(2,1)...) custom-call(s32[2]{0:T(128)S(1)} %pad_add_fusion.where, ...), custom_call_target="tpu_custom_call" | custom-call | flops 1 | bytes 1 | tf_op jit(solution)/shard_map/pallas_call | solution.py:19
  79.8 1.6 %collective-permute-start.12 = (bf16[2,128,512]{2,1,0:T(8,128)(2,1)S(1)}, bf16[2,128,512]{2,1,0:T(8,128)(2,1)S(1)}, u32[]{:S(2)}, u32[]{:S(2)}) collective-permute-start(bf16[2,128,512]{2,1,0:T(8,128)(2,1)S(1)} %get-tuple-element.101), channel_id=1, source_target_pairs={{0,1},{1,0},{2,3},{3,2},{4,5},{5,4},{6,7},{7,6},{8,9},{9,8},{10,11... | collective-permute-start | bytes 786440 | tf_op jit(solution)/shard_map/ppermute | solution.py:47
  81.5 1.8 %collective-permute-start.14 = (bf16[2,128,512]{2,1,0:T(8,128)(2,1)S(1)}, bf16[2,128,512]{2,1,0:T(8,128)(2,1)S(1)}, u32[]{:S(2)}, u32[]{:S(2)}) collective-permute-start(bf16[2,128,512]{2,1,0:T(8,128)(2,1)S(1)} %get-tuple-element.103), channel_id=1, source_target_pairs={{0,3},{1,2},{2,1},{3,0},{4,7},{5,6},{6,5},{7,4},{8,11},{9,10},{10,... | collective-permute-start | bytes 786440 | tf_op jit(solution)/shard_map/ppermute | solution.py:47
  83.3 8.9 %shard_map.97 = (bf16[1,128,512]{2,1,0:T(8,128)(2,1)S(1)}, bf16[1,128,512]{2,1,0:T(8,128)(2,1)}, bf16[1,128,512]{2,1,0:T(8,128)(2,1)}, bf16[1,128,512]{2,1,0:T(8...) custom-call(s32[2]{0:T(128)S(1)} %pad_add_fusion.where, ...), custom_call_target="tpu_custom_call" | custom-call | flops 1 | bytes 1 | tf_op jit(solution)/shard_map/pallas_call | solution.py:19
  92.2 1.6 %collective-permute-start.15 = (bf16[1,128,512]{2,1,0:T(8,128)(2,1)}, bf16[1,128,512]{2,1,0:T(8,128)(2,1)S(1)}, u32[]{:S(2)}, u32[]{:S(2)}) collective-permute-start(bf16[1,128,512]{2,1,0:T(8,128)(2,1)} %get-tuple-element.110), channel_id=1, source_target_pairs={{0,1},{1,0},{2,3},{3,2},{4,5},{5,4},{6,7},{7,6},{8,9},{9,8},{10,11... | collective-permute-start | bytes 393224 | tf_op jit(solution)/shard_map/ppermute | solution.py:47
  93.8 5.6 %shard_map.98 = (bf16[1,128,512]{2,1,0:T(8,128)(2,1)S(1)}, bf16[1,128,512]{2,1,0:T(8,128)(2,1)}, bf16[1,128,512]{2,1,0:T(8,128)(2,1)S(1)}, bf16[1,128,512]{2,1,0:T(8,128)(2,1)S(1)}, f32[32,8,128]{2,1,0:T(8,128)}) custom-call(s32[2]{0:T(128)S(1)} %pad_add_fusion.where, bf16[2048,2048]{1,0:T(8,128)(2,1)S(1)} %shard_map.95.chaos.refs_4_, ...), custom_call_target="tpu_custom_call" | custom-call | flops 1 | bytes 1 | tf_op jit(solution)/shard_map/pallas_call | solution.py:19
  99.5 4.1 %all-to-all-start.2 = ((f32[32,8,128]{2,1,0:T(8,128)}), f32[32,8,128]{2,1,0:T(8,128)S(1)}, u32[]{:S(2)}, u32[]{:S(2)}) async-start(f32[32,8,128]{2,1,0:T(8,128)} %get-tuple-element.104), calls=%async_computation.2 | async-start | bytes 262144 | tf_op jit(solution)/shard_map/all_to_all | solution.py:413
  103.6 1.8 %collective-permute-start.16 = (bf16[1,128,512]{2,1,0:T(8,128)(2,1)}, bf16[1,128,512]{2,1,0:T(8,128)(2,1)S(1)}, u32[]{:S(2)}, u32[]{:S(2)}) collective-permute-start(bf16[1,128,512]{2,1,0:T(8,128)(2,1)} %get-tuple-element.111), channel_id=1, source_target_pairs={{0,2},{1,3},{2,0},{3,1},{4,6},{5,7},{6,4},{7,5},{8,10},{9,11},{10,... | collective-permute-start | bytes 393224 | tf_op jit(solution)/shard_map/ppermute | solution.py:47
  105.4 1.5 %collective-permute-start.17 = (bf16[1,128,512]{2,1,0:T(8,128)(2,1)}, bf16[1,128,512]{2,1,0:T(8,128)(2,1)S(1)}, u32[]{:S(2)}, u32[]{:S(2)}) collective-permute-start(bf16[1,128,512]{2,1,0:T(8,128)(2,1)} %get-tuple-element.112), channel_id=1, source_target_pairs={{0,3},{1,2},{2,1},{3,0},{4,7},{5,6},{6,5},{7,4},{8,11},{9,10},{10,... | collective-permute-start | bytes 393224 | tf_op jit(solution)/shard_map/ppermute | solution.py:47
  107.1 1.8 %collective-permute-start.19 = (bf16[1,128,512]{2,1,0:T(8,128)(2,1)S(1)}, bf16[1,128,512]{2,1,0:T(8,128)(2,1)S(1)}, u32[]{:S(2)}, u32[]{:S(2)}) collective-permute-start(bf16[1,128,512]{2,1,0:T(8,128)(2,1)S(1)} %get-tuple-element.115), channel_id=1, source_target_pairs={{0,2},{1,3},{2,0},{3,1},{4,6},{5,7},{6,4},{7,5},{8,10},{9,11},{10,... | collective-permute-start | bytes 393224 | tf_op jit(solution)/shard_map/ppermute | solution.py:47
  108.9 1.5 %collective-permute-start.20 = (bf16[1,128,512]{2,1,0:T(8,128)(2,1)S(1)}, bf16[1,128,512]{2,1,0:T(8,128)(2,1)S(1)}, u32[]{:S(2)}, u32[]{:S(2)}) collective-permute-start(bf16[1,128,512]{2,1,0:T(8,128)(2,1)S(1)} %get-tuple-element.116), channel_id=1, source_target_pairs={{0,3},{1,2},{2,1},{3,0},{4,7},{5,6},{6,5},{7,4},{8,11},{9,10},{10,... | collective-permute-start | bytes 393224 | tf_op jit(solution)/shard_map/ppermute | solution.py:47
  110.3 3.8 %collective-permute-done.16.refs_6_ = bf16[1,128,512]{2,1,0:T(8,128)(2,1)S(1)} collective-permute-done((bf16[1,128,512]{2,1,0:T(8,128)(2,1)}, bf16[1,128,512]{2,1,0:T(8,128)(2,1)S(1)}, u32[]{:S(2)}, u32[]{:S(2)}) %collective-permute-start.16) | collective-permute-done | bytes 131104 | tf_op jit(solution)/shard_map/ppermute | solution.py:47
  115.0 4.2 %collective-permute-done.19.refs_10_ = bf16[1,128,512]{2,1,0:T(8,128)(2,1)S(1)} collective-permute-done((bf16[1,128,512]{2,1,0:T(8,128)(2,1)S(1)}, bf16[1,128,512]{2,1,0:T(8,128)(2,1)S(1)}, u32[]{:S(2)}, u32[]{:S(2)}) %collective-permute-start.19) | collective-permute-done | bytes 131104 | tf_op jit(solution)/shard_map/ppermute | solution.py:47
  119.3 2.3 %shard_map.99 = f32[512,512]{1,0:T(8,128)} custom-call(s32[2]{0:T(128)S(1)} %pad_add_fusion.where, f32[512,512]{1,0:T(8,128)S(1)} %copy-done.3, f32[32,8,128]{2,1,0:T(8,128)S(1)} %all-to-all-done.2.dots, bf16[2,128,512]{2,1,0:T(8,128)(2,1)S(1)} %copy-done.13, bf16[2,128,512]{2,1,0:T(8,128)(2,1)S(1)} %collective-permute-done.12.refs_1_, ...), custom_call_target="tpu_custom_call" | custom-call | flops 1 | bytes 1 | tf_op jit(solution)/shard_map/pallas_call | solution.py:19
  (71 shorter events, 17.8 us)
Async XLA Ops:
  2.4 24.8 %all-to-all-start = ((bf16[4,8,128,128]{3,2,1,0:T(8,128)(2,1)}), bf16[4,8,128,128]{3,2,1,0:T(8,128)(2,1)}, u32[]{:S(2)}, u32[]{:S(2)}) async-start(bf16[4,8,128,128]{3,2,1,0:T(8,128)(2,1)} %broadcast_in_dim.2), calls=%async_computation | async-start | bytes 2097152 | tf_op jit(solution)/shard_map/all_to_all | solution.py:55
  7.6 8.3 %copy-start.1 = (bf16[512,512]{1,0:T(8,128)(2,1)S(1)}, bf16[512,512]{1,0:T(8,128)(2,1)}, u32[]{:S(2)}) copy-start(bf16[512,512]{1,0:T(8,128)(2,1)} %diag.5) | copy-start | bytes 1572868
  7.6 8.3 %copy-start.5 = (bf16[512,256]{1,0:T(8,128)(2,1)S(1)}, bf16[512,256]{1,0:T(8,128)(2,1)}, u32[]{:S(2)}) copy-start(bf16[512,256]{1,0:T(8,128)(2,1)} %ghostly.5) | copy-start | bytes 786436
  7.6 8.3 %copy-start.9 = (f32[512,512]{1,0:T(8,128)S(1)}, f32[512,512]{1,0:T(8,128)}, u32[]{:S(2)}) copy-start(f32[512,512]{1,0:T(8,128)} %f_ref.1) | copy-start | bytes 3145732
  8.8 5.2 %collective-permute-start = (bf16[128,512]{1,0:T(8,128)(2,1)S(1)}, bf16[128,512]{1,0:T(8,128)(2,1)S(1)}, u32[]{:S(2)}, u32[]{:S(2)}) collective-permute-start(bf16[128,512]{1,0:T(8,128)(2,1)S(1)} %get-tuple-element.61), channel_id=1, source_target_pairs={{0,4},{4,8},{8,12},{12,16},{16,20},{20,24},{24,28},{1,5},{5,9},{9,... | collective-permute-start | bytes 393224 | tf_op jit(solution)/shard_map/ppermute | solution.py:60
  10.5 5.4 %collective-permute-start.1 = (bf16[128,512]{1,0:T(8,128)(2,1)S(1)}, bf16[128,512]{1,0:T(8,128)(2,1)S(1)}, u32[]{:S(2)}, u32[]{:S(2)}) collective-permute-start(bf16[128,512]{1,0:T(8,128)(2,1)S(1)} %get-tuple-element.62), channel_id=1, source_target_pairs={{4,0},{8,4},{12,8},{16,12},{20,16},{24,20},{28,24},{5,1},{9,5},{13... | collective-permute-start | bytes 393224 | tf_op jit(solution)/shard_map/ppermute | solution.py:61
  20.1 9.5 %collective-permute-start.2 = (bf16[128,1024]{1,0:T(8,128)(2,1)}, bf16[128,1024]{1,0:T(8,128)(2,1)S(1)}, u32[]{:S(2)}, u32[]{:S(2)}) collective-permute-start(bf16[128,1024]{1,0:T(8,128)(2,1)} %get-tuple-element.67), channel_id=1, source_target_pairs={{0,4},{4,8},{8,12},{12,16},{16,20},{20,24},{24,28},{1,5},{5,9},{9,... | collective-permute-start | bytes 786440 | tf_op jit(solution)/shard_map/ppermute | solution.py:60
  25.9 3.6 %collective-permute-start.3 = (bf16[128,1024]{1,0:T(8,128)(2,1)S(1)}, bf16[128,1024]{1,0:T(8,128)(2,1)S(1)}, u32[]{:S(2)}, u32[]{:S(2)}) collective-permute-start(bf16[128,1024]{1,0:T(8,128)(2,1)S(1)} %get-tuple-element.68), channel_id=1, source_target_pairs={{4,0},{8,4},{12,8},{16,12},{20,16},{24,20},{28,24},{5,1},{9,5},{13... | collective-permute-start | bytes 786440 | tf_op jit(solution)/shard_map/ppermute | solution.py:61
  30.3 21.2 %collective-permute-start.5 = (bf16[3,8,128,128]{3,2,1,0:T(8,128)(2,1)}, bf16[3,8,128,128]{3,2,1,0:T(8,128)(2,1)}, u32[]{:S(2)}, u32[]{:S(2)}) collective-permute-start(bf16[3,8,128,128]{3,2,1,0:T(8,128)(2,1)} %fusion.here), channel_id=1, source_target_pairs={{0,8},{4,12},{8,0},{12,4},{16,24},{20,28},{24,16},{28,20},{1,9},{5... | collective-permute-start | bytes 2359304 | tf_op jit(solution)/shard_map/ppermute | solution.py:47
  34.1 30.1 %all-to-all-start.1 = ((bf16[4,4,128,512]{3,2,1,0:T(8,128)(2,1)}), bf16[4,4,128,512]{3,2,1,0:T(8,128)(2,1)S(1)}, u32[]{:S(2)}, u32[]{:S(2)}) async-start(bf16[4,4,128,512]{3,2,1,0:T(8,128)(2,1)} %copy-done.6), calls=%async_computation.1 | async-start | bytes 4194304 | tf_op jit(solution)/shard_map/all_to_all | solution.py:55
  40.3 19.7 %copy-start.17 = (s32[16,8]{0,1:T(8,128)S(1)}, s32[16,8]{0,1:T(8,128)}, u32[]{:S(2)}) copy-start(s32[16,8]{0,1:T(8,128)} %param.15) | copy-start | bytes 1540
  40.3 23.8 %copy-start.16 = (s32[16]{0:T(128)S(1)}, s32[16]{0:T(128)}, u32[]{:S(2)}) copy-start(s32[16]{0:T(128)} %counts.1) | copy-start | bytes 196
  41.8 4.6 %collective-permute-start.6 = (bf16[128,512]{1,0:T(8,128)(2,1)S(1)}, bf16[128,512]{1,0:T(8,128)(2,1)S(1)}, u32[]{:S(2)}, u32[]{:S(2)}) collective-permute-start(bf16[128,512]{1,0:T(8,128)(2,1)S(1)} %get-tuple-element.75), channel_id=1, source_target_pairs={{0,4},{4,8},{8,12},{12,16},{16,20},{20,24},{24,28},{1,5},{5,9},{9,... | collective-permute-start | bytes 393224 | tf_op jit(solution)/shard_map/ppermute | solution.py:60
  45.0 3.2 %collective-permute-start.7 = (bf16[128,512]{1,0:T(8,128)(2,1)S(1)}, bf16[128,512]{1,0:T(8,128)(2,1)S(1)}, u32[]{:S(2)}, u32[]{:S(2)}) collective-permute-start(bf16[128,512]{1,0:T(8,128)(2,1)S(1)} %get-tuple-element.76), channel_id=1, source_target_pairs={{4,0},{8,4},{12,8},{16,12},{20,16},{24,20},{28,24},{5,1},{9,5},{13... | collective-permute-start | bytes 393224 | tf_op jit(solution)/shard_map/ppermute | solution.py:61
  51.4 12.7 %collective-permute-start.8 = (bf16[3,8,128,128]{3,2,1,0:T(8,128)(2,1)}, bf16[3,8,128,128]{3,2,1,0:T(8,128)(2,1)S(1)}, u32[]{:S(2)}, u32[]{:S(2)}) collective-permute-start(bf16[3,8,128,128]{3,2,1,0:T(8,128)(2,1)} %collective-permute-done.5.there), channel_id=1, source_target_pairs={{0,4},{4,0},{8,12},{12,8},{16,20},{20,16},{24,28},{28,24},{1,5},{5... | collective-permute-start | bytes 2359304 | tf_op jit(solution)/shard_map/ppermute | solution.py:47
  56.5 7.7 %collective-permute-start.4 = (bf16[3,8,128,128]{3,2,1,0:T(8,128)(2,1)}, bf16[3,8,128,128]{3,2,1,0:T(8,128)(2,1)}, u32[]{:S(2)}, u32[]{:S(2)}) collective-permute-start(bf16[3,8,128,128]{3,2,1,0:T(8,128)(2,1)} %fusion.here), channel_id=1, source_target_pairs={{0,4},{4,0},{8,12},{12,8},{16,20},{20,16},{24,28},{28,24},{1,5},{5... | collective-permute-start | bytes 2359304 | tf_op jit(solution)/shard_map/ppermute | solution.py:47
  56.5 25.0 %collective-permute-start.9 = (bf16[3,128,512]{2,1,0:T(8,128)(2,1)}, bf16[3,128,512]{2,1,0:T(8,128)(2,1)}, u32[]{:S(2)}, u32[]{:S(2)}) collective-permute-start(bf16[3,128,512]{2,1,0:T(8,128)(2,1)} %get-tuple-element.87), channel_id=1, source_target_pairs={{0,1},{1,0},{2,3},{3,2},{4,5},{5,4},{6,7},{7,6},{8,9},{9,8},{10,11... | collective-permute-start | bytes 1179656 | tf_op jit(solution)/shard_map/ppermute | solution.py:47
  58.4 24.9 %collective-permute-start.10 = (bf16[3,128,512]{2,1,0:T(8,128)(2,1)}, bf16[3,128,512]{2,1,0:T(8,128)(2,1)}, u32[]{:S(2)}, u32[]{:S(2)}) collective-permute-start(bf16[3,128,512]{2,1,0:T(8,128)(2,1)} %get-tuple-element.88), channel_id=1, source_target_pairs={{0,2},{1,3},{2,0},{3,1},{4,6},{5,7},{6,4},{7,5},{8,10},{9,11},{10,... | collective-permute-start | bytes 1179656 | tf_op jit(solution)/shard_map/ppermute | solution.py:47
  59.9 23.4 %collective-permute-start.11 = (bf16[3,128,512]{2,1,0:T(8,128)(2,1)}, bf16[3,128,512]{2,1,0:T(8,128)(2,1)}, u32[]{:S(2)}, u32[]{:S(2)}) collective-permute-start(bf16[3,128,512]{2,1,0:T(8,128)(2,1)} %get-tuple-element.89), channel_id=1, source_target_pairs={{0,3},{1,2},{2,1},{3,0},{4,7},{5,6},{6,5},{7,4},{8,11},{9,10},{10,... | collective-permute-start | bytes 1179656 | tf_op jit(solution)/shard_map/ppermute | solution.py:47
  79.7 12.5 %copy-start.12 = (bf16[2,128,512]{2,1,0:T(8,128)(2,1)}, bf16[2,128,512]{2,1,0:T(8,128)(2,1)S(1)}, u32[]{:S(2)}) copy-start(bf16[2,128,512]{2,1,0:T(8,128)(2,1)S(1)} %get-tuple-element.105.refs_0_) | copy-start | bytes 786436
  79.8 19.7 %collective-permute-start.12 = (bf16[2,128,512]{2,1,0:T(8,128)(2,1)S(1)}, bf16[2,128,512]{2,1,0:T(8,128)(2,1)S(1)}, u32[]{:S(2)}, u32[]{:S(2)}) collective-permute-start(bf16[2,128,512]{2,1,0:T(8,128)(2,1)S(1)} %get-tuple-element.101), channel_id=1, source_target_pairs={{0,1},{1,0},{2,3},{3,2},{4,5},{5,4},{6,7},{7,6},{8,9},{9,8},{10,11... | collective-permute-start | bytes 786440 | tf_op jit(solution)/shard_map/ppermute | solution.py:47
  81.4 18.1 %collective-permute-start.13 = (bf16[2,128,512]{2,1,0:T(8,128)(2,1)S(1)}, bf16[2,128,512]{2,1,0:T(8,128)(2,1)S(1)}, u32[]{:S(2)}, u32[]{:S(2)}) collective-permute-start(bf16[2,128,512]{2,1,0:T(8,128)(2,1)S(1)} %get-tuple-element.102), channel_id=1, source_target_pairs={{0,2},{1,3},{2,0},{3,1},{4,6},{5,7},{6,4},{7,5},{8,10},{9,11},{10,... | collective-permute-start | bytes 786440 | tf_op jit(solution)/shard_map/ppermute | solution.py:47
  81.5 18.0 %collective-permute-start.14 = (bf16[2,128,512]{2,1,0:T(8,128)(2,1)S(1)}, bf16[2,128,512]{2,1,0:T(8,128)(2,1)S(1)}, u32[]{:S(2)}, u32[]{:S(2)}) collective-permute-start(bf16[2,128,512]{2,1,0:T(8,128)(2,1)S(1)} %get-tuple-element.103), channel_id=1, source_target_pairs={{0,3},{1,2},{2,1},{3,0},{4,7},{5,6},{6,5},{7,4},{8,11},{9,10},{10,... | collective-permute-start | bytes 786440 | tf_op jit(solution)/shard_map/ppermute | solution.py:47
  92.2 16.7 %collective-permute-start.15 = (bf16[1,128,512]{2,1,0:T(8,128)(2,1)}, bf16[1,128,512]{2,1,0:T(8,128)(2,1)S(1)}, u32[]{:S(2)}, u32[]{:S(2)}) collective-permute-start(bf16[1,128,512]{2,1,0:T(8,128)(2,1)} %get-tuple-element.110), channel_id=1, source_target_pairs={{0,1},{1,0},{2,3},{3,2},{4,5},{5,4},{6,7},{7,6},{8,9},{9,8},{10,11... | collective-permute-start | bytes 393224 | tf_op jit(solution)/shard_map/ppermute | solution.py:47
  93.8 25.4 %copy-start.3 = (f32[512,512]{1,0:T(8,128)S(1)}, f32[512,512]{1,0:T(8,128)}, u32[]{:S(2)}) copy-start(f32[512,512]{1,0:T(8,128)} %u_ref.3) | copy-start | bytes 3145732
  93.8 25.4 %copy-start.13 = (bf16[2,128,512]{2,1,0:T(8,128)(2,1)S(1)}, bf16[2,128,512]{2,1,0:T(8,128)(2,1)}, u32[]{:S(2)}) copy-start(bf16[2,128,512]{2,1,0:T(8,128)(2,1)} %copy-done.12) | copy-start | bytes 786436
  99.5 19.8 %all-to-all-start.2 = ((f32[32,8,128]{2,1,0:T(8,128)}), f32[32,8,128]{2,1,0:T(8,128)S(1)}, u32[]{:S(2)}, u32[]{:S(2)}) async-start(f32[32,8,128]{2,1,0:T(8,128)} %get-tuple-element.104), calls=%async_computation.2 | async-start | bytes 262144 | tf_op jit(solution)/shard_map/all_to_all | solution.py:413
  103.6 10.6 %collective-permute-start.16 = (bf16[1,128,512]{2,1,0:T(8,128)(2,1)}, bf16[1,128,512]{2,1,0:T(8,128)(2,1)S(1)}, u32[]{:S(2)}, u32[]{:S(2)}) collective-permute-start(bf16[1,128,512]{2,1,0:T(8,128)(2,1)} %get-tuple-element.111), channel_id=1, source_target_pairs={{0,2},{1,3},{2,0},{3,1},{4,6},{5,7},{6,4},{7,5},{8,10},{9,11},{10,... | collective-permute-start | bytes 393224 | tf_op jit(solution)/shard_map/ppermute | solution.py:47
  105.4 8.8 %collective-permute-start.17 = (bf16[1,128,512]{2,1,0:T(8,128)(2,1)}, bf16[1,128,512]{2,1,0:T(8,128)(2,1)S(1)}, u32[]{:S(2)}, u32[]{:S(2)}) collective-permute-start(bf16[1,128,512]{2,1,0:T(8,128)(2,1)} %get-tuple-element.112), channel_id=1, source_target_pairs={{0,3},{1,2},{2,1},{3,0},{4,7},{5,6},{6,5},{7,4},{8,11},{9,10},{10,... | collective-permute-start | bytes 393224 | tf_op jit(solution)/shard_map/ppermute | solution.py:47
  106.9 8.2 %collective-permute-start.18 = (bf16[1,128,512]{2,1,0:T(8,128)(2,1)}, bf16[1,128,512]{2,1,0:T(8,128)(2,1)S(1)}, u32[]{:S(2)}, u32[]{:S(2)}) collective-permute-start(bf16[1,128,512]{2,1,0:T(8,128)(2,1)} %get-tuple-element.114), channel_id=1, source_target_pairs={{0,1},{1,0},{2,3},{3,2},{4,5},{5,4},{6,7},{7,6},{8,9},{9,8},{10,11... | collective-permute-start | bytes 393224 | tf_op jit(solution)/shard_map/ppermute | solution.py:47
  107.1 12.1 %collective-permute-start.19 = (bf16[1,128,512]{2,1,0:T(8,128)(2,1)S(1)}, bf16[1,128,512]{2,1,0:T(8,128)(2,1)S(1)}, u32[]{:S(2)}, u32[]{:S(2)}) collective-permute-start(bf16[1,128,512]{2,1,0:T(8,128)(2,1)S(1)} %get-tuple-element.115), channel_id=1, source_target_pairs={{0,2},{1,3},{2,0},{3,1},{4,6},{5,7},{6,4},{7,5},{8,10},{9,11},{10,... | collective-permute-start | bytes 393224 | tf_op jit(solution)/shard_map/ppermute | solution.py:47
  108.9 10.3 %collective-permute-start.20 = (bf16[1,128,512]{2,1,0:T(8,128)(2,1)S(1)}, bf16[1,128,512]{2,1,0:T(8,128)(2,1)S(1)}, u32[]{:S(2)}, u32[]{:S(2)}) collective-permute-start(bf16[1,128,512]{2,1,0:T(8,128)(2,1)S(1)} %get-tuple-element.116), channel_id=1, source_target_pairs={{0,3},{1,2},{2,1},{3,0},{4,7},{5,6},{6,5},{7,4},{8,11},{9,10},{10,... | collective-permute-start | bytes 393224 | tf_op jit(solution)/shard_map/ppermute | solution.py:47
  (11 other events, 31.1 us)

commit v4 on v3

--- a/solution.py
+++ b/solution.py
@@ -210,7 +210,7 @@
     qs = refs[:n]
     chaos, inverse, w0, c1, ca0 = refs[n : n + 5]
     outs = refs[n + 5 : 2 * n + 5]
-    v1, held, sums_out, pair, more = refs[2 * n + 5 :]
+    dots, v1, held, pair, more = refs[2 * n + 5 :]
     me = where[0]
     rows = w0.shape[1]
     for g in range(n):
@@ -233,7 +233,7 @@
         pair[g, rows:] = (held[g] + value).astype(BF16)
 
     by_table(n, me, lambda k: more[k, :rows], chaos, coupled)
-    sums = [0.0] * 3
+    sums = [0.0] * 6
 
     def first(g, value):
         v = value[:rows]
@@ -245,7 +245,19 @@
         sums[2] += jnp.sum(v * v)
 
     by_inverse(n, me, lambda k: pair[k], inverse, first)
-    lanes_of(sums_out, sums, 0)
+    def last_in(g, value):
+        more[g, :rows] = (held[g] + value).astype(BF16)
+
+    by_table(n, me, lambda k: outs[k][0], chaos, last_in)
+
+    def second(g, value):
+        outs[g][1] = value.astype(BF16)
+        sums[3] += jnp.sum(w0[g] * value)
+        sums[4] += jnp.sum(v1[g] * value)
+        sums[5] += jnp.sum(value * value)
+
+    by_inverse(n, me, lambda k: more[k, :rows], inverse, second)
+    lanes_of(dots, sums, 0)
 
 
 def lanes_of(out, sums, base):
@@ -256,32 +268,8 @@
     out[...] = row
 
 
-def stage_c(n, where, chaos, inverse, w0, v1, held, sums_in, *refs):
-    outs = refs[:n]
-    dots, one, two = refs[n:]
-    me = where[0]
-    for g in range(n):
-        one[g] = v1[g].astype(BF16)
-
-    def last_in(g, value):
-        two[g] = (held[g] + value).astype(BF16)
-
-    by_table(n, me, lambda k: one[k], chaos, last_in)
-    sums = [0.0] * 3
-
-    def second(g, value):
-        outs[g][0] = value.astype(BF16)
-        sums[0] += jnp.sum(w0[g] * value)
-        sums[1] += jnp.sum(v1[g] * value)
-        sums[2] += jnp.sum(value * value)
-
-    by_inverse(n, me, lambda k: two[k], inverse, second)
-    lanes_of(dots, sums, 3)
-    dots[...] = dots[...] + sums_in[...]
-
-
 def end_body(n, cells, where, u_ref, dots, *refs):
-    ws, vs, xs, out = refs[:n], refs[n : 2 * n], refs[2 * n : 3 * n], refs[3 * n]
+    ws, vs, out = refs[:n], refs[n : 2 * n], refs[2 * n]
     rows = u_ref.shape[0] // n
     means = jnp.sum(dots[...], axis=0)[:1] / cells
     lane = lax.broadcasted_iota(jnp.int32, means.shape, 1)
@@ -304,7 +292,7 @@
     for k in range(n):
         at = rows_of(where[0] ^ k, rows)
         w = ws[k][0].astype(F32) + ws[k][1].astype(F32)
-        moved = x0 * w + x1 * vs[k][0].astype(F32) + x2 * xs[k][0].astype(F32)
+        moved = x0 * w + x1 * vs[k][0].astype(F32) + x2 * vs[k][1].astype(F32)
         out[at, :] = u_ref[at, :] + moved
 
 
@@ -393,28 +381,20 @@
     )
     ws = trade(ws)
     tile = shaped((devices, 8, 128), F32)
-    *vs, v1, held, sums = call(
+    *vs, dots = call(
         functools.partial(stage_b, n),
-        sent(1) + [slab, slab, tile],
+        sent(2) + [tile],
         [where] + qs + [chaos, mean_inverse, w0, c1, ca0],
         1,
-        [double, double],
-    )
+        [slab, slab, double, double],
+    )
+    dots, vs, ws = lax.optimization_barrier((dots, vs, ws))
     vs = trade(vs)
-    *xs, dots = call(
-        functools.partial(stage_c, n),
-        sent(1) + [tile],
-        [where, chaos, mean_inverse, w0, v1, held, sums],
-        1,
-        [shaped((n, rows, width))] * 2,
-    )
-    dots, xs, ws = lax.optimization_barrier((dots, xs, ws))
-    xs = trade(xs)
     dots = lax.all_to_all(dots, ("space", "mode"), split_axis=0, concat_axis=0, tiled=True)
     (field,) = call(
         functools.partial(end_body, n, cells),
         [shaped((nodes, width), F32)],
-        [where, guess, dots] + ws + vs + xs,
+        [where, guess, dots] + ws + vs,
         1,
     )
     return field

time: 122 us -> 115 us (0.943)
  blocking collectives: 0 us -> 12.6 us
  starting transfers between devices: 52.2 us -> 43.3 us
  waiting for transfers between devices: 17.6 us -> 8.75 us
  Pallas kernels: 33.6 us -> 31.7 us
    all_to_all x0 -> x1, blocking collectives: none -> 12.6 us  [shards(): lax.all_to_all(dots, ('space', 'mode'), split_axis=0, concat_axis=0, tile...]
    ppermute x15 -> x12, waiting for transfers between devices: 9.8 us -> 0.95 us  [flip_permute(): lax.ppermute(x, axis, [(i, i ^ bit) for i in range(lax.axis_size(axis))])]
    ppermute x15 -> x12, starting transfers between devices: 24.2 us -> 19.4 us  [flip_permute(): lax.ppermute(x, axis, [(i, i ^ bit) for i in range(lax.axis_size(axis))])]
    all_to_all x1 -> x0, starting transfers between devices: 4.08 us -> none  [shards(): lax.all_to_all(dots, ('space', 'mode'), split_axis=0, concat_axis=0, tile...]
    pallas_call x9 -> x8, Pallas kernels: 33.6 us -> 31.7 us  [call(): pl.pallas_call(body, out_shape=outs, in_specs=[SMEM] * scalars + [VMEM] *...]
  transfers between devices with their start and end apart: 24 -> 20, of which waited for: 7 -> 4; matrix products, arithmetic and copies ran while one was open for 4% -> 4% of each run, Pallas kernels for 26% -> 26%
where the time goes in v4:
time: 115 us; the launch traced here: 114 us
  starting transfers between devices  43.3 us (38%)
  Pallas kernels  31.7 us (28%)
  local copies, waits for them, and re-layouts  15.4 us (13%)
  blocking collectives  12.6 us (11%)
  waiting for transfers between devices  8.75 us (8%)
  other arithmetic  2.5 us (2%)
    pallas_call x8, Pallas kernels, call(): pl.pallas_call(body, out_shape=outs, in_specs=[SMEM] * scalars + [VMEM] *...  31.7 us
    ppermute x12, starting transfers between devices, flip_permute(): lax.ppermute(x, axis, [(i, i ^ bit) for i in range(lax.axis_size(axis))])  19.4 us
    unnamed x40, local copies, waits for them, and re-layouts  13 us
    all_to_all x1, blocking collectives, shards(): lax.all_to_all(dots, ('space', 'mode'), split_axis=0, concat_axis=0, tile...  12.6 us
    ppermute x3, starting transfers between devices, halo(): below = lax.ppermute(upper, 'space', [(i, i + 1) for i in range(count - 1)])  10.7 us
    all_to_all x2, starting transfers between devices, swap(): return lax.all_to_all(x, 'mode', split_axis=0, concat_axis=0, tiled=True)  9.28 us
    all_to_all x2, waiting for transfers between devices, swap(): return lax.all_to_all(x, 'mode', split_axis=0, concat_axis=0, tiled=True)  4.1 us
    ppermute x3, starting transfers between devices, halo(): above = lax.ppermute(lower, 'space', [(i + 1, i) for i in range(count - 1)])  3.88 us
  transfers between devices with their start and end apart: 20, of which 4 were waited for; matrix products, arithmetic and copies ran while one was open for 4% of the time, Pallas kernels for 26%

profile of v4, /device:TPU:0, one launch (start us, length us, event | category | flops | bytes accessed | tf_op | source)
XLA Modules:
  0.0 114.5 jit_solution(6845725628760739395)
XLA Ops:
  1.2 1.2 %broadcast_in_dim.2 = bf16[4,8,128,128]{3,2,1,0:T(8,128)(2,1)} broadcast(bf16[8,128,128]{2,1,0:T(8,128)(2,1)S(1)} %copy.10), dimensions={1,2,3} | broadcast | bytes 1310720 | tf_op jit(solution)/shard_map/broadcast_in_dim | solution.py:336
  2.4 5.2 %all-to-all-start = ((bf16[4,8,128,128]{3,2,1,0:T(8,128)(2,1)}), bf16[4,8,128,128]{3,2,1,0:T(8,128)(2,1)}, u32[]{:S(2)}, u32[]{:S(2)}) async-start(bf16[4,8,128,128]{3,2,1,0:T(8,128)(2,1)} %broadcast_in_dim.2), calls=%async_computation | async-start | bytes 2097152 | tf_op jit(solution)/shard_map/all_to_all | solution.py:55
  8.8 1.6 %collective-permute-start = (bf16[128,512]{1,0:T(8,128)(2,1)S(1)}, bf16[128,512]{1,0:T(8,128)(2,1)S(1)}, u32[]{:S(2)}, u32[]{:S(2)}) collective-permute-start(bf16[128,512]{1,0:T(8,128)(2,1)S(1)} %get-tuple-element.55), channel_id=1, source_target_pairs={{0,4},{4,8},{8,12},{12,16},{16,20},{20,24},{24,28},{1,5},{5,9},{9,... | collective-permute-start | bytes 393224 | tf_op jit(solution)/shard_map/ppermute | solution.py:60
  10.5 1.3 %collective-permute-start.1 = (bf16[128,512]{1,0:T(8,128)(2,1)S(1)}, bf16[128,512]{1,0:T(8,128)(2,1)S(1)}, u32[]{:S(2)}, u32[]{:S(2)}) collective-permute-start(bf16[128,512]{1,0:T(8,128)(2,1)S(1)} %get-tuple-element.56), channel_id=1, source_target_pairs={{4,0},{8,4},{12,8},{16,12},{20,16},{24,20},{28,24},{5,1},{9,5},{13... | collective-permute-start | bytes 393224 | tf_op jit(solution)/shard_map/ppermute | solution.py:61
  11.8 2.3 %copy.11 = bf16[32,128,128]{1,2,0:T(8,128)(2,1)} copy(bf16[32,128,128]{2,1,0:T(8,128)(2,1)} %param.14) | data formatting | bytes 2097152 | tf_op args[5]
  14.1 1.8 %collective-permute-done.1.above = bf16[128,512]{1,0:T(8,128)(2,1)S(1)} collective-permute-done((bf16[128,512]{1,0:T(8,128)(2,1)S(1)}, bf16[128,512]{1,0:T(8,128)(2,1)S(1)}, u32[]{:S(2)}, u32[]{:S(2)}) %collective-permute-start.1) | collective-permute-done | bytes 131104 | tf_op jit(solution)/shard_map/ppermute | solution.py:61
  15.9 1.8 %shard_map.92 = (bf16[512,1024]{1,0:T(8,128)(2,1)S(1)}, bf16[128,1024]{1,0:T(8,128)(2,1)S(1)}, bf16[128,1024]{1,0:T(8,128)(2,1)}, bf16[4,4,128,512]{3,2,1,0:T(8,128)(2,1)S(1)}) custom-call(bf16[512,512]{1,0:T(8,128)(2,1)S(1)} %copy-done.1, bf16[512,256]{1,0:T(8,128)(2,1)S(1)} %copy-done.5, f32[512,512]{1,0:T(8,128)S(1)} %copy-done.9, ...), custom_call_target="tpu_custom_call" | custom-call | flops 1 | bytes 1 | tf_op jit(solution)/shard_map/pallas_call | solution.py:19
  17.8 1.3 %copy-done.6 = bf16[4,4,128,512]{3,2,1,0:T(8,128)(2,1)} copy-done((bf16[4,4,128,512]{3,2,1,0:T(8,128)(2,1)}, bf16[4,4,128,512]{3,2,1,0:T(8,128)(2,1)S(1)}, u32[]{:S(2)}) %copy-start.6) | copy-done | bytes 2097176
  20.0 5.8 %collective-permute-start.2 = (bf16[128,1024]{1,0:T(8,128)(2,1)}, bf16[128,1024]{1,0:T(8,128)(2,1)S(1)}, u32[]{:S(2)}, u32[]{:S(2)}) collective-permute-start(bf16[128,1024]{1,0:T(8,128)(2,1)} %get-tuple-element.59), channel_id=1, source_target_pairs={{0,4},{4,8},{8,12},{12,16},{16,20},{20,24},{24,28},{1,5},{5,9},{9,... | collective-permute-start | bytes 786440 | tf_op jit(solution)/shard_map/ppermute | solution.py:60
  25.9 1.3 %collective-permute-start.3 = (bf16[128,1024]{1,0:T(8,128)(2,1)S(1)}, bf16[128,1024]{1,0:T(8,128)(2,1)S(1)}, u32[]{:S(2)}, u32[]{:S(2)}) collective-permute-start(bf16[128,1024]{1,0:T(8,128)(2,1)S(1)} %get-tuple-element.60), channel_id=1, source_target_pairs={{4,0},{8,4},{12,8},{16,12},{20,16},{24,20},{28,24},{5,1},{9,5},{13... | collective-permute-start | bytes 786440 | tf_op jit(solution)/shard_map/ppermute | solution.py:61
  27.2 2.3 %fusion.here = bf16[3,8,128,128]{3,2,1,0:T(8,128)(2,1)} fusion(s32[]{:T(128)S(6)} %select_n.15, bf16[4,8,128,128]{3,2,1,0:T(8,128)(2,1)} %all-to-all-done), kind=kLoop, calls=%fused_computation.2 | loop fusion | flops 393216 | bytes 1835012 | tf_op jit(solution)/shard_map/concatenate | solution.py:337
  30.3 3.8 %collective-permute-start.4 = (bf16[3,8,128,128]{3,2,1,0:T(8,128)(2,1)}, bf16[3,8,128,128]{3,2,1,0:T(8,128)(2,1)}, u32[]{:S(2)}, u32[]{:S(2)}) collective-permute-start(bf16[3,8,128,128]{3,2,1,0:T(8,128)(2,1)} %fusion.here), channel_id=1, source_target_pairs={{0,8},{4,12},{8,0},{12,4},{16,24},{20,28},{24,16},{28,20},{1,9},{5... | collective-permute-start | bytes 2359304 | tf_op jit(solution)/shard_map/ppermute | solution.py:47
  34.1 4.1 %all-to-all-start.1 = ((bf16[4,4,128,512]{3,2,1,0:T(8,128)(2,1)}), bf16[4,4,128,512]{3,2,1,0:T(8,128)(2,1)S(1)}, u32[]{:S(2)}, u32[]{:S(2)}) async-start(bf16[4,4,128,512]{3,2,1,0:T(8,128)(2,1)} %copy-done.6), calls=%async_computation.1 | async-start | bytes 4194304 | tf_op jit(solution)/shard_map/all_to_all | solution.py:55
  40.4 1.4 %shard_map.93 = (bf16[512,1024]{1,0:T(8,128)(2,1)S(1)}, bf16[512,512]{1,0:T(8,128)(2,1)S(1)}, bf16[128,512]{1,0:T(8,128)(2,1)S(1)}, bf16[128,512]{1,0:T(8,128)(2,1)S(1)}) custom-call(bf16[512,512]{1,0:T(8,128)(2,1)S(1)} %copy-done.1, bf16[512,256]{1,0:T(8,128)(2,1)S(1)} %copy-done.5, bf16[512,1024]{1,0:T(8,128)(2,1)S(1)} %copy-done.8, ...), custom_call_target="tpu_custom_call" | custom-call | flops 1 | bytes 1 | tf_op jit(solution)/shard_map/pallas_call | solution.py:19
  41.8 3.2 %collective-permute-start.5 = (bf16[128,512]{1,0:T(8,128)(2,1)S(1)}, bf16[128,512]{1,0:T(8,128)(2,1)S(1)}, u32[]{:S(2)}, u32[]{:S(2)}) collective-permute-start(bf16[128,512]{1,0:T(8,128)(2,1)S(1)} %get-tuple-element.67), channel_id=1, source_target_pairs={{0,4},{4,8},{8,12},{12,16},{16,20},{20,24},{24,28},{1,5},{5,9},{9,... | collective-permute-start | bytes 393224 | tf_op jit(solution)/shard_map/ppermute | solution.py:60
  45.0 1.3 %collective-permute-start.6 = (bf16[128,512]{1,0:T(8,128)(2,1)S(1)}, bf16[128,512]{1,0:T(8,128)(2,1)S(1)}, u32[]{:S(2)}, u32[]{:S(2)}) collective-permute-start(bf16[128,512]{1,0:T(8,128)(2,1)S(1)} %get-tuple-element.68), channel_id=1, source_target_pairs={{4,0},{8,4},{12,8},{16,12},{20,16},{24,20},{28,24},{5,1},{9,5},{13... | collective-permute-start | bytes 393224 | tf_op jit(solution)/shard_map/ppermute | solution.py:61
  46.4 1.9 %collective-permute-done.6.above = bf16[128,512]{1,0:T(8,128)(2,1)S(1)} collective-permute-done((bf16[128,512]{1,0:T(8,128)(2,1)S(1)}, bf16[128,512]{1,0:T(8,128)(2,1)S(1)}, u32[]{:S(2)}, u32[]{:S(2)}) %collective-permute-start.6) | collective-permute-done | bytes 131104 | tf_op jit(solution)/shard_map/ppermute | solution.py:61
  48.3 2.3 %shard_map.94 = (bf16[3,128,512]{2,1,0:T(8,128)(2,1)S(1)}, bf16[3,128,512]{2,1,0:T(8,128)(2,1)}, bf16[3,128,512]{2,1,0:T(8,128)(2,1)}, bf16[3,128,512]{2,1,0:T(8,128)(2,1)}) custom-call(s32[2]{0:T(128)S(1)} %pad_add_fusion.where, bf16[512,512]{1,0:T(8,128)(2,1)S(1)} %copy-done.1, bf16[512,256]{1,0:T(8,128)(2,1)S(1)} %copy-done.5, ...), custom_call_target="tpu_custom_call" | custom-call | flops 1 | bytes 1 | tf_op jit(solution)/shard_map/pallas_call | solution.py:19
  51.4 5.0 %collective-permute-start.11 = (bf16[3,8,128,128]{3,2,1,0:T(8,128)(2,1)}, bf16[3,8,128,128]{3,2,1,0:T(8,128)(2,1)S(1)}, u32[]{:S(2)}, u32[]{:S(2)}) collective-permute-start(bf16[3,8,128,128]{3,2,1,0:T(8,128)(2,1)} %collective-permute-done.4.there), channel_id=1, source_target_pairs={{0,4},{4,0},{8,12},{12,8},{16,20},{20,16},{24,28},{28,24},{1,5},{5... | collective-permute-start | bytes 2359304 | tf_op jit(solution)/shard_map/ppermute | solution.py:47
  56.5 1.9 %collective-permute-start.7 = (bf16[3,128,512]{2,1,0:T(8,128)(2,1)}, bf16[3,128,512]{2,1,0:T(8,128)(2,1)}, u32[]{:S(2)}, u32[]{:S(2)}) collective-permute-start(bf16[3,128,512]{2,1,0:T(8,128)(2,1)} %get-tuple-element.74), channel_id=1, source_target_pairs={{0,1},{1,0},{2,3},{3,2},{4,5},{5,4},{6,7},{7,6},{8,9},{9,8},{10,11... | collective-permute-start | bytes 1179656 | tf_op jit(solution)/shard_map/ppermute | solution.py:47
  58.4 1.5 %collective-permute-start.8 = (bf16[3,128,512]{2,1,0:T(8,128)(2,1)}, bf16[3,128,512]{2,1,0:T(8,128)(2,1)}, u32[]{:S(2)}, u32[]{:S(2)}) collective-permute-start(bf16[3,128,512]{2,1,0:T(8,128)(2,1)} %get-tuple-element.75), channel_id=1, source_target_pairs={{0,2},{1,3},{2,0},{3,1},{4,6},{5,7},{6,4},{7,5},{8,10},{9,11},{10,... | collective-permute-start | bytes 1179656 | tf_op jit(solution)/shard_map/ppermute | solution.py:47
  60.0 4.1 %all-to-all-done.1.ps = bf16[4,4,128,512]{3,2,1,0:T(8,128)(2,1)S(1)} async-done(((bf16[4,4,128,512]{3,2,1,0:T(8,128)(2,1)}), bf16[4,4,128,512]{3,2,1,0:T(8,128)(2,1)S(1)}, u32[]{:S(2)}, u32[]{:S(2)}) %all-to-all-start.1) | async-done | bytes 2097184 | tf_op jit(solution)/shard_map/all_to_all | solution.py:55
  65.4 4.6 %shard_map.95.chaos.refs_4_ = bf16[2048,2048]{1,0:T(8,128)(2,1)S(1)} custom-call(s32[2]{0:T(128)S(1)} %pad_add_fusion.where, s32[16,8]{1,0:T(8,128)S(1)} %copy.12.targets, s32[16]{0:T(128)S(1)} %copy-done.14, bf16[32,128,128]{2,1,0:T(8,128)(2,1)S(1)} %bitcast.8, bf16[3,8,128,128]{3,2,1,0:T(8,128)(2,1)} %fusion.here, ...), custom_call_target="tpu_custom_call" | custom-call | flops 1 | bytes 1 | tf_op jit(solution)/shard_map/pallas_call | solution.py:19
  70.0 3.4 %copy-done = bf16[2048,2048]{1,0:T(8,128)(2,1)S(1)} copy-done((bf16[2048,2048]{1,0:T(8,128)(2,1)S(1)}, bf16[2048,2048]{1,0:T(8,128)(2,1)}, u32[]{:S(2)}) %copy-start) | copy-done | bytes 8388632
  73.4 6.4 %shard_map.96 = (f32[4,128,512]{2,1,0:T(8,128)S(1)}, f32[4,128,512]{2,1,0:T(8,128)S(1)}, f32[4,128,512]{2,1,0:T(8,128)S(1)}, bf16[2,128,512]{2,1,0:T(8,128)(2,1)...) custom-call(s32[2]{0:T(128)S(1)} %pad_add_fusion.where, ...), custom_call_target="tpu_custom_call" | custom-call | flops 1 | bytes 1 | tf_op jit(solution)/shard_map/pallas_call | solution.py:19
  79.8 1.6 %collective-permute-start.12 = (bf16[2,128,512]{2,1,0:T(8,128)(2,1)S(1)}, bf16[2,128,512]{2,1,0:T(8,128)(2,1)S(1)}, u32[]{:S(2)}, u32[]{:S(2)}) collective-permute-start(bf16[2,128,512]{2,1,0:T(8,128)(2,1)S(1)} %get-tuple-element.91), channel_id=1, source_target_pairs={{0,1},{1,0},{2,3},{3,2},{4,5},{5,4},{6,7},{7,6},{8,9},{9,8},{10,11... | collective-permute-start | bytes 786440 | tf_op jit(solution)/shard_map/ppermute | solution.py:47
  81.5 1.9 %collective-permute-start.14 = (bf16[2,128,512]{2,1,0:T(8,128)(2,1)S(1)}, bf16[2,128,512]{2,1,0:T(8,128)(2,1)S(1)}, u32[]{:S(2)}, u32[]{:S(2)}) collective-permute-start(bf16[2,128,512]{2,1,0:T(8,128)(2,1)S(1)} %get-tuple-element.93), channel_id=1, source_target_pairs={{0,3},{1,2},{2,1},{3,0},{4,7},{5,6},{6,5},{7,4},{8,11},{9,10},{10,... | collective-permute-start | bytes 786440 | tf_op jit(solution)/shard_map/ppermute | solution.py:47
  83.4 12.7 %shard_map.97 = (bf16[2,128,512]{2,1,0:T(8,128)(2,1)S(1)}, bf16[2,128,512]{2,1,0:T(8,128)(2,1)S(1)}, bf16[2,128,512]{2,1,0:T(8,128)(2,1)S(1)}, bf16[2,128,512]{2,1,0:T(8,128)(2,1)S(1)}, f32[32,8,128]{2,1,0:T(8,128)S(1)}) custom-call(s32[2]{0:T(128)S(1)} %pad_add_fusion.where, bf16[3,128,512]{2,1,0:T(8,128)(2,1)S(1)} %get-tuple-element.73.refs_0_, ...), custom_call_target="tpu_custom_call" | custom-call | flops 1 | bytes 1 | tf_op jit(solution)/shard_map/pallas_call | solution.py:19
  96.1 1.7 %collective-permute-start.15 = (bf16[2,128,512]{2,1,0:T(8,128)(2,1)S(1)}, bf16[2,128,512]{2,1,0:T(8,128)(2,1)S(1)}, u32[]{:S(2)}, u32[]{:S(2)}) collective-permute-start(bf16[2,128,512]{2,1,0:T(8,128)(2,1)S(1)} %get-tuple-element.100), channel_id=1, source_target_pairs={{0,1},{1,0},{2,3},{3,2},{4,5},{5,4},{6,7},{7,6},{8,9},{9,8},{10,11... | collective-permute-start | bytes 786440 | tf_op jit(solution)/shard_map/ppermute | solution.py:47
  97.9 1.8 %collective-permute-start.17 = (bf16[2,128,512]{2,1,0:T(8,128)(2,1)S(1)}, bf16[2,128,512]{2,1,0:T(8,128)(2,1)S(1)}, u32[]{:S(2)}, u32[]{:S(2)}) collective-permute-start(bf16[2,128,512]{2,1,0:T(8,128)(2,1)S(1)} %get-tuple-element.102), channel_id=1, source_target_pairs={{0,3},{1,2},{2,1},{3,0},{4,7},{5,6},{6,5},{7,4},{8,11},{9,10},{10,... | collective-permute-start | bytes 786440 | tf_op jit(solution)/shard_map/ppermute | solution.py:47
  99.6 12.6 %all_to_all.15.dots = f32[32,8,128]{2,1,0:T(8,128)S(1)} all-to-all(f32[32,8,128]{2,1,0:T(8,128)S(1)} %get-tuple-element.94), channel_id=1, replica_groups=mesh['space'=8,'mode'=4] {'space','mode'}, dimensions={0} | all-to-all | bytes 262144 | tf_op jit(solution)/shard_map/all_to_all | solution.py:393
  112.3 2.2 %shard_map.98 = f32[512,512]{1,0:T(8,128)} custom-call(s32[2]{0:T(128)S(1)} %pad_add_fusion.where, f32[512,512]{1,0:T(8,128)S(1)} %copy-done.3, f32[32,8,128]{2,1,0:T(8,128)S(1)} %all_to_all.15.dots, bf16[2,128,512]{2,1,0:T(8,128)(2,1)S(1)} %get-tuple-element.95.refs_0_, bf16[2,128,512]{2,1,0:T(8,128)(2,1)S(1)} %collective-permute-done.12.refs_1_, ...), custom_call_target="tpu_custom_call" | custom-call | flops 1 | bytes 1 | tf_op jit(solution)/shard_map/pallas_call | solution.py:19
  (64 shorter events, 8.9 us)
Async XLA Ops:
  1.0 6.6 %copy-start.16 = (s32[2,128]{1,0:T(2,128)S(1)}, s32[2,128]{1,0:T(2,128)}, u32[]{:S(2)}) copy-start(s32[2,128]{1,0:T(2,128)} %param.13) | copy-start | bytes 3076
  1.0 6.7 %copy-start.2 = (f32[512,512]{1,0:T(8,128)S(1)}, f32[512,512]{1,0:T(8,128)}, u32[]{:S(2)}) copy-start(f32[512,512]{1,0:T(8,128)} %u_ref.3) | copy-start | bytes 3145732
  2.4 24.8 %all-to-all-start = ((bf16[4,8,128,128]{3,2,1,0:T(8,128)(2,1)}), bf16[4,8,128,128]{3,2,1,0:T(8,128)(2,1)}, u32[]{:S(2)}, u32[]{:S(2)}) async-start(bf16[4,8,128,128]{3,2,1,0:T(8,128)(2,1)} %broadcast_in_dim.2), calls=%async_computation | async-start | bytes 2097152 | tf_op jit(solution)/shard_map/all_to_all | solution.py:55
  7.6 8.3 %copy-start.1 = (bf16[512,512]{1,0:T(8,128)(2,1)S(1)}, bf16[512,512]{1,0:T(8,128)(2,1)}, u32[]{:S(2)}) copy-start(bf16[512,512]{1,0:T(8,128)(2,1)} %diag.5) | copy-start | bytes 1572868
  7.6 8.3 %copy-start.5 = (bf16[512,256]{1,0:T(8,128)(2,1)S(1)}, bf16[512,256]{1,0:T(8,128)(2,1)}, u32[]{:S(2)}) copy-start(bf16[512,256]{1,0:T(8,128)(2,1)} %ghostly.5) | copy-start | bytes 786436
  7.6 8.3 %copy-start.9 = (f32[512,512]{1,0:T(8,128)S(1)}, f32[512,512]{1,0:T(8,128)}, u32[]{:S(2)}) copy-start(f32[512,512]{1,0:T(8,128)} %f_ref.1) | copy-start | bytes 3145732
  8.8 7.1 %copy-start.11 = (bf16[512,512]{1,0:T(8,128)(2,1)S(1)}, bf16[512,512]{1,0:T(8,128)(2,1)}, u32[]{:S(2)}) copy-start(bf16[512,512]{1,0:T(8,128)(2,1)} %copy-done.10) | copy-start | bytes 1572868
  8.8 5.2 %collective-permute-start = (bf16[128,512]{1,0:T(8,128)(2,1)S(1)}, bf16[128,512]{1,0:T(8,128)(2,1)S(1)}, u32[]{:S(2)}, u32[]{:S(2)}) collective-permute-start(bf16[128,512]{1,0:T(8,128)(2,1)S(1)} %get-tuple-element.55), channel_id=1, source_target_pairs={{0,4},{4,8},{8,12},{12,16},{16,20},{20,24},{24,28},{1,5},{5,9},{9,... | collective-permute-start | bytes 393224 | tf_op jit(solution)/shard_map/ppermute | solution.py:60
  10.5 5.4 %collective-permute-start.1 = (bf16[128,512]{1,0:T(8,128)(2,1)S(1)}, bf16[128,512]{1,0:T(8,128)(2,1)S(1)}, u32[]{:S(2)}, u32[]{:S(2)}) collective-permute-start(bf16[128,512]{1,0:T(8,128)(2,1)S(1)} %get-tuple-element.56), channel_id=1, source_target_pairs={{4,0},{8,4},{12,8},{16,12},{20,16},{24,20},{28,24},{5,1},{9,5},{13... | collective-permute-start | bytes 393224 | tf_op jit(solution)/shard_map/ppermute | solution.py:61
  20.0 9.5 %collective-permute-start.2 = (bf16[128,1024]{1,0:T(8,128)(2,1)}, bf16[128,1024]{1,0:T(8,128)(2,1)S(1)}, u32[]{:S(2)}, u32[]{:S(2)}) collective-permute-start(bf16[128,1024]{1,0:T(8,128)(2,1)} %get-tuple-element.59), channel_id=1, source_target_pairs={{0,4},{4,8},{8,12},{12,16},{16,20},{20,24},{24,28},{1,5},{5,9},{9,... | collective-permute-start | bytes 786440 | tf_op jit(solution)/shard_map/ppermute | solution.py:60
  25.9 3.6 %collective-permute-start.3 = (bf16[128,1024]{1,0:T(8,128)(2,1)S(1)}, bf16[128,1024]{1,0:T(8,128)(2,1)S(1)}, u32[]{:S(2)}, u32[]{:S(2)}) collective-permute-start(bf16[128,1024]{1,0:T(8,128)(2,1)S(1)} %get-tuple-element.60), channel_id=1, source_target_pairs={{4,0},{8,4},{12,8},{16,12},{20,16},{24,20},{28,24},{5,1},{9,5},{13... | collective-permute-start | bytes 786440 | tf_op jit(solution)/shard_map/ppermute | solution.py:61
  30.3 21.2 %collective-permute-start.4 = (bf16[3,8,128,128]{3,2,1,0:T(8,128)(2,1)}, bf16[3,8,128,128]{3,2,1,0:T(8,128)(2,1)}, u32[]{:S(2)}, u32[]{:S(2)}) collective-permute-start(bf16[3,8,128,128]{3,2,1,0:T(8,128)(2,1)} %fusion.here), channel_id=1, source_target_pairs={{0,8},{4,12},{8,0},{12,4},{16,24},{20,28},{24,16},{28,20},{1,9},{5... | collective-permute-start | bytes 2359304 | tf_op jit(solution)/shard_map/ppermute | solution.py:47
  34.1 30.1 %all-to-all-start.1 = ((bf16[4,4,128,512]{3,2,1,0:T(8,128)(2,1)}), bf16[4,4,128,512]{3,2,1,0:T(8,128)(2,1)S(1)}, u32[]{:S(2)}, u32[]{:S(2)}) async-start(bf16[4,4,128,512]{3,2,1,0:T(8,128)(2,1)} %copy-done.6), calls=%async_computation.1 | async-start | bytes 4194304 | tf_op jit(solution)/shard_map/all_to_all | solution.py:55
  40.3 19.6 %copy-start.15 = (s32[16,8]{0,1:T(8,128)S(1)}, s32[16,8]{0,1:T(8,128)}, u32[]{:S(2)}) copy-start(s32[16,8]{0,1:T(8,128)} %param.15) | copy-start | bytes 1540
  40.3 23.8 %copy-start.14 = (s32[16]{0:T(128)S(1)}, s32[16]{0:T(128)}, u32[]{:S(2)}) copy-start(s32[16]{0:T(128)} %counts.1) | copy-start | bytes 196
  41.8 4.6 %collective-permute-start.5 = (bf16[128,512]{1,0:T(8,128)(2,1)S(1)}, bf16[128,512]{1,0:T(8,128)(2,1)S(1)}, u32[]{:S(2)}, u32[]{:S(2)}) collective-permute-start(bf16[128,512]{1,0:T(8,128)(2,1)S(1)} %get-tuple-element.67), channel_id=1, source_target_pairs={{0,4},{4,8},{8,12},{12,16},{16,20},{20,24},{24,28},{1,5},{5,9},{9,... | collective-permute-start | bytes 393224 | tf_op jit(solution)/shard_map/ppermute | solution.py:60
  45.0 3.2 %collective-permute-start.6 = (bf16[128,512]{1,0:T(8,128)(2,1)S(1)}, bf16[128,512]{1,0:T(8,128)(2,1)S(1)}, u32[]{:S(2)}, u32[]{:S(2)}) collective-permute-start(bf16[128,512]{1,0:T(8,128)(2,1)S(1)} %get-tuple-element.68), channel_id=1, source_target_pairs={{4,0},{8,4},{12,8},{16,12},{20,16},{24,20},{28,24},{5,1},{9,5},{13... | collective-permute-start | bytes 393224 | tf_op jit(solution)/shard_map/ppermute | solution.py:61
  51.4 12.7 %collective-permute-start.11 = (bf16[3,8,128,128]{3,2,1,0:T(8,128)(2,1)}, bf16[3,8,128,128]{3,2,1,0:T(8,128)(2,1)S(1)}, u32[]{:S(2)}, u32[]{:S(2)}) collective-permute-start(bf16[3,8,128,128]{3,2,1,0:T(8,128)(2,1)} %collective-permute-done.4.there), channel_id=1, source_target_pairs={{0,4},{4,0},{8,12},{12,8},{16,20},{20,16},{24,28},{28,24},{1,5},{5... | collective-permute-start | bytes 2359304 | tf_op jit(solution)/shard_map/ppermute | solution.py:47
  56.4 7.7 %collective-permute-start.10 = (bf16[3,8,128,128]{3,2,1,0:T(8,128)(2,1)}, bf16[3,8,128,128]{3,2,1,0:T(8,128)(2,1)}, u32[]{:S(2)}, u32[]{:S(2)}) collective-permute-start(bf16[3,8,128,128]{3,2,1,0:T(8,128)(2,1)} %fusion.here), channel_id=1, source_target_pairs={{0,4},{4,0},{8,12},{12,8},{16,20},{20,16},{24,28},{28,24},{1,5},{5... | collective-permute-start | bytes 2359304 | tf_op jit(solution)/shard_map/ppermute | solution.py:47
  56.5 25.0 %collective-permute-start.7 = (bf16[3,128,512]{2,1,0:T(8,128)(2,1)}, bf16[3,128,512]{2,1,0:T(8,128)(2,1)}, u32[]{:S(2)}, u32[]{:S(2)}) collective-permute-start(bf16[3,128,512]{2,1,0:T(8,128)(2,1)} %get-tuple-element.74), channel_id=1, source_target_pairs={{0,1},{1,0},{2,3},{3,2},{4,5},{5,4},{6,7},{7,6},{8,9},{9,8},{10,11... | collective-permute-start | bytes 1179656 | tf_op jit(solution)/shard_map/ppermute | solution.py:47
  58.4 24.9 %collective-permute-start.8 = (bf16[3,128,512]{2,1,0:T(8,128)(2,1)}, bf16[3,128,512]{2,1,0:T(8,128)(2,1)}, u32[]{:S(2)}, u32[]{:S(2)}) collective-permute-start(bf16[3,128,512]{2,1,0:T(8,128)(2,1)} %get-tuple-element.75), channel_id=1, source_target_pairs={{0,2},{1,3},{2,0},{3,1},{4,6},{5,7},{6,4},{7,5},{8,10},{9,11},{10,... | collective-permute-start | bytes 1179656 | tf_op jit(solution)/shard_map/ppermute | solution.py:47
  59.9 23.5 %collective-permute-start.9 = (bf16[3,128,512]{2,1,0:T(8,128)(2,1)}, bf16[3,128,512]{2,1,0:T(8,128)(2,1)}, u32[]{:S(2)}, u32[]{:S(2)}) collective-permute-start(bf16[3,128,512]{2,1,0:T(8,128)(2,1)} %get-tuple-element.76), channel_id=1, source_target_pairs={{0,3},{1,2},{2,1},{3,0},{4,7},{5,6},{6,5},{7,4},{8,11},{9,10},{10,... | collective-permute-start | bytes 1179656 | tf_op jit(solution)/shard_map/ppermute | solution.py:47
  65.4 18.0 %slice-start = ((s8[8388608]{0:T(1024)(128)(4,1)}), s8[4194304]{0:T(1024)(128)(4,1)S(1)}, s32[]{:S(2)}) async-start(s8[8388608]{0:T(1024)(128)(4,1)} %bitcast.6), calls=%async_computation.3 | async-start | bytes 8388608
  70.0 3.4 %copy-start = (bf16[2048,2048]{1,0:T(8,128)(2,1)S(1)}, bf16[2048,2048]{1,0:T(8,128)(2,1)}, u32[]{:S(2)}) copy-start(bf16[2048,2048]{1,0:T(8,128)(2,1)} %refs_5_.1) | copy-start | bytes 25165828
  73.4 10.0 %slice-start.1 = ((s8[8388608]{0:T(1024)(128)(4,1)}), s8[4194304]{0:T(1024)(128)(4,1)S(1)}, s32[]{:S(2)}) async-start(s8[8388608]{0:T(1024)(128)(4,1)} %bitcast.6), calls=%async_computation.4 | async-start | bytes 8388608
  79.8 16.3 %collective-permute-start.12 = (bf16[2,128,512]{2,1,0:T(8,128)(2,1)S(1)}, bf16[2,128,512]{2,1,0:T(8,128)(2,1)S(1)}, u32[]{:S(2)}, u32[]{:S(2)}) collective-permute-start(bf16[2,128,512]{2,1,0:T(8,128)(2,1)S(1)} %get-tuple-element.91), channel_id=1, source_target_pairs={{0,1},{1,0},{2,3},{3,2},{4,5},{5,4},{6,7},{7,6},{8,9},{9,8},{10,11... | collective-permute-start | bytes 786440 | tf_op jit(solution)/shard_map/ppermute | solution.py:47
  81.4 14.7 %collective-permute-start.13 = (bf16[2,128,512]{2,1,0:T(8,128)(2,1)S(1)}, bf16[2,128,512]{2,1,0:T(8,128)(2,1)S(1)}, u32[]{:S(2)}, u32[]{:S(2)}) collective-permute-start(bf16[2,128,512]{2,1,0:T(8,128)(2,1)S(1)} %get-tuple-element.92), channel_id=1, source_target_pairs={{0,2},{1,3},{2,0},{3,1},{4,6},{5,7},{6,4},{7,5},{8,10},{9,11},{10,... | collective-permute-start | bytes 786440 | tf_op jit(solution)/shard_map/ppermute | solution.py:47
  81.5 14.6 %collective-permute-start.14 = (bf16[2,128,512]{2,1,0:T(8,128)(2,1)S(1)}, bf16[2,128,512]{2,1,0:T(8,128)(2,1)S(1)}, u32[]{:S(2)}, u32[]{:S(2)}) collective-permute-start(bf16[2,128,512]{2,1,0:T(8,128)(2,1)S(1)} %get-tuple-element.93), channel_id=1, source_target_pairs={{0,3},{1,2},{2,1},{3,0},{4,7},{5,6},{6,5},{7,4},{8,11},{9,10},{10,... | collective-permute-start | bytes 786440 | tf_op jit(solution)/shard_map/ppermute | solution.py:47
  83.4 28.9 %copy-start.3 = (f32[512,512]{1,0:T(8,128)S(1)}, f32[512,512]{1,0:T(8,128)}, u32[]{:S(2)}) copy-start(f32[512,512]{1,0:T(8,128)} %u_ref.3) | copy-start | bytes 3145732
  96.1 16.1 %collective-permute-start.15 = (bf16[2,128,512]{2,1,0:T(8,128)(2,1)S(1)}, bf16[2,128,512]{2,1,0:T(8,128)(2,1)S(1)}, u32[]{:S(2)}, u32[]{:S(2)}) collective-permute-start(bf16[2,128,512]{2,1,0:T(8,128)(2,1)S(1)} %get-tuple-element.100), channel_id=1, source_target_pairs={{0,1},{1,0},{2,3},{3,2},{4,5},{5,4},{6,7},{7,6},{8,9},{9,8},{10,11... | collective-permute-start | bytes 786440 | tf_op jit(solution)/shard_map/ppermute | solution.py:47
  97.8 14.5 %collective-permute-start.16 = (bf16[2,128,512]{2,1,0:T(8,128)(2,1)S(1)}, bf16[2,128,512]{2,1,0:T(8,128)(2,1)S(1)}, u32[]{:S(2)}, u32[]{:S(2)}) collective-permute-start(bf16[2,128,512]{2,1,0:T(8,128)(2,1)S(1)} %get-tuple-element.101), channel_id=1, source_target_pairs={{0,2},{1,3},{2,0},{3,1},{4,6},{5,7},{6,4},{7,5},{8,10},{9,11},{10,... | collective-permute-start | bytes 786440 | tf_op jit(solution)/shard_map/ppermute | solution.py:47
  97.9 14.4 %collective-permute-start.17 = (bf16[2,128,512]{2,1,0:T(8,128)(2,1)S(1)}, bf16[2,128,512]{2,1,0:T(8,128)(2,1)S(1)}, u32[]{:S(2)}, u32[]{:S(2)}) collective-permute-start(bf16[2,128,512]{2,1,0:T(8,128)(2,1)S(1)} %get-tuple-element.102), channel_id=1, source_target_pairs={{0,3},{1,2},{2,1},{3,0},{4,7},{5,6},{6,5},{7,4},{8,11},{9,10},{10,... | collective-permute-start | bytes 786440 | tf_op jit(solution)/shard_map/ppermute | solution.py:47
  (7 other events, 7.2 us)

commit v5 on v4

--- a/solution.py
+++ b/solution.py
@@ -206,6 +206,13 @@
     by_table(n, me, lambda k: quick[k], chaos, coupled)
 
 
+def table_and_a(
+    n, slots, where, targets, counts, own, here, beside, there, across, ps, inverse, chaos, *refs
+):
+    table_body(n, slots, where, targets, counts, own, here, beside, there, across, chaos)
+    stage_a(n, where, ps, chaos, inverse, *refs)
+
+
 def stage_b(n, where, *refs):
     qs = refs[:n]
     chaos, inverse, w0, c1, ca0 = refs[n : n + 5]
@@ -251,12 +258,13 @@
     by_table(n, me, lambda k: outs[k][0], chaos, last_in)
 
     def second(g, value):
+        value = value[:rows]
         outs[g][1] = value.astype(BF16)
         sums[3] += jnp.sum(w0[g] * value)
         sums[4] += jnp.sum(v1[g] * value)
         sums[5] += jnp.sum(value * value)
 
-    by_inverse(n, me, lambda k: more[k, :rows], inverse, second)
+    by_inverse(n, me, lambda k: more[k], inverse, second)
     lanes_of(dots, sums, 0)
 
 
@@ -364,19 +372,13 @@
     qs = trade(qs)
     beside, across = flip_permute(here, "space", 1), flip_permute(there, "space", 1)
     across, ps = lax.optimization_barrier((across, ps))
-    (chaos,) = call(
-        functools.partial(table_body, n, slots),
-        [square],
-        [where, chaos_targets, chaos_count, own, here, beside, there, across],
-        3,
-    )
     slab = shaped((n, rows, width), F32)
     double = shaped((n, 2 * rows, width))
-    w0, c1, ca0, *ws = call(
-        functools.partial(stage_a, n),
-        [slab, slab, slab] + sent(2),
-        [where, ps, chaos, mean_inverse],
-        1,
+    chaos, w0, c1, ca0, *ws = call(
+        functools.partial(table_and_a, n, slots),
+        [square, slab, slab, slab] + sent(2),
+        [where, chaos_targets, chaos_count, own, here, beside, there, across, ps, mean_inverse],
+        3,
         [double, shaped((n, rows, width))],
     )
     ws = trade(ws)

time: 115 us -> 114 us (level)
    pallas_call x8 -> x7, Pallas kernels: 31.7 us -> 30.8 us  [call(): pl.pallas_call(body, out_shape=outs, in_specs=[SMEM] * scalars + [VMEM] *...]
    unnamed x40 -> x38, local copies, waits for them, and re-layouts: 13 us -> 13 us
  transfers between devices with their start and end apart: 20 -> 20, of which waited for: 4 -> 4; matrix products, arithmetic and copies ran while one was open for 4% -> 4% of each run, Pallas kernels for 26% -> 25%
where the time goes in v5:
time: 114 us
  starting transfers between devices  43.2 us (38%)
  Pallas kernels  30.8 us (27%)
  local copies, waits for them, and re-layouts  15.4 us (14%)
  blocking collectives  12.6 us (11%)
  waiting for transfers between devices  8.75 us (8%)
  other arithmetic  2.48 us (2%)
    pallas_call x7, Pallas kernels, call(): pl.pallas_call(body, out_shape=outs, in_specs=[SMEM] * scalars + [VMEM] *...  30.8 us
    ppermute x12, starting transfers between devices, flip_permute(): lax.ppermute(x, axis, [(i, i ^ bit) for i in range(lax.axis_size(axis))])  19.4 us
    unnamed x38, local copies, waits for them, and re-layouts  13 us
    all_to_all x1, blocking collectives, shards(): lax.all_to_all(dots, ('space', 'mode'), split_axis=0, concat_axis=0, tile...  12.6 us
    ppermute x3, starting transfers between devices, halo(): below = lax.ppermute(upper, 'space', [(i, i + 1) for i in range(count - 1)])  10.7 us
    all_to_all x2, starting transfers between devices, swap(): return lax.all_to_all(x, 'mode', split_axis=0, concat_axis=0, tiled=True)  9.28 us
    all_to_all x2, waiting for transfers between devices, swap(): return lax.all_to_all(x, 'mode', split_axis=0, concat_axis=0, tiled=True)  4.1 us
    ppermute x3, starting transfers between devices, halo(): above = lax.ppermute(lower, 'space', [(i + 1, i) for i in range(count - 1)])  3.88 us
  transfers between devices with their start and end apart: 20, of which 4 were waited for; matrix products, arithmetic and copies ran while one was open for 4% of the time, Pallas kernels for 25%

profile of v5, /device:TPU:0, one launch (start us, length us, event | category | flops | bytes accessed | tf_op | source)
XLA Modules:
  0.0 113.6 jit_solution(9158679525508650504)
XLA Ops:
  1.2 1.3 %broadcast_in_dim.2 = bf16[4,8,128,128]{3,2,1,0:T(8,128)(2,1)} broadcast(bf16[8,128,128]{2,1,0:T(8,128)(2,1)S(1)} %copy.10), dimensions={1,2,3} | broadcast | bytes 1310720 | tf_op jit(solution)/shard_map/broadcast_in_dim | solution.py:344
  2.4 5.2 %all-to-all-start = ((bf16[4,8,128,128]{3,2,1,0:T(8,128)(2,1)}), bf16[4,8,128,128]{3,2,1,0:T(8,128)(2,1)}, u32[]{:S(2)}, u32[]{:S(2)}) async-start(bf16[4,8,128,128]{3,2,1,0:T(8,128)(2,1)} %broadcast_in_dim.2), calls=%async_computation | async-start | bytes 2097152 | tf_op jit(solution)/shard_map/all_to_all | solution.py:55
  8.8 1.6 %collective-permute-start = (bf16[128,512]{1,0:T(8,128)(2,1)S(1)}, bf16[128,512]{1,0:T(8,128)(2,1)S(1)}, u32[]{:S(2)}, u32[]{:S(2)}) collective-permute-start(bf16[128,512]{1,0:T(8,128)(2,1)S(1)} %get-tuple-element.56), channel_id=1, source_target_pairs={{0,4},{4,8},{8,12},{12,16},{16,20},{20,24},{24,28},{1,5},{5,9},{9,... | collective-permute-start | bytes 393224 | tf_op jit(solution)/shard_map/ppermute | solution.py:60
  10.5 1.3 %collective-permute-start.1 = (bf16[128,512]{1,0:T(8,128)(2,1)S(1)}, bf16[128,512]{1,0:T(8,128)(2,1)S(1)}, u32[]{:S(2)}, u32[]{:S(2)}) collective-permute-start(bf16[128,512]{1,0:T(8,128)(2,1)S(1)} %get-tuple-element.57), channel_id=1, source_target_pairs={{4,0},{8,4},{12,8},{16,12},{20,16},{24,20},{28,24},{5,1},{9,5},{13... | collective-permute-start | bytes 393224 | tf_op jit(solution)/shard_map/ppermute | solution.py:61
  11.8 2.3 %copy.11 = bf16[32,128,128]{1,2,0:T(8,128)(2,1)} copy(bf16[32,128,128]{2,1,0:T(8,128)(2,1)} %param.14) | data formatting | bytes 2097152 | tf_op args[5]
  14.1 1.8 %collective-permute-done.1.above = bf16[128,512]{1,0:T(8,128)(2,1)S(1)} collective-permute-done((bf16[128,512]{1,0:T(8,128)(2,1)S(1)}, bf16[128,512]{1,0:T(8,128)(2,1)S(1)}, u32[]{:S(2)}, u32[]{:S(2)}) %collective-permute-start.1) | collective-permute-done | bytes 131104 | tf_op jit(solution)/shard_map/ppermute | solution.py:61
  15.9 1.9 %shard_map.92 = (bf16[512,1024]{1,0:T(8,128)(2,1)S(1)}, bf16[128,1024]{1,0:T(8,128)(2,1)S(1)}, bf16[128,1024]{1,0:T(8,128)(2,1)}, bf16[4,4,128,512]{3,2,1,0:T(8,128)(2,1)S(1)}) custom-call(bf16[512,512]{1,0:T(8,128)(2,1)S(1)} %copy-done.2, bf16[512,256]{1,0:T(8,128)(2,1)S(1)} %copy-done.6, f32[512,512]{1,0:T(8,128)S(1)} %copy-done.10, ...), custom_call_target="tpu_custom_call" | custom-call | flops 1 | bytes 1 | tf_op jit(solution)/shard_map/pallas_call | solution.py:19
  17.8 1.3 %copy-done.7 = bf16[4,4,128,512]{3,2,1,0:T(8,128)(2,1)} copy-done((bf16[4,4,128,512]{3,2,1,0:T(8,128)(2,1)}, bf16[4,4,128,512]{3,2,1,0:T(8,128)(2,1)S(1)}, u32[]{:S(2)}) %copy-start.7) | copy-done | bytes 2097176
  20.1 5.8 %collective-permute-start.2 = (bf16[128,1024]{1,0:T(8,128)(2,1)}, bf16[128,1024]{1,0:T(8,128)(2,1)S(1)}, u32[]{:S(2)}, u32[]{:S(2)}) collective-permute-start(bf16[128,1024]{1,0:T(8,128)(2,1)} %get-tuple-element.60), channel_id=1, source_target_pairs={{0,4},{4,8},{8,12},{12,16},{16,20},{20,24},{24,28},{1,5},{5,9},{9,... | collective-permute-start | bytes 786440 | tf_op jit(solution)/shard_map/ppermute | solution.py:60
  25.9 1.3 %collective-permute-start.3 = (bf16[128,1024]{1,0:T(8,128)(2,1)S(1)}, bf16[128,1024]{1,0:T(8,128)(2,1)S(1)}, u32[]{:S(2)}, u32[]{:S(2)}) collective-permute-start(bf16[128,1024]{1,0:T(8,128)(2,1)S(1)} %get-tuple-element.61), channel_id=1, source_target_pairs={{4,0},{8,4},{12,8},{16,12},{20,16},{24,20},{28,24},{5,1},{9,5},{13... | collective-permute-start | bytes 786440 | tf_op jit(solution)/shard_map/ppermute | solution.py:61
  27.2 2.3 %fusion.here = bf16[3,8,128,128]{3,2,1,0:T(8,128)(2,1)} fusion(s32[]{:T(128)S(6)} %select_n.15, bf16[4,8,128,128]{3,2,1,0:T(8,128)(2,1)} %all-to-all-done), kind=kLoop, calls=%fused_computation.2 | loop fusion | flops 393216 | bytes 1835012 | tf_op jit(solution)/shard_map/concatenate | solution.py:345
  30.3 3.8 %collective-permute-start.4 = (bf16[3,8,128,128]{3,2,1,0:T(8,128)(2,1)}, bf16[3,8,128,128]{3,2,1,0:T(8,128)(2,1)}, u32[]{:S(2)}, u32[]{:S(2)}) collective-permute-start(bf16[3,8,128,128]{3,2,1,0:T(8,128)(2,1)} %fusion.here), channel_id=1, source_target_pairs={{0,8},{4,12},{8,0},{12,4},{16,24},{20,28},{24,16},{28,20},{1,9},{5... | collective-permute-start | bytes 2359304 | tf_op jit(solution)/shard_map/ppermute | solution.py:47
  34.1 4.1 %all-to-all-start.1 = ((bf16[4,4,128,512]{3,2,1,0:T(8,128)(2,1)}), bf16[4,4,128,512]{3,2,1,0:T(8,128)(2,1)S(1)}, u32[]{:S(2)}, u32[]{:S(2)}) async-start(bf16[4,4,128,512]{3,2,1,0:T(8,128)(2,1)} %copy-done.7), calls=%async_computation.1 | async-start | bytes 4194304 | tf_op jit(solution)/shard_map/all_to_all | solution.py:55
  38.2 1.2 %copy-done.9 = bf16[512,1024]{1,0:T(8,128)(2,1)S(1)} copy-done((bf16[512,1024]{1,0:T(8,128)(2,1)S(1)}, bf16[512,1024]{1,0:T(8,128)(2,1)}, u32[]{:S(2)}) %copy-start.9) | copy-done | bytes 1048600
  40.4 1.4 %shard_map.93 = (bf16[512,1024]{1,0:T(8,128)(2,1)S(1)}, bf16[512,512]{1,0:T(8,128)(2,1)S(1)}, bf16[128,512]{1,0:T(8,128)(2,1)S(1)}, bf16[128,512]{1,0:T(8,128)(2,1)S(1)}) custom-call(bf16[512,512]{1,0:T(8,128)(2,1)S(1)} %copy-done.2, bf16[512,256]{1,0:T(8,128)(2,1)S(1)} %copy-done.6, bf16[512,1024]{1,0:T(8,128)(2,1)S(1)} %copy-done.9, ...), custom_call_target="tpu_custom_call" | custom-call | flops 1 | bytes 1 | tf_op jit(solution)/shard_map/pallas_call | solution.py:19
  41.8 3.2 %collective-permute-start.5 = (bf16[128,512]{1,0:T(8,128)(2,1)S(1)}, bf16[128,512]{1,0:T(8,128)(2,1)S(1)}, u32[]{:S(2)}, u32[]{:S(2)}) collective-permute-start(bf16[128,512]{1,0:T(8,128)(2,1)S(1)} %get-tuple-element.68), channel_id=1, source_target_pairs={{0,4},{4,8},{8,12},{12,16},{16,20},{20,24},{24,28},{1,5},{5,9},{9,... | collective-permute-start | bytes 393224 | tf_op jit(solution)/shard_map/ppermute | solution.py:60
  45.0 1.3 %collective-permute-start.6 = (bf16[128,512]{1,0:T(8,128)(2,1)S(1)}, bf16[128,512]{1,0:T(8,128)(2,1)S(1)}, u32[]{:S(2)}, u32[]{:S(2)}) collective-permute-start(bf16[128,512]{1,0:T(8,128)(2,1)S(1)} %get-tuple-element.69), channel_id=1, source_target_pairs={{4,0},{8,4},{12,8},{16,12},{20,16},{24,20},{28,24},{5,1},{9,5},{13... | collective-permute-start | bytes 393224 | tf_op jit(solution)/shard_map/ppermute | solution.py:61
  46.4 1.9 %collective-permute-done.6.above = bf16[128,512]{1,0:T(8,128)(2,1)S(1)} collective-permute-done((bf16[128,512]{1,0:T(8,128)(2,1)S(1)}, bf16[128,512]{1,0:T(8,128)(2,1)S(1)}, u32[]{:S(2)}, u32[]{:S(2)}) %collective-permute-start.6) | collective-permute-done | bytes 131104 | tf_op jit(solution)/shard_map/ppermute | solution.py:61
  48.3 2.3 %shard_map.94 = (bf16[3,128,512]{2,1,0:T(8,128)(2,1)S(1)}, bf16[3,128,512]{2,1,0:T(8,128)(2,1)}, bf16[3,128,512]{2,1,0:T(8,128)(2,1)}, bf16[3,128,512]{2,1,0:T(8,128)(2,1)}) custom-call(s32[2]{0:T(128)S(1)} %pad_add_fusion.where, bf16[512,512]{1,0:T(8,128)(2,1)S(1)} %copy-done.2, bf16[512,256]{1,0:T(8,128)(2,1)S(1)} %copy-done.6, ...), custom_call_target="tpu_custom_call" | custom-call | flops 1 | bytes 1 | tf_op jit(solution)/shard_map/pallas_call | solution.py:19
  51.5 5.0 %collective-permute-start.11 = (bf16[3,8,128,128]{3,2,1,0:T(8,128)(2,1)}, bf16[3,8,128,128]{3,2,1,0:T(8,128)(2,1)S(1)}, u32[]{:S(2)}, u32[]{:S(2)}) collective-permute-start(bf16[3,8,128,128]{3,2,1,0:T(8,128)(2,1)} %collective-permute-done.4.there), channel_id=1, source_target_pairs={{0,4},{4,0},{8,12},{12,8},{16,20},{20,16},{24,28},{28,24},{1,5},{5... | collective-permute-start | bytes 2359304 | tf_op jit(solution)/shard_map/ppermute | solution.py:47
  56.5 1.9 %collective-permute-start.7 = (bf16[3,128,512]{2,1,0:T(8,128)(2,1)}, bf16[3,128,512]{2,1,0:T(8,128)(2,1)}, u32[]{:S(2)}, u32[]{:S(2)}) collective-permute-start(bf16[3,128,512]{2,1,0:T(8,128)(2,1)} %get-tuple-element.75), channel_id=1, source_target_pairs={{0,1},{1,0},{2,3},{3,2},{4,5},{5,4},{6,7},{7,6},{8,9},{9,8},{10,11... | collective-permute-start | bytes 1179656 | tf_op jit(solution)/shard_map/ppermute | solution.py:47
  58.4 1.5 %collective-permute-start.8 = (bf16[3,128,512]{2,1,0:T(8,128)(2,1)}, bf16[3,128,512]{2,1,0:T(8,128)(2,1)}, u32[]{:S(2)}, u32[]{:S(2)}) collective-permute-start(bf16[3,128,512]{2,1,0:T(8,128)(2,1)} %get-tuple-element.76), channel_id=1, source_target_pairs={{0,2},{1,3},{2,0},{3,1},{4,6},{5,7},{6,4},{7,5},{8,10},{9,11},{10,... | collective-permute-start | bytes 1179656 | tf_op jit(solution)/shard_map/ppermute | solution.py:47
  60.0 4.1 %all-to-all-done.1.ps = bf16[4,4,128,512]{3,2,1,0:T(8,128)(2,1)S(1)} async-done(((bf16[4,4,128,512]{3,2,1,0:T(8,128)(2,1)}), bf16[4,4,128,512]{3,2,1,0:T(8,128)(2,1)S(1)}, u32[]{:S(2)}, u32[]{:S(2)}) %all-to-all-start.1) | async-done | bytes 2097184 | tf_op jit(solution)/shard_map/all_to_all | solution.py:55
  64.2 3.4 %copy-done = bf16[2048,2048]{1,0:T(8,128)(2,1)S(1)} copy-done((bf16[2048,2048]{1,0:T(8,128)(2,1)S(1)}, bf16[2048,2048]{1,0:T(8,128)(2,1)}, u32[]{:S(2)}) %copy-start) | copy-done | bytes 8388632
  68.8 10.6 %shard_map.95 = (bf16[2048,2048]{1,0:T(8,128)(2,1)S(1)}, f32[4,128,512]{2,1,0:T(8,128)S(1)}, f32[4,128,512]{2,1,0:T(8,128)S(1)}, f32[4,128,512]{2,1,0:T(8,128)S(...) custom-call(s32[2]{0:T(128)S(1)} %pad_add_fusion.where, ...), custom_call_target="tpu_custom_call" | custom-call | flops 1 | bytes 1 | tf_op jit(solution)/shard_map/pallas_call | solution.py:19
  79.4 1.6 %collective-permute-start.12 = (bf16[2,128,512]{2,1,0:T(8,128)(2,1)S(1)}, bf16[2,128,512]{2,1,0:T(8,128)(2,1)S(1)}, u32[]{:S(2)}, u32[]{:S(2)}) collective-permute-start(bf16[2,128,512]{2,1,0:T(8,128)(2,1)S(1)} %get-tuple-element.93), channel_id=1, source_target_pairs={{0,1},{1,0},{2,3},{3,2},{4,5},{5,4},{6,7},{7,6},{8,9},{9,8},{10,11... | collective-permute-start | bytes 786440 | tf_op jit(solution)/shard_map/ppermute | solution.py:47
  81.1 1.8 %collective-permute-start.14 = (bf16[2,128,512]{2,1,0:T(8,128)(2,1)S(1)}, bf16[2,128,512]{2,1,0:T(8,128)(2,1)S(1)}, u32[]{:S(2)}, u32[]{:S(2)}) collective-permute-start(bf16[2,128,512]{2,1,0:T(8,128)(2,1)S(1)} %get-tuple-element.95), channel_id=1, source_target_pairs={{0,3},{1,2},{2,1},{3,0},{4,7},{5,6},{6,5},{7,4},{8,11},{9,10},{10,... | collective-permute-start | bytes 786440 | tf_op jit(solution)/shard_map/ppermute | solution.py:47
  83.0 12.1 %shard_map.96 = (bf16[2,128,512]{2,1,0:T(8,128)(2,1)S(1)}, bf16[2,128,512]{2,1,0:T(8,128)(2,1)S(1)}, bf16[2,128,512]{2,1,0:T(8,128)(2,1)S(1)}, bf16[2,128,512]{2,1,0:T(8,128)(2,1)S(1)}, f32[32,8,128]{2,1,0:T(8,128)S(1)}) custom-call(s32[2]{0:T(128)S(1)} %pad_add_fusion.where, bf16[3,128,512]{2,1,0:T(8,128)(2,1)S(1)} %get-tuple-element.74.refs_0_, ...), custom_call_target="tpu_custom_call" | custom-call | flops 1 | bytes 1 | tf_op jit(solution)/shard_map/pallas_call | solution.py:19
  95.1 1.7 %collective-permute-start.15 = (bf16[2,128,512]{2,1,0:T(8,128)(2,1)S(1)}, bf16[2,128,512]{2,1,0:T(8,128)(2,1)S(1)}, u32[]{:S(2)}, u32[]{:S(2)}) collective-permute-start(bf16[2,128,512]{2,1,0:T(8,128)(2,1)S(1)} %get-tuple-element.102), channel_id=1, source_target_pairs={{0,1},{1,0},{2,3},{3,2},{4,5},{5,4},{6,7},{7,6},{8,9},{9,8},{10,11... | collective-permute-start | bytes 786440 | tf_op jit(solution)/shard_map/ppermute | solution.py:47
  97.4 1.3 %collective-permute-start.17 = (bf16[2,128,512]{2,1,0:T(8,128)(2,1)S(1)}, bf16[2,128,512]{2,1,0:T(8,128)(2,1)S(1)}, u32[]{:S(2)}, u32[]{:S(2)}) collective-permute-start(bf16[2,128,512]{2,1,0:T(8,128)(2,1)S(1)} %get-tuple-element.104), channel_id=1, source_target_pairs={{0,3},{1,2},{2,1},{3,0},{4,7},{5,6},{6,5},{7,4},{8,11},{9,10},{10,... | collective-permute-start | bytes 786440 | tf_op jit(solution)/shard_map/ppermute | solution.py:47
  98.7 12.6 %all_to_all.15.dots = f32[32,8,128]{2,1,0:T(8,128)S(1)} all-to-all(f32[32,8,128]{2,1,0:T(8,128)S(1)} %get-tuple-element.96), channel_id=1, replica_groups=mesh['space'=8,'mode'=4] {'space','mode'}, dimensions={0} | all-to-all | bytes 262144 | tf_op jit(solution)/shard_map/all_to_all | solution.py:395
  111.3 2.2 %shard_map.97 = f32[512,512]{1,0:T(8,128)} custom-call(s32[2]{0:T(128)S(1)} %pad_add_fusion.where, f32[512,512]{1,0:T(8,128)S(1)} %copy-done.4, f32[32,8,128]{2,1,0:T(8,128)S(1)} %all_to_all.15.dots, bf16[2,128,512]{2,1,0:T(8,128)(2,1)S(1)} %get-tuple-element.97.refs_0_, bf16[2,128,512]{2,1,0:T(8,128)(2,1)S(1)} %collective-permute-done.12.refs_1_, ...), custom_call_target="tpu_custom_call" | custom-call | flops 1 | bytes 1 | tf_op jit(solution)/shard_map/pallas_call | solution.py:19
  (60 shorter events, 8.2 us)
Async XLA Ops:
  1.0 6.6 %copy-start.17 = (s32[2,128]{1,0:T(2,128)S(1)}, s32[2,128]{1,0:T(2,128)}, u32[]{:S(2)}) copy-start(s32[2,128]{1,0:T(2,128)} %param.13) | copy-start | bytes 3076
  1.0 6.8 %copy-start.3 = (f32[512,512]{1,0:T(8,128)S(1)}, f32[512,512]{1,0:T(8,128)}, u32[]{:S(2)}) copy-start(f32[512,512]{1,0:T(8,128)} %u_ref.3) | copy-start | bytes 3145732
  2.4 24.8 %all-to-all-start = ((bf16[4,8,128,128]{3,2,1,0:T(8,128)(2,1)}), bf16[4,8,128,128]{3,2,1,0:T(8,128)(2,1)}, u32[]{:S(2)}, u32[]{:S(2)}) async-start(bf16[4,8,128,128]{3,2,1,0:T(8,128)(2,1)} %broadcast_in_dim.2), calls=%async_computation | async-start | bytes 2097152 | tf_op jit(solution)/shard_map/all_to_all | solution.py:55
  7.6 8.3 %copy-start.2 = (bf16[512,512]{1,0:T(8,128)(2,1)S(1)}, bf16[512,512]{1,0:T(8,128)(2,1)}, u32[]{:S(2)}) copy-start(bf16[512,512]{1,0:T(8,128)(2,1)} %diag.5) | copy-start | bytes 1572868
  7.6 8.3 %copy-start.6 = (bf16[512,256]{1,0:T(8,128)(2,1)S(1)}, bf16[512,256]{1,0:T(8,128)(2,1)}, u32[]{:S(2)}) copy-start(bf16[512,256]{1,0:T(8,128)(2,1)} %ghostly.5) | copy-start | bytes 786436
  7.6 8.3 %copy-start.10 = (f32[512,512]{1,0:T(8,128)S(1)}, f32[512,512]{1,0:T(8,128)}, u32[]{:S(2)}) copy-start(f32[512,512]{1,0:T(8,128)} %f_ref.1) | copy-start | bytes 3145732
  8.8 7.1 %copy-start.12 = (bf16[512,512]{1,0:T(8,128)(2,1)S(1)}, bf16[512,512]{1,0:T(8,128)(2,1)}, u32[]{:S(2)}) copy-start(bf16[512,512]{1,0:T(8,128)(2,1)} %copy-done.11) | copy-start | bytes 1572868
  8.8 5.2 %collective-permute-start = (bf16[128,512]{1,0:T(8,128)(2,1)S(1)}, bf16[128,512]{1,0:T(8,128)(2,1)S(1)}, u32[]{:S(2)}, u32[]{:S(2)}) collective-permute-start(bf16[128,512]{1,0:T(8,128)(2,1)S(1)} %get-tuple-element.56), channel_id=1, source_target_pairs={{0,4},{4,8},{8,12},{12,16},{16,20},{20,24},{24,28},{1,5},{5,9},{9,... | collective-permute-start | bytes 393224 | tf_op jit(solution)/shard_map/ppermute | solution.py:60
  10.5 5.4 %collective-permute-start.1 = (bf16[128,512]{1,0:T(8,128)(2,1)S(1)}, bf16[128,512]{1,0:T(8,128)(2,1)S(1)}, u32[]{:S(2)}, u32[]{:S(2)}) collective-permute-start(bf16[128,512]{1,0:T(8,128)(2,1)S(1)} %get-tuple-element.57), channel_id=1, source_target_pairs={{4,0},{8,4},{12,8},{16,12},{20,16},{24,20},{28,24},{5,1},{9,5},{13... | collective-permute-start | bytes 393224 | tf_op jit(solution)/shard_map/ppermute | solution.py:61
  17.8 1.3 %copy-start.7 = (bf16[4,4,128,512]{3,2,1,0:T(8,128)(2,1)}, bf16[4,4,128,512]{3,2,1,0:T(8,128)(2,1)S(1)}, u32[]{:S(2)}) copy-start(bf16[4,4,128,512]{3,2,1,0:T(8,128)(2,1)S(1)} %get-tuple-element.80) | copy-start | bytes 6291460
  20.1 9.5 %collective-permute-start.2 = (bf16[128,1024]{1,0:T(8,128)(2,1)}, bf16[128,1024]{1,0:T(8,128)(2,1)S(1)}, u32[]{:S(2)}, u32[]{:S(2)}) collective-permute-start(bf16[128,1024]{1,0:T(8,128)(2,1)} %get-tuple-element.60), channel_id=1, source_target_pairs={{0,4},{4,8},{8,12},{12,16},{16,20},{20,24},{24,28},{1,5},{5,9},{9,... | collective-permute-start | bytes 786440 | tf_op jit(solution)/shard_map/ppermute | solution.py:60
  25.9 3.6 %collective-permute-start.3 = (bf16[128,1024]{1,0:T(8,128)(2,1)S(1)}, bf16[128,1024]{1,0:T(8,128)(2,1)S(1)}, u32[]{:S(2)}, u32[]{:S(2)}) collective-permute-start(bf16[128,1024]{1,0:T(8,128)(2,1)S(1)} %get-tuple-element.61), channel_id=1, source_target_pairs={{4,0},{8,4},{12,8},{16,12},{20,16},{24,20},{28,24},{5,1},{9,5},{13... | collective-permute-start | bytes 786440 | tf_op jit(solution)/shard_map/ppermute | solution.py:61
  30.3 21.2 %collective-permute-start.4 = (bf16[3,8,128,128]{3,2,1,0:T(8,128)(2,1)}, bf16[3,8,128,128]{3,2,1,0:T(8,128)(2,1)}, u32[]{:S(2)}, u32[]{:S(2)}) collective-permute-start(bf16[3,8,128,128]{3,2,1,0:T(8,128)(2,1)} %fusion.here), channel_id=1, source_target_pairs={{0,8},{4,12},{8,0},{12,4},{16,24},{20,28},{24,16},{28,20},{1,9},{5... | collective-permute-start | bytes 2359304 | tf_op jit(solution)/shard_map/ppermute | solution.py:47
  34.1 30.1 %all-to-all-start.1 = ((bf16[4,4,128,512]{3,2,1,0:T(8,128)(2,1)}), bf16[4,4,128,512]{3,2,1,0:T(8,128)(2,1)S(1)}, u32[]{:S(2)}, u32[]{:S(2)}) async-start(bf16[4,4,128,512]{3,2,1,0:T(8,128)(2,1)} %copy-done.7), calls=%async_computation.1 | async-start | bytes 4194304 | tf_op jit(solution)/shard_map/all_to_all | solution.py:55
  40.4 19.6 %copy-start.16 = (s32[16,8]{0,1:T(8,128)S(1)}, s32[16,8]{0,1:T(8,128)}, u32[]{:S(2)}) copy-start(s32[16,8]{0,1:T(8,128)} %param.15) | copy-start | bytes 1540
  40.4 23.8 %copy-start.15 = (s32[16]{0:T(128)S(1)}, s32[16]{0:T(128)}, u32[]{:S(2)}) copy-start(s32[16]{0:T(128)} %counts.1) | copy-start | bytes 196
  41.8 4.6 %collective-permute-start.5 = (bf16[128,512]{1,0:T(8,128)(2,1)S(1)}, bf16[128,512]{1,0:T(8,128)(2,1)S(1)}, u32[]{:S(2)}, u32[]{:S(2)}) collective-permute-start(bf16[128,512]{1,0:T(8,128)(2,1)S(1)} %get-tuple-element.68), channel_id=1, source_target_pairs={{0,4},{4,8},{8,12},{12,16},{16,20},{20,24},{24,28},{1,5},{5,9},{9,... | collective-permute-start | bytes 393224 | tf_op jit(solution)/shard_map/ppermute | solution.py:60
  45.0 3.2 %collective-permute-start.6 = (bf16[128,512]{1,0:T(8,128)(2,1)S(1)}, bf16[128,512]{1,0:T(8,128)(2,1)S(1)}, u32[]{:S(2)}, u32[]{:S(2)}) collective-permute-start(bf16[128,512]{1,0:T(8,128)(2,1)S(1)} %get-tuple-element.69), channel_id=1, source_target_pairs={{4,0},{8,4},{12,8},{16,12},{20,16},{24,20},{28,24},{5,1},{9,5},{13... | collective-permute-start | bytes 393224 | tf_op jit(solution)/shard_map/ppermute | solution.py:61
  51.5 12.7 %collective-permute-start.11 = (bf16[3,8,128,128]{3,2,1,0:T(8,128)(2,1)}, bf16[3,8,128,128]{3,2,1,0:T(8,128)(2,1)S(1)}, u32[]{:S(2)}, u32[]{:S(2)}) collective-permute-start(bf16[3,8,128,128]{3,2,1,0:T(8,128)(2,1)} %collective-permute-done.4.there), channel_id=1, source_target_pairs={{0,4},{4,0},{8,12},{12,8},{16,20},{20,16},{24,28},{28,24},{1,5},{5... | collective-permute-start | bytes 2359304 | tf_op jit(solution)/shard_map/ppermute | solution.py:47
  56.5 7.7 %collective-permute-start.10 = (bf16[3,8,128,128]{3,2,1,0:T(8,128)(2,1)}, bf16[3,8,128,128]{3,2,1,0:T(8,128)(2,1)}, u32[]{:S(2)}, u32[]{:S(2)}) collective-permute-start(bf16[3,8,128,128]{3,2,1,0:T(8,128)(2,1)} %fusion.here), channel_id=1, source_target_pairs={{0,4},{4,0},{8,12},{12,8},{16,20},{20,16},{24,28},{28,24},{1,5},{5... | collective-permute-start | bytes 2359304 | tf_op jit(solution)/shard_map/ppermute | solution.py:47
  56.5 24.6 %collective-permute-start.7 = (bf16[3,128,512]{2,1,0:T(8,128)(2,1)}, bf16[3,128,512]{2,1,0:T(8,128)(2,1)}, u32[]{:S(2)}, u32[]{:S(2)}) collective-permute-start(bf16[3,128,512]{2,1,0:T(8,128)(2,1)} %get-tuple-element.75), channel_id=1, source_target_pairs={{0,1},{1,0},{2,3},{3,2},{4,5},{5,4},{6,7},{7,6},{8,9},{9,8},{10,11... | collective-permute-start | bytes 1179656 | tf_op jit(solution)/shard_map/ppermute | solution.py:47
  58.4 24.5 %collective-permute-start.8 = (bf16[3,128,512]{2,1,0:T(8,128)(2,1)}, bf16[3,128,512]{2,1,0:T(8,128)(2,1)}, u32[]{:S(2)}, u32[]{:S(2)}) collective-permute-start(bf16[3,128,512]{2,1,0:T(8,128)(2,1)} %get-tuple-element.76), channel_id=1, source_target_pairs={{0,2},{1,3},{2,0},{3,1},{4,6},{5,7},{6,4},{7,5},{8,10},{9,11},{10,... | collective-permute-start | bytes 1179656 | tf_op jit(solution)/shard_map/ppermute | solution.py:47
  59.9 23.1 %collective-permute-start.9 = (bf16[3,128,512]{2,1,0:T(8,128)(2,1)}, bf16[3,128,512]{2,1,0:T(8,128)(2,1)}, u32[]{:S(2)}, u32[]{:S(2)}) collective-permute-start(bf16[3,128,512]{2,1,0:T(8,128)(2,1)} %get-tuple-element.77), channel_id=1, source_target_pairs={{0,3},{1,2},{2,1},{3,0},{4,7},{5,6},{6,5},{7,4},{8,11},{9,10},{10,... | collective-permute-start | bytes 1179656 | tf_op jit(solution)/shard_map/ppermute | solution.py:47
  64.2 3.4 %copy-start = (bf16[2048,2048]{1,0:T(8,128)(2,1)S(1)}, bf16[2048,2048]{1,0:T(8,128)(2,1)}, u32[]{:S(2)}) copy-start(bf16[2048,2048]{1,0:T(8,128)(2,1)} %refs_5_.1) | copy-start | bytes 25165828
  68.8 14.2 %copy-start.1 = (bf16[2048,2048]{1,0:T(8,128)(2,1)S(1)}, bf16[2048,2048]{1,0:T(8,128)(2,1)}, u32[]{:S(2)}) copy-start(bf16[2048,2048]{1,0:T(8,128)(2,1)} %refs_5_.1) | copy-start | bytes 25165828
  79.4 15.7 %collective-permute-start.12 = (bf16[2,128,512]{2,1,0:T(8,128)(2,1)S(1)}, bf16[2,128,512]{2,1,0:T(8,128)(2,1)S(1)}, u32[]{:S(2)}, u32[]{:S(2)}) collective-permute-start(bf16[2,128,512]{2,1,0:T(8,128)(2,1)S(1)} %get-tuple-element.93), channel_id=1, source_target_pairs={{0,1},{1,0},{2,3},{3,2},{4,5},{5,4},{6,7},{7,6},{8,9},{9,8},{10,11... | collective-permute-start | bytes 786440 | tf_op jit(solution)/shard_map/ppermute | solution.py:47
  81.0 14.1 %collective-permute-start.13 = (bf16[2,128,512]{2,1,0:T(8,128)(2,1)S(1)}, bf16[2,128,512]{2,1,0:T(8,128)(2,1)S(1)}, u32[]{:S(2)}, u32[]{:S(2)}) collective-permute-start(bf16[2,128,512]{2,1,0:T(8,128)(2,1)S(1)} %get-tuple-element.94), channel_id=1, source_target_pairs={{0,2},{1,3},{2,0},{3,1},{4,6},{5,7},{6,4},{7,5},{8,10},{9,11},{10,... | collective-permute-start | bytes 786440 | tf_op jit(solution)/shard_map/ppermute | solution.py:47
  81.1 14.0 %collective-permute-start.14 = (bf16[2,128,512]{2,1,0:T(8,128)(2,1)S(1)}, bf16[2,128,512]{2,1,0:T(8,128)(2,1)S(1)}, u32[]{:S(2)}, u32[]{:S(2)}) collective-permute-start(bf16[2,128,512]{2,1,0:T(8,128)(2,1)S(1)} %get-tuple-element.95), channel_id=1, source_target_pairs={{0,3},{1,2},{2,1},{3,0},{4,7},{5,6},{6,5},{7,4},{8,11},{9,10},{10,... | collective-permute-start | bytes 786440 | tf_op jit(solution)/shard_map/ppermute | solution.py:47
  83.0 28.4 %copy-start.4 = (f32[512,512]{1,0:T(8,128)S(1)}, f32[512,512]{1,0:T(8,128)}, u32[]{:S(2)}) copy-start(f32[512,512]{1,0:T(8,128)} %u_ref.3) | copy-start | bytes 3145732
  95.1 16.2 %collective-permute-start.15 = (bf16[2,128,512]{2,1,0:T(8,128)(2,1)S(1)}, bf16[2,128,512]{2,1,0:T(8,128)(2,1)S(1)}, u32[]{:S(2)}, u32[]{:S(2)}) collective-permute-start(bf16[2,128,512]{2,1,0:T(8,128)(2,1)S(1)} %get-tuple-element.102), channel_id=1, source_target_pairs={{0,1},{1,0},{2,3},{3,2},{4,5},{5,4},{6,7},{7,6},{8,9},{9,8},{10,11... | collective-permute-start | bytes 786440 | tf_op jit(solution)/shard_map/ppermute | solution.py:47
  96.8 14.5 %collective-permute-start.16 = (bf16[2,128,512]{2,1,0:T(8,128)(2,1)S(1)}, bf16[2,128,512]{2,1,0:T(8,128)(2,1)S(1)}, u32[]{:S(2)}, u32[]{:S(2)}) collective-permute-start(bf16[2,128,512]{2,1,0:T(8,128)(2,1)S(1)} %get-tuple-element.103), channel_id=1, source_target_pairs={{0,2},{1,3},{2,0},{3,1},{4,6},{5,7},{6,4},{7,5},{8,10},{9,11},{10,... | collective-permute-start | bytes 786440 | tf_op jit(solution)/shard_map/ppermute | solution.py:47
  97.4 13.9 %collective-permute-start.17 = (bf16[2,128,512]{2,1,0:T(8,128)(2,1)S(1)}, bf16[2,128,512]{2,1,0:T(8,128)(2,1)S(1)}, u32[]{:S(2)}, u32[]{:S(2)}) collective-permute-start(bf16[2,128,512]{2,1,0:T(8,128)(2,1)S(1)} %get-tuple-element.104), channel_id=1, source_target_pairs={{0,3},{1,2},{2,1},{3,0},{4,7},{5,6},{6,5},{7,4},{8,11},{9,10},{10,... | collective-permute-start | bytes 786440 | tf_op jit(solution)/shard_map/ppermute | solution.py:47
  (6 other events, 5.9 us)
